TPU v7x, 512 devices: a whole 4x8x8 slice. The times are simulated.
512 devices in a mesh: section: 32 (over y, z_hi), tp: 16 (over z_lo, x, core).
Axes of the slice: x: 4, y: 8, z: 8 (z_hi: 4, z_lo: 2; z = z_hi * 2 + z_lo), core: 2. Of those that a mesh axis runs over, the one named last changes fastest.
Arguments:
- carried_acts: bfloat16 [32, 2, 32, 4096], P('section', None, 'tp'), may hold values from -6 to 6
- fresh_acts: bfloat16 [2, 1, 32, 4096], P(None, None, 'tp'), may hold values from -6 to 6
- stashed_acts: bfloat16 [32, 2, 2, 32, 4096], P('section', None, None, 'tp'), may hold values from -6 to 6
- carried_grads: bfloat16 [32, 2, 32, 4096], P('section', None, 'tp'), may hold values from -6 to 6
- fresh_grads: bfloat16 [2, 1, 32, 4096], P(None, None, 'tp'), may hold values from -6 to 6
- norm_gain: bfloat16 [32, 2048], P('section'), may hold values from 0.59765625 to 1.3984375
- query_weight: bfloat16 [32, 2048, 4096], P('section', None, 'tp'), may hold values from -0.09375 to 0.09375
- keyval_weight: bfloat16 [32, 2048, 1024], P('section', None, 'tp'), may hold values from -0.09375 to 0.09375
- output_weight: bfloat16 [32, 4096, 2048], P('section', 'tp'), may hold values from -0.09375 to 0.09375
Outputs:
- layer_outputs: bfloat16 [32, 2, 2, 32, 4096], P('section', None, None, 'tp')
- input_grads: bfloat16 [32, 2, 2, 32, 4096], P('section', None, None, 'tp')
- grad_query: bfloat16 [32, 2048, 4096], P('section', None, 'tp')
- grad_keyval: bfloat16 [32, 2048, 1024], P('section', None, 'tp')
- grad_output: bfloat16 [32, 2048, 4096], P('section', None, 'tp')
- grad_gain: bfloat16 [32, 2048], P('section')
All inputs are finite; a program needn't handle non-finite values.
Results may differ from a plain program's by a relative error of at most 0.035.
Values may be sent and summed in bfloat16 or wider, within the bound.
No kernel may reach another device: no remote copies, remote signals or barrier semaphores. Data moves between devices by JAX's collectives and lax.ppermute only.
A program may use at most 64 MiB of HBM per device.

v0:
```python
import math

import jax
import jax.numpy as jnp
from jax import lax
from jax.sharding import PartitionSpec as P

HD = 128
KVH = 4


EPSILON = 1e-05


def passed_along(block, axis, distance):
    devices = range(lax.axis_size(axis))
    route = [(i - distance, i) for i in devices if i - distance in devices]
    return lax.ppermute(block, axis, route)


def normalize(value_rows, gain):
    widened = value_rows.astype(jnp.float32)
    inverse = lax.rsqrt(jnp.mean(widened * widened, axis=-1, keepdims=True) + EPSILON)
    unit = widened * inverse
    return (unit, inverse, (unit * gain.astype(jnp.float32)).astype(jnp.bfloat16))


def softmax_rows(queries, keys):
    tokens = queries.shape[1]
    causal = lax.broadcasted_iota(jnp.int32, (tokens, tokens), 0) >= lax.broadcasted_iota(
        jnp.int32, (tokens, tokens), 1
    )
    scores = jnp.einsum(
        "cowy,cly->cwol",
        queries,
        keys,
        preferred_element_type=jnp.float32,
        precision=lax.Precision.HIGHEST,
    ) / math.sqrt(queries.shape[-1])
    scores = jnp.where(causal, scores, -jnp.inf)
    weights = jnp.exp(scores - jnp.max(scores, axis=-1, keepdims=True))
    return weights / jnp.sum(weights, axis=-1, keepdims=True)


def exact_mix(queries, keys, value_rows):
    attention_probabilities = softmax_rows(queries, keys)
    return jnp.einsum(
        "yfgp,ypj->ygfj", attention_probabilities, value_rows, precision=lax.Precision.HIGHEST
    )


def flip_blocks(received, section_count):
    blocks = received.reshape((section_count, -1) + received.shape[1:])
    return blocks[::-1].reshape(received.shape)


def from_mirror(moving, section_count):
    received = (
        lax.all_to_all(moving[0], "section", split_axis=0, concat_axis=0, tiled=True),
        lax.all_to_all(moving[1], "section", split_axis=0, concat_axis=0, tiled=True),
        lax.all_to_all(moving[2], "section", split_axis=0, concat_axis=0, tiled=True),
        lax.all_to_all(moving[3], "section", split_axis=0, concat_axis=0, tiled=True),
    )
    flipped = tuple((flip_blocks(portion_half, section_count) for portion_half in received))
    return (
        lax.all_to_all(flipped[0], "section", split_axis=0, concat_axis=0, tiled=True),
        lax.all_to_all(flipped[1], "section", split_axis=0, concat_axis=0, tiled=True),
        lax.all_to_all(flipped[2], "section", split_axis=0, concat_axis=0, tiled=True),
        lax.all_to_all(flipped[3], "section", split_axis=0, concat_axis=0, tiled=True),
    )


def join_halves(mine, theirs, lower_half, axis):
    return jnp.where(
        lower_half,
        jnp.concatenate([mine, theirs], axis=axis),
        jnp.concatenate([theirs, mine], axis=axis),
    )


def split_halves(whole, lower_half, axis):
    half = whole.shape[axis] // 2
    first = lax.slice_in_dim(whole, 0, half, axis=axis)
    second = lax.slice_in_dim(whole, half, 2 * half, axis=axis)
    return (jnp.where(lower_half, first, second), jnp.where(lower_half, second, first))


def two_dots(left, mine_mat, theirs_mat, lower_half):
    own_part, other_part = split_halves(left, lower_half, 2)
    total = jnp.einsum("dtk,kc->dtc", own_part, mine_mat, preferred_element_type=jnp.float32)
    return total + jnp.einsum(
        "dtk,kc->dtc", other_part, theirs_mat, preferred_element_type=jnp.float32
    )


def on_device(
    carried_acts,
    fresh_acts,
    stashed_acts,
    carried_grads,
    fresh_grads,
    norm_gain,
    query_weight,
    keyval_weight,
    output_weight,
):
    section_count = lax.axis_size("section")
    tensor_parallel_count = lax.axis_size("tp")
    section_index = lax.axis_index("section")
    tp_index = lax.axis_index("tp")
    first_section = section_index == 0
    last_section = section_index == section_count - 1
    lower_half = section_index < section_count // 2
    own_layer = (norm_gain[0], query_weight[0], keyval_weight[0], output_weight[0])
    partner_layer = from_mirror(own_layer, section_count)
    gain = join_halves(own_layer[0], partner_layer[0], lower_half, 0)
    query_mine, query_theirs = (own_layer[1], partner_layer[1])
    keyval_mine, keyval_theirs = (own_layer[2], partner_layer[2])
    output_mine, output_theirs = (own_layer[3], partner_layer[3])
    row_count = carried_acts.shape[2]
    width = carried_acts.shape[3]
    tokens = row_count * tensor_parallel_count
    ticks = stashed_acts.shape[2]
    local_heads = query_mine.shape[1] // HD
    groups = local_heads * tensor_parallel_count // KVH
    kv_head = tp_index * local_heads // groups
    first_row_offset = tp_index * row_count
    held_rows = stashed_acts[0].reshape(2 * ticks, row_count, width)
    stacked = jnp.concatenate(
        [
            carried_acts[0],
            carried_grads[0],
            held_rows,
            fresh_acts.reshape(-1, row_count, width),
            fresh_grads.reshape(-1, row_count, width),
        ],
        axis=0,
    )
    gathered = lax.all_gather(stacked, "tp", axis=1, tiled=True)
    acts_now = gathered[0:2]
    grads_now = gathered[2:4]
    held_full = gathered[4 : 4 + 2 * ticks].reshape(2, ticks, tokens, width)
    spare = gathered[4 + 2 * ticks :]

    def rows_of(value_rows):
        return lax.dynamic_slice_in_dim(value_rows, first_row_offset, row_count, 1)

    def local_forward(current):
        unit, inverse, normed = normalize(current, gain)
        queries = two_dots(normed, query_mine, query_theirs, lower_half).astype(jnp.bfloat16)
        packed = two_dots(normed, keyval_mine, keyval_theirs, lower_half).astype(jnp.bfloat16)
        keyvals = lax.all_gather(packed, "tp", axis=2, tiled=True)
        keys = lax.dynamic_slice_in_dim(keyvals, kv_head * HD, HD, 2)
        value_rows = lax.dynamic_slice_in_dim(keyvals, KVH * HD + kv_head * HD, HD, 2)
        heads = queries.reshape(2, tokens, local_heads, HD)
        attention_probabilities = softmax_rows(heads, keys).astype(jnp.bfloat16)
        mixed = jnp.einsum(
            "yfgp,ypj->ygfj",
            attention_probabilities,
            value_rows,
            preferred_element_type=jnp.float32,
        ).astype(jnp.bfloat16)
        return (unit, inverse, normed, heads, keys, value_rows, mixed.reshape(2, tokens, -1))

    def back_rows_of(back_mat, mine_mat, theirs_mat):
        own_rows = jnp.einsum("dtc,kc->dtk", back_mat, mine_mat, preferred_element_type=jnp.float32)
        other_rows = jnp.einsum(
            "dtc,kc->dtk", back_mat, theirs_mat, preferred_element_type=jnp.float32
        )
        return (own_rows, other_rows)

    acc_gain = jnp.zeros((width,), jnp.float32)
    output_rows = []
    back_rows_all = []
    kept_normed = []
    kept_query_back = []
    kept_keyval_back = []
    kept_upstream = []
    kept_mixed = []
    for tick_index in range(ticks):
        unit, inverse, normed, heads, keys, value_rows, mixed = local_forward(acts_now)
        own_cols = jnp.einsum("dtc,ck->dtk", mixed, output_mine, preferred_element_type=jnp.float32)
        other_cols = jnp.einsum(
            "dtc,ck->dtk", mixed, output_theirs, preferred_element_type=jnp.float32
        )
        parts = join_halves(own_cols, other_cols, lower_half, 2)
        total = lax.psum(parts.astype(jnp.bfloat16), "tp").astype(jnp.float32)
        layer_out = (acts_now.astype(jnp.float32) + total).astype(jnp.bfloat16)
        out_rows = rows_of(layer_out)
        output_rows.append(out_rows)
        upstream = grads_now
        unit, inverse, normed, heads, keys, value_rows, mixed = local_forward(
            held_full[:, tick_index]
        )
        up_own, up_other = split_halves(upstream, lower_half, 2)
        back_mixed = jnp.einsum(
            "dtk,ck->dtc", up_own, output_mine, preferred_element_type=jnp.float32
        )
        back_mixed = (
            back_mixed
            + jnp.einsum("dtk,ck->dtc", up_other, output_theirs, preferred_element_type=jnp.float32)
        ).astype(jnp.bfloat16)
        unused, pullback = jax.vjp(
            exact_mix,
            heads.astype(jnp.float32),
            keys.astype(jnp.float32),
            value_rows.astype(jnp.float32),
        )
        grad_heads, key_gradients, grad_values = pullback(
            back_mixed.reshape(heads.shape).astype(jnp.float32)
        )
        spread = jnp.zeros((2, tokens, 2 * KVH * HD), jnp.float32)
        spread = lax.dynamic_update_slice_in_dim(spread, key_gradients, kv_head * HD, 2)
        spread = lax.dynamic_update_slice_in_dim(spread, grad_values, KVH * HD + kv_head * HD, 2)
        keyval_back = lax.psum_scatter(
            spread.astype(jnp.bfloat16), "tp", scatter_dimension=2, tiled=True
        )
        query_back = grad_heads.reshape(2, tokens, -1).astype(jnp.bfloat16)
        kept_normed.append(normed)
        kept_query_back.append(query_back)
        kept_keyval_back.append(keyval_back)
        kept_upstream.append(upstream)
        kept_mixed.append(mixed)
        query_own, query_other = back_rows_of(query_back, query_mine, query_theirs)
        keyval_own, keyval_other = back_rows_of(keyval_back, keyval_mine, keyval_theirs)
        partial_value = join_halves(
            query_own + keyval_own, query_other + keyval_other, lower_half, 2
        )
        back_normed = lax.psum(partial_value.astype(jnp.bfloat16), "tp").astype(jnp.float32)
        scaled = back_normed * gain.astype(jnp.float32)
        acc_gain = acc_gain + jnp.sum(back_normed * unit, axis=(0, 1))
        correction = inverse * (scaled - unit * jnp.mean(scaled * unit, axis=-1, keepdims=True))
        back_input = (upstream.astype(jnp.float32) + correction).astype(jnp.bfloat16)
        back_rows = rows_of(back_input)
        back_rows_all.append(back_rows)
        if tick_index + 1 < ticks:
            ahead = passed_along((layer_out[0], back_input[1]), "section", 1)
            behind = passed_along((layer_out[1], back_input[0]), "section", -1)
            fresh_full = spare[: 2 * (ticks - 1)].reshape(2, ticks - 1, tokens, width)
            fresh_back = spare[2 * (ticks - 1) :].reshape(2, ticks - 1, tokens, width)
            down_acts = jnp.where(first_section, fresh_full[0, tick_index], ahead[0])
            up_acts = jnp.where(last_section, fresh_full[1, tick_index], behind[0])
            down_back = jnp.where(last_section, fresh_back[0, tick_index], behind[1])
            up_back = jnp.where(first_section, fresh_back[1, tick_index], ahead[1])
            acts_now = jnp.stack([down_acts, up_acts], axis=0)
            grads_now = jnp.stack([down_back, up_back], axis=0)
    all_normed = jnp.concatenate(kept_normed, axis=0)
    all_query_back = jnp.concatenate(kept_query_back, axis=0)
    all_keyval_back = jnp.concatenate(kept_keyval_back, axis=0)
    all_upstream = jnp.concatenate(kept_upstream, axis=0)
    all_mixed = jnp.concatenate(kept_mixed, axis=0)
    normed_own, normed_other = split_halves(all_normed, lower_half, 2)
    upstream_own, upstream_other = split_halves(all_upstream, lower_half, 2)

    def outer(left, right):
        return jnp.einsum("dtk,dtc->kc", left, right, preferred_element_type=jnp.float32).astype(
            jnp.bfloat16
        )

    kept_query, sent_query = (
        outer(normed_own, all_query_back),
        outer(normed_other, all_query_back),
    )
    kept_keyval, sent_keyval = (
        outer(normed_own, all_keyval_back),
        outer(normed_other, all_keyval_back),
    )
    kept_output, sent_output = (outer(upstream_own, all_mixed), outer(upstream_other, all_mixed))
    kept_gain, sent_gain = split_halves(acc_gain.astype(jnp.bfloat16), lower_half, 0)
    arrived_grads = from_mirror((sent_gain, sent_query, sent_keyval, sent_output), section_count)
    owned = (kept_gain, kept_query, kept_keyval, kept_output)
    totals = tuple(
        (
            (mine.astype(jnp.float32) + theirs.astype(jnp.float32)).astype(jnp.bfloat16)
            for mine, theirs in zip(owned, arrived_grads)
        )
    )
    layer_outputs = jnp.stack(output_rows, axis=1)[None]
    input_grads = jnp.stack(back_rows_all, axis=1)[None]
    return (
        layer_outputs,
        input_grads,
        totals[1][None],
        totals[2][None],
        totals[3][None],
        totals[0][None],
    )


def solution(mesh):
    in_specs = (
        P("section", None, "tp", None),
        P(None, None, "tp", None),
        P("section", None, None, "tp", None),
        P("section", None, "tp", None),
        P(None, None, "tp", None),
        P("section", None),
        P("section", None, "tp"),
        P("section", None, "tp"),
        P("section", "tp", None),
    )
    out_specs = (
        P("section", None, None, "tp", None),
        P("section", None, None, "tp", None),
        P("section", None, "tp"),
        P("section", None, "tp"),
        P("section", None, "tp"),
        P("section", None),
    )
    return jax.shard_map(
        on_device, mesh=mesh, in_specs=in_specs, out_specs=out_specs, check_vma=False
    )
```

profile of v0, /device:TPU:78, one launch (start us, length us, event | category | flops | bytes accessed | tf_op | source)
XLA Modules:
  0.0 970.5 jit_solution(17920560810059615276)
XLA Ops:
  12.8 15.3 %all-to-all-start = ((bf16[32,64,1]{1,2,0:T(2,128)(2,1)}), bf16[32,64,1]{1,2,0:T(2,128)(2,1)S(1)}, u32[]{:S(2)}, u32[]{:S(2)}) async-start(bf16[32,64,1]{1,2,0:T(2,128)(2,1)} %all_to_all.134), calls=%async_computation | async-start | bytes 32768 | tf_op jit(solution)/shard_map/all_to_all | solution.py:59
  30.9 8.1 all-to-all-done
  44.6 12.9 %all-to-all-done.2 = bf16[32,2,2048]{2,1,0:T(2,128)(2,1)S(1)} async-done(((bf16[32,2,2048]{2,1,0:T(2,128)(2,1)}), bf16[32,2,2048]{2,1,0:T(2,128)(2,1)S(1)}, u32[]{:S(2)}, u32[]{:S(2)}) %all-to-all-start.2) | async-done | bytes 262176 | tf_op jit(solution)/shard_map/all_to_all | solution.py:61
  62.3 10.1 %all-to-all-done.1 = bf16[32,64,1]{1,2,0:T(2,128)(2,1)S(1)} async-done(((bf16[32,64,1]{1,2,0:T(2,128)(2,1)}), bf16[32,64,1]{1,2,0:T(2,128)(2,1)S(1)}, u32[]{:S(2)}, u32[]{:S(2)}) %all-to-all-start.1) | async-done | bytes 4128 | tf_op jit(solution)/shard_map/all_to_all | solution.py:66
  72.4 17.3 %all_to_all.153 = bf16[32,2,2048]{2,1,0:T(2,128)(2,1)S(1)} all-to-all(bf16[32,2,2048]{2,1,0:T(2,128)(2,1)S(1)} %reshape.357), channel_id=1, replica_groups=mesh['section'=32,'tp'=16] {'section'}, dimensions={0} | all-to-all | bytes 524288 | tf_op jit(solution)/shard_map/all_to_all | solution.py:68
  89.7 31.2 %all_to_all.154 = bf16[32,64,256]{2,1,0:T(8,128)(2,1)S(1)} all-to-all(bf16[32,64,256]{2,1,0:T(8,128)(2,1)S(1)} %bitcast.529), channel_id=1, replica_groups=mesh['section'=32,'tp'=16] {'section'}, dimensions={0} | all-to-all | bytes 2097152 | tf_op jit(solution)/shard_map/all_to_all | solution.py:60
  134.7 20.9 %all-to-all-done.6 = bf16[32,8,2048]{2,1,0:T(8,128)(2,1)S(1)} async-done(((bf16[32,8,2048]{2,1,0:T(8,128)(2,1)}), bf16[32,8,2048]{2,1,0:T(8,128)(2,1)S(1)}, u32[]{:S(2)}, u32[]{:S(2)}) %all-to-all-start.6) | async-done | bytes 1048608 | tf_op jit(solution)/shard_map/all_to_all | solution.py:62
  176.1 22.5 %all_gather.18 = bf16[2,32,1024]{1,0,2:T(2,128)(2,1)} all-gather(bf16[2,32,64]{1,0,2:T(2,128)(2,1)S(1)} %copy.134), channel_id=1, replica_groups=mesh['section'=32,'tp'=16] {'tp'}, dimensions={2}, use_global_device_ids=true | all-gather | bytes 139264 | tf_op jit(solution)/shard_map/all_gather | solution.py:152
  201.5 10.3 %all-to-all-start.7 = ((bf16[32,8,2048]{2,1,0:T(8,128)(2,1)}), bf16[32,8,2048]{2,1,0:T(8,128)(2,1)S(1)}, u32[]{:S(2)}, u32[]{:S(2)}) async-start(bf16[32,8,2048]{2,1,0:T(8,128)(2,1)} %all_to_all.116), calls=%async_computation.7 | async-start | bytes 2097152 | tf_op jit(solution)/shard_map/all_to_all | solution.py:69
  224.0 17.4 %all-to-all-done.7 = bf16[32,8,2048]{2,1,0:T(8,128)(2,1)S(1)} async-done(((bf16[32,8,2048]{2,1,0:T(8,128)(2,1)}), bf16[32,8,2048]{2,1,0:T(8,128)(2,1)S(1)}, u32[]{:S(2)}, u32[]{:S(2)}) %all-to-all-start.7) | async-done | bytes 1048608 | tf_op jit(solution)/shard_map/all_to_all | solution.py:69
  251.2 17.8 %all_gather.16 = bf16[2,32,1024]{1,0,2:T(2,128)(2,1)S(1)} all-gather(bf16[2,32,64]{1,0,2:T(2,128)(2,1)} %copy.114), channel_id=1, replica_groups=mesh['section'=32,'tp'=16] {'tp'}, dimensions={2}, use_global_device_ids=true | all-gather | bytes 139264 | tf_op jit(solution)/shard_map/all_gather | solution.py:152
  279.5 31.1 %reduce-scatter.7.cloned.1.call-done = bf16[64,64]{1,0:T(8,128)(2,1)} async-done(((bf16[1024,64]{1,0:T(8,128)(2,1)}), bf16[64,64]{1,0:T(8,128)(2,1)}) %reduce-scatter.7.cloned.1.call-update) | async-done | bytes 8208
  315.1 6.4 fusion.233
  321.5 122.2 %all-reduce.7.cloned.1.call-done = (bf16[2,32,4096]{2,1,0:T(8,128)(2,1)}, bf16[2,32,4096]{2,1,0:T(8,128)(2,1)}) async-done(((bf16[2,32,4096]{2,1,0:T(8,128)(2,1)}, bf16[2,32,4096]{2,1,0:T(8,128)(2,1)}), (bf16[2,32,4096]{2,1,0:T(8,128)(2,1)}, bf16[2,32,4096]{2,1,0:T(8,128)(2,1)})) %all-reduce.7.cloned.1.call-update) | async-done | bytes 1048592 | tf_op jit(solution)/shard_map/psum | solution.py:187
  477.1 8.0 collective-permute-start.3
  487.0 28.6 %all_gather.19 = bf16[2,32,1024]{1,0,2:T(2,128)(2,1)S(1)} all-gather(bf16[2,32,64]{1,0,2:T(2,128)(2,1)S(1)} %copy.145), channel_id=1, replica_groups=mesh['section'=32,'tp'=16] {'tp'}, dimensions={2}, use_global_device_ids=true | all-gather | bytes 139264 | tf_op jit(solution)/shard_map/all_gather | solution.py:152
  517.1 18.3 %all_gather.17 = bf16[2,32,1024]{1,0,2:T(2,128)(2,1)S(1)} all-gather(bf16[2,32,64]{1,0,2:T(2,128)(2,1)} %copy.122), channel_id=1, replica_groups=mesh['section'=32,'tp'=16] {'tp'}, dimensions={2}, use_global_device_ids=true | all-gather | bytes 139264 | tf_op jit(solution)/shard_map/all_gather | solution.py:152
  561.6 60.7 %reduce-scatter.9.cloned.1.call-done = bf16[64,64]{1,0:T(8,128)(2,1)} async-done(((bf16[1024,64]{1,0:T(8,128)(2,1)}), bf16[64,64]{1,0:T(8,128)(2,1)}) %reduce-scatter.9.cloned.1.call-update) | async-done | bytes 8208
  632.5 12.1 %all-to-all-start.10 = ((bf16[32,2,2048]{2,1,0:T(2,128)(2,1)}), bf16[32,2,2048]{2,1,0:T(2,128)(2,1)}, u32[]{:S(2)}, u32[]{:S(2)}) async-start(bf16[32,2,2048]{2,1,0:T(2,128)(2,1)} %reshape.359), calls=%async_computation.10 | async-start | bytes 524288 | tf_op jit(solution)/shard_map/all_to_all | solution.py:61
  647.5 12.1 %all-to-all-done.10 = bf16[32,2,2048]{2,1,0:T(2,128)(2,1)} async-done(((bf16[32,2,2048]{2,1,0:T(2,128)(2,1)}), bf16[32,2,2048]{2,1,0:T(2,128)(2,1)}, u32[]{:S(2)}, u32[]{:S(2)}) %all-to-all-start.10) | async-done | bytes 262176 | tf_op jit(solution)/shard_map/all_to_all | solution.py:61
  660.9 95.9 %all-reduce.5.cloned.1.call-done = (bf16[2,32,4096]{2,1,0:T(8,128)(2,1)}, bf16[2,32,4096]{2,1,0:T(8,128)(2,1)}) async-done(((bf16[2,32,4096]{2,1,0:T(8,128)(2,1)}, bf16[2,32,4096]{2,1,0:T(8,128)(2,1)}), (bf16[2,32,4096]{2,1,0:T(8,128)(2,1)}, bf16[2,32,4096]{2,1,0:T(8,128)(2,1)})) %all-reduce.5.cloned.1.call-update) | async-done | bytes 1048592 | tf_op jit(solution)/shard_map/psum | solution.py:187
  760.6 12.8 %all-to-all-start.14 = ((bf16[32,64,1]{1,2,0:T(2,128)(2,1)}), bf16[32,64,1]{1,2,0:T(2,128)(2,1)S(1)}, u32[]{:S(2)}, u32[]{:S(2)}) async-start(bf16[32,64,1]{1,2,0:T(2,128)(2,1)} %select_n.264), calls=%async_computation.14 | async-start | bytes 32768 | tf_op jit(solution)/shard_map/all_to_all | solution.py:59
  774.6 9.8 %all-to-all-done.14 = bf16[32,64,1]{1,2,0:T(2,128)(2,1)S(1)} async-done(((bf16[32,64,1]{1,2,0:T(2,128)(2,1)}), bf16[32,64,1]{1,2,0:T(2,128)(2,1)S(1)}, u32[]{:S(2)}, u32[]{:S(2)}) %all-to-all-start.14) | async-done | bytes 4128 | tf_op jit(solution)/shard_map/all_to_all | solution.py:59
  791.2 12.7 %all-to-all-done.11 = bf16[32,2,2048]{2,1,0:T(2,128)(2,1)S(1)} async-done(((bf16[32,2,2048]{2,1,0:T(2,128)(2,1)}), bf16[32,2,2048]{2,1,0:T(2,128)(2,1)S(1)}, u32[]{:S(2)}, u32[]{:S(2)}) %all-to-all-start.11) | async-done | bytes 262176 | tf_op jit(solution)/shard_map/all_to_all | solution.py:68
  811.8 8.2 all-to-all-done.15
  826.6 27.2 %all-to-all-done.12 = bf16[32,64,256]{2,1,0:T(8,128)(2,1)S(1)} async-done(((bf16[32,64,256]{2,1,0:T(8,128)(2,1)}), bf16[32,64,256]{2,1,0:T(8,128)(2,1)S(1)}, u32[]{:S(2)}, u32[]{:S(2)}) %all-to-all-start.12) | async-done | bytes 1048608 | tf_op jit(solution)/shard_map/all_to_all | solution.py:62
  853.7 6.5 all-to-all-start.8
  862.4 27.1 %all-to-all-done.8 = bf16[32,64,256]{2,1,0:T(8,128)(2,1)S(1)} async-done(((bf16[32,64,256]{2,1,0:T(8,128)(2,1)}), bf16[32,64,256]{2,1,0:T(8,128)(2,1)S(1)}, u32[]{:S(2)}, u32[]{:S(2)}) %all-to-all-start.8) | async-done | bytes 1048608 | tf_op jit(solution)/shard_map/all_to_all | solution.py:60
  889.5 6.4 all-to-all-start.13
  906.5 18.4 %all-to-all-done.13 = bf16[32,64,256]{2,1,0:T(8,128)(2,1)} async-done(((bf16[32,64,256]{2,1,0:T(8,128)(2,1)}), bf16[32,64,256]{2,1,0:T(8,128)(2,1)}, u32[]{:S(2)}, u32[]{:S(2)}) %all-to-all-start.13) | async-done | bytes 1048608 | tf_op jit(solution)/shard_map/all_to_all | solution.py:69
  924.9 6.8 all-to-all-start.9
  937.1 24.0 %all-to-all-done.9 = bf16[32,64,256]{2,1,0:T(8,128)(2,1)} async-done(((bf16[32,64,256]{2,1,0:T(8,128)(2,1)}), bf16[32,64,256]{2,1,0:T(8,128)(2,1)}, u32[]{:S(2)}, u32[]{:S(2)}) %all-to-all-start.9) | async-done | bytes 1048608 | tf_op jit(solution)/shard_map/all_to_all | solution.py:67
  (344 shorter events, 216.3 us)
Async XLA Ops:
  7.2 155.4 %all-gather.2.cloned.1.call-start = ((), (), s32[]{:S(2)}) async-start(), calls=%async_computation.18 | async-start | bytes 4456448 | tf_op jit(solution)/shard_map/all_gather | solution.py:139
  12.8 26.2 %all-to-all-start = ((bf16[32,64,1]{1,2,0:T(2,128)(2,1)}), bf16[32,64,1]{1,2,0:T(2,128)(2,1)S(1)}, u32[]{:S(2)}, u32[]{:S(2)}) async-start(bf16[32,64,1]{1,2,0:T(2,128)(2,1)} %all_to_all.134), calls=%async_computation | async-start | bytes 32768 | tf_op jit(solution)/shard_map/all_to_all | solution.py:59
  29.8 60.0 %copy-start = (bf16[1,2048,256]{2,1,0:T(8,128)(2,1)S(1)}, bf16[1,2048,256]{2,1,0:T(8,128)(2,1)}, u32[]{:S(2)}) copy-start(bf16[1,2048,256]{2,1,0:T(8,128)(2,1)} %param.15) | copy-start | bytes 3145732
  39.0 18.6 %all-to-all-start.2 = ((bf16[32,2,2048]{2,1,0:T(2,128)(2,1)}), bf16[32,2,2048]{2,1,0:T(2,128)(2,1)S(1)}, u32[]{:S(2)}, u32[]{:S(2)}) async-start(bf16[32,2,2048]{2,1,0:T(2,128)(2,1)} %reshape.355), calls=%async_computation.2 | async-start | bytes 524288 | tf_op jit(solution)/shard_map/all_to_all | solution.py:61
  57.5 14.9 %all-to-all-start.1 = ((bf16[32,64,1]{1,2,0:T(2,128)(2,1)}), bf16[32,64,1]{1,2,0:T(2,128)(2,1)S(1)}, u32[]{:S(2)}, u32[]{:S(2)}) async-start(bf16[32,64,1]{1,2,0:T(2,128)(2,1)} %copy.111), calls=%async_computation.1 | async-start | bytes 32768 | tf_op jit(solution)/shard_map/all_to_all | solution.py:66
  121.0 34.6 %all-to-all-start.6 = ((bf16[32,8,2048]{2,1,0:T(8,128)(2,1)}), bf16[32,8,2048]{2,1,0:T(8,128)(2,1)S(1)}, u32[]{:S(2)}, u32[]{:S(2)}) async-start(bf16[32,8,2048]{2,1,0:T(8,128)(2,1)} %bitcast.21), calls=%async_computation.6 | async-start | bytes 2097152 | tf_op jit(solution)/shard_map/all_to_all | solution.py:62
  128.1 336.3 %copy-start.38 = (f32[4096]{0:T(1024)}, f32[4096]{0:T(1024)S(1)}, u32[]{:S(2)}) copy-start(f32[4096]{0:T(1024)S(1)} %fusion.214) | copy-start | bytes 49156
  155.5 45.0 %all-to-all-start.5 = ((bf16[32,64,256]{2,1,0:T(8,128)(2,1)}), bf16[32,64,256]{2,1,0:T(8,128)(2,1)S(1)}, u32[]{:S(2)}, u32[]{:S(2)}) async-start(bf16[32,64,256]{2,1,0:T(8,128)(2,1)} %all_to_all.111), calls=%async_computation.5 | async-start | bytes 2097152 | tf_op jit(solution)/shard_map/all_to_all | solution.py:67
  165.6 279.6 %copy-start.60 = (f32[2,32]{1,0:T(2,128)}, f32[2,32]{1,0:T(2,128)S(1)}, u32[]{:S(2)}) copy-start(f32[2,32]{1,0:T(2,128)S(1)} %add_rsqrt_fusion.1) | copy-start | bytes 772
  201.5 39.9 %all-to-all-start.7 = ((bf16[32,8,2048]{2,1,0:T(8,128)(2,1)}), bf16[32,8,2048]{2,1,0:T(8,128)(2,1)S(1)}, u32[]{:S(2)}, u32[]{:S(2)}) async-start(bf16[32,8,2048]{2,1,0:T(8,128)(2,1)} %all_to_all.116), calls=%async_computation.7 | async-start | bytes 2097152 | tf_op jit(solution)/shard_map/all_to_all | solution.py:69
  211.8 98.8 %reduce-scatter.7.cloned.1.call-start = ((), (), s32[]{:S(2)}) async-start(), calls=%async_computation.19 | async-start | bytes 278528
  244.2 34.1 %copy-start.45 = (bf16[2,2,4,8,128]{4,3,2,1,0:T(8,128)(2,1)}, bf16[2,2,4,8,128]{4,3,2,1,0:T(8,128)(2,1)S(1)}, u32[]{:S(2)}) copy-start(bf16[2,2,4,8,128]{4,3,2,1,0:T(8,128)(2,1)S(1)} %fusion.47) | copy-start | bytes 98308
  251.2 192.5 %all-reduce.7.cloned.1.call-start = ((), (), s32[]{:S(2)}) async-start(), calls=%async_computation.22 | async-start | bytes 2097152 | tf_op jit(solution)/shard_map/psum | solution.py:187
  315.0 307.3 %reduce-scatter.9.cloned.1.call-start = ((), (), s32[]{:S(2)}) async-start(), calls=%async_computation.20 | async-start | bytes 278528
  447.6 14.0 %collective-permute-start = (bf16[32,4096]{1,0:T(8,128)(2,1)S(1)}, bf16[32,4096]{1,0:T(8,128)(2,1)S(1)}, u32[]{:S(2)}, u32[]{:S(2)}) collective-permute-start(bf16[32,4096]{1,0:T(8,128)(2,1)S(1)} %get-tuple-element.39), channel_id=1, source_target_pairs={{0,16},{16,32},{32,48},{48,64},{64,80},{80,96},{96,112},{112,128},... | collective-permute-start | bytes 786440 | tf_op jit(solution)/shard_map/ppermute | solution.py:18
  452.4 11.4 %collective-permute-start.1 = (bf16[32,4096]{1,0:T(8,128)(2,1)S(1)}, bf16[32,4096]{1,0:T(8,128)(2,1)S(1)}, u32[]{:S(2)}, u32[]{:S(2)}) collective-permute-start(bf16[32,4096]{1,0:T(8,128)(2,1)S(1)} %get-tuple-element.40), channel_id=1, source_target_pairs={{16,0},{32,16},{48,32},{64,48},{80,64},{96,80},{112,96},{128,112},... | collective-permute-start | bytes 786440 | tf_op jit(solution)/shard_map/ppermute | solution.py:18
  477.1 69.8 %collective-permute-start.3 = (bf16[32,4096]{1,0:T(8,128)(2,1)}, bf16[32,4096]{1,0:T(8,128)(2,1)}, u32[]{:S(2)}, u32[]{:S(2)}) collective-permute-start(bf16[32,4096]{1,0:T(8,128)(2,1)} %get-tuple-element.35), channel_id=1, source_target_pairs={{0,16},{16,32},{32,48},{48,64},{64,80},{80,96},{96,112},{112,128},... | collective-permute-start | bytes 786440 | tf_op jit(solution)/shard_map/ppermute | solution.py:18
  485.1 63.2 %collective-permute-start.2 = (bf16[32,4096]{1,0:T(8,128)(2,1)}, bf16[32,4096]{1,0:T(8,128)(2,1)}, u32[]{:S(2)}, u32[]{:S(2)}) collective-permute-start(bf16[32,4096]{1,0:T(8,128)(2,1)} %get-tuple-element.36), channel_id=1, source_target_pairs={{16,0},{32,16},{48,32},{64,48},{80,64},{96,80},{112,96},{128,112},... | collective-permute-start | bytes 786440 | tf_op jit(solution)/shard_map/ppermute | solution.py:18
  554.7 68.5 %copy-start.15 = (bf16[2048,64,1]{0,1,2:T(8,128)(2,1)S(1)}, bf16[2048,64,1]{0,1,2:T(8,128)(2,1)}, u32[]{:S(2)}) copy-start(bf16[2048,64,1]{0,1,2:T(8,128)(2,1)} %reshape.317) | copy-start | bytes 786436
  555.6 67.9 %copy-start.12 = (bf16[1,2048,64]{1,2,0:T(8,128)(2,1)S(1)}, bf16[1,2048,64]{1,2,0:T(8,128)(2,1)}, u32[]{:S(2)}) copy-start(bf16[1,2048,64]{1,2,0:T(8,128)(2,1)} %param.16) | copy-start | bytes 786436
  559.6 197.2 %all-reduce.5.cloned.1.call-start = ((), (), s32[]{:S(2)}) async-start(), calls=%async_computation.21 | async-start | bytes 2097152 | tf_op jit(solution)/shard_map/psum | solution.py:187
  632.5 27.1 %all-to-all-start.10 = ((bf16[32,2,2048]{2,1,0:T(2,128)(2,1)}), bf16[32,2,2048]{2,1,0:T(2,128)(2,1)}, u32[]{:S(2)}, u32[]{:S(2)}) async-start(bf16[32,2,2048]{2,1,0:T(2,128)(2,1)} %reshape.359), calls=%async_computation.10 | async-start | bytes 524288 | tf_op jit(solution)/shard_map/all_to_all | solution.py:61
  760.6 23.8 %all-to-all-start.14 = ((bf16[32,64,1]{1,2,0:T(2,128)(2,1)}), bf16[32,64,1]{1,2,0:T(2,128)(2,1)S(1)}, u32[]{:S(2)}, u32[]{:S(2)}) async-start(bf16[32,64,1]{1,2,0:T(2,128)(2,1)} %select_n.264), calls=%async_computation.14 | async-start | bytes 32768 | tf_op jit(solution)/shard_map/all_to_all | solution.py:59
  784.5 19.4 %all-to-all-start.11 = ((bf16[32,2,2048]{2,1,0:T(2,128)(2,1)}), bf16[32,2,2048]{2,1,0:T(2,128)(2,1)S(1)}, u32[]{:S(2)}, u32[]{:S(2)}) async-start(bf16[32,2,2048]{2,1,0:T(2,128)(2,1)} %reshape.361), calls=%async_computation.11 | async-start | bytes 524288 | tf_op jit(solution)/shard_map/all_to_all | solution.py:68
  803.9 16.2 %all-to-all-start.15 = ((bf16[32,64,1]{1,2,0:T(2,128)(2,1)}), bf16[32,64,1]{1,2,0:T(2,128)(2,1)S(1)}, u32[]{:S(2)}, u32[]{:S(2)}) async-start(bf16[32,64,1]{1,2,0:T(2,128)(2,1)} %copy.159), calls=%async_computation.15 | async-start | bytes 32768 | tf_op jit(solution)/shard_map/all_to_all | solution.py:66
  820.1 33.7 %all-to-all-start.12 = ((bf16[32,64,256]{2,1,0:T(8,128)(2,1)}), bf16[32,64,256]{2,1,0:T(8,128)(2,1)S(1)}, u32[]{:S(2)}, u32[]{:S(2)}) async-start(bf16[32,64,256]{2,1,0:T(8,128)(2,1)} %bitcast.99), calls=%async_computation.12 | async-start | bytes 2097152 | tf_op jit(solution)/shard_map/all_to_all | solution.py:62
  825.1 35.2 %copy-start.59 = (f32[2,32]{1,0:T(2,128)S(1)}, f32[2,32]{1,0:T(2,128)}, u32[]{:S(2)}) copy-start(f32[2,32]{1,0:T(2,128)} %copy-done.58) | copy-start | bytes 772
  853.7 35.8 %all-to-all-start.8 = ((bf16[32,64,256]{2,1,0:T(8,128)(2,1)}), bf16[32,64,256]{2,1,0:T(8,128)(2,1)S(1)}, u32[]{:S(2)}, u32[]{:S(2)}) async-start(bf16[32,64,256]{2,1,0:T(8,128)(2,1)} %bitcast.544), calls=%async_computation.8 | async-start | bytes 2097152 | tf_op jit(solution)/shard_map/all_to_all | solution.py:60
  862.4 34.5 %copy-start.9 = (bf16[1,32,4096]{2,1,0:T(8,128)(2,1)S(1)}, bf16[1,32,4096]{2,1,0:T(8,128)(2,1)}, u32[]{:S(2)}) copy-start(bf16[1,32,4096]{2,1,0:T(8,128)(2,1)} %copy-done.8) | copy-start | bytes 786436
  862.4 35.5 %copy-start.33 = (bf16[32,2,2048]{2,1,0:T(2,128)(2,1)S(1)}, bf16[32,2,2048]{2,1,0:T(2,128)(2,1)}, u32[]{:S(2)}) copy-start(bf16[32,2,2048]{2,1,0:T(2,128)(2,1)} %copy-done.32) | copy-start | bytes 786436
  889.5 35.4 %all-to-all-start.13 = ((bf16[32,64,256]{2,1,0:T(8,128)(2,1)}), bf16[32,64,256]{2,1,0:T(8,128)(2,1)}, u32[]{:S(2)}, u32[]{:S(2)}) async-start(bf16[32,64,256]{2,1,0:T(8,128)(2,1)} %all_to_all.129), calls=%async_computation.13 | async-start | bytes 2097152 | tf_op jit(solution)/shard_map/all_to_all | solution.py:69
  924.9 36.2 %all-to-all-start.9 = ((bf16[32,64,256]{2,1,0:T(8,128)(2,1)}), bf16[32,64,256]{2,1,0:T(8,128)(2,1)}, u32[]{:S(2)}, u32[]{:S(2)}) async-start(bf16[32,64,256]{2,1,0:T(8,128)(2,1)} %all_to_all.121), calls=%async_computation.9 | async-start | bytes 2097152 | tf_op jit(solution)/shard_map/all_to_all | solution.py:67
  (59 other events, 643.3 us)
Sparse Core Ops, SparseCore 0:
  11.5 48.9 all-gather.1
  251.3 59.2 reduce-scatter.6
  315.2 128.4 all-reduce.6
  559.7 62.5 reduce-scatter.8
  625.9 130.8 all-reduce.4
where the time goes:
time: 983 us; the launch traced here: 971 us
  waiting for transfers between devices  526 us (54%)
  blocking collectives  136 us (14%)
  starting transfers between devices  126 us (13%)
  local copies, waits for them, and re-layouts  78.7 us (8%)
  matrix products  60.9 us (6%)
  other arithmetic  28.6 us (3%)
  between operations  15.2 us (2%)
    psum x2, waiting for transfers between devices, on_device(): total = lax.psum(parts.astype(jnp.bfloat16), 'tp').astype(jnp.float32)  218 us
    unnamed x7, waiting for transfers between devices  91.8 us
    all_gather x4, blocking collectives, local_forward(): keyvals = lax.all_gather(packed, 'tp', axis=2, tiled=True)  87.2 us
    all_to_all x2, waiting for transfers between devices, from_mirror(): lax.all_to_all(moving[3], 'section', split_axis=0, concat_axis=0, tiled=T...  48.1 us
    all_to_all x2, waiting for transfers between devices, from_mirror(): lax.all_to_all(flipped[3], 'section', split_axis=0, concat_axis=0, tiled=...  35.8 us
    unnamed x168, local copies, waits for them, and re-layouts  31.5 us
    all_to_all x1, blocking collectives, from_mirror(): lax.all_to_all(moving[1], 'section', split_axis=0, concat_axis=0, tiled=T...  31.2 us
    all_to_all x2, starting transfers between devices, from_mirror(): lax.all_to_all(moving[0], 'section', split_axis=0, concat_axis=0, tiled=T...  28.1 us
  transfers between devices with their start and end apart: 23, of which 19 were waited for; matrix products, arithmetic and copies ran while one was open for 10% of the time, Pallas kernels for 0%

commit v1 on v0

v1 whole, which is shorter than its diff:
```python
import math

import jax
import jax.numpy as jnp
from jax import lax
from jax.sharding import PartitionSpec as P

HD = 128
KVH = 4
EPSILON = 1e-05
BF = jnp.bfloat16
F32 = jnp.float32


def mm(left, right, dims=((1,), (0,))):
    return lax.dot_general(left, right, (dims, ((), ())), preferred_element_type=F32)


def mm_t(left, right):
    return mm(left, right, ((1,), (1,)))


def t_mm(left, right):
    return mm(left, right, ((0,), (0,)))


def split_f32(values):
    high = values.astype(BF)
    return high, (values - high.astype(F32)).astype(BF)


def pair_mask(tokens):
    def parts(axis):
        i = lax.broadcasted_iota(jnp.int32, (tokens, tokens), axis)
        return (i // 2) % 4, (i // 8) * 2 + i % 2

    (query_group, query_time), (key_group, key_time) = parts(0), parts(1)
    return (query_group == key_group) & (key_time <= query_time)


def stack_heads(columns):
    return jnp.concatenate([columns[:, i : i + HD] for i in range(0, columns.shape[1], HD)], axis=0)


def unstack_heads(rows, tokens):
    return jnp.concatenate(
        [rows[i : i + tokens] for i in range(0, rows.shape[0], tokens)], axis=1
    )


def attention(queries, keyvals, mask):
    tokens = queries.shape[0]
    stacked, keys, values = stack_heads(queries), keyvals[:, :HD], keyvals[:, HD:]
    scores = mm_t(stacked, keys) / math.sqrt(HD)
    scores = jnp.where(jnp.concatenate([mask] * (queries.shape[1] // HD), 0), scores, -jnp.inf)
    weights = jnp.exp(scores - jnp.max(scores, axis=-1, keepdims=True))
    probs = weights / jnp.sum(weights, axis=-1, keepdims=True)
    mixed = mm(probs.astype(BF), values).astype(BF)
    return probs, unstack_heads(mixed, tokens)


def attention_back(queries, keyvals, probs, back_mixed):
    tokens = queries.shape[0]
    stacked, keys, values = stack_heads(queries), keyvals[:, :HD], keyvals[:, HD:]
    back = stack_heads(back_mixed)
    back_probs = mm_t(back, values)
    inner = jnp.sum(probs * back_probs, axis=-1, keepdims=True)
    back_scores = (probs * (back_probs - inner) / math.sqrt(HD)).astype(BF)
    query_back = unstack_heads(mm(back_scores, keys).astype(BF), tokens)
    key_back = t_mm(back_scores, stacked).astype(BF)
    value_back = t_mm(probs.astype(BF), back).astype(BF)
    return query_back, jnp.concatenate([key_back, value_back], axis=1)


def on_device(
    carried_acts,
    fresh_acts,
    stashed_acts,
    carried_grads,
    fresh_grads,
    norm_gain,
    query_weight,
    keyval_weight,
    output_weight,
):
    sections = lax.axis_size("section")
    shards = lax.axis_size("tp")
    section = lax.axis_index("section")
    me = lax.axis_index("tp")
    lower = section < sections // 2
    ticks = stashed_acts.shape[2]
    width = carried_acts.shape[3]
    half = width // 2
    row_count = carried_acts.shape[2]
    rows = 4 * row_count
    tokens = rows * shards
    gain = norm_gain[0].astype(F32)
    query_mat, output_mat = query_weight[0], output_weight[0]
    mirror = [(i, sections - 1 - i) for i in range(sections)]
    kv_group = shards // KVH

    def halves(whole):
        first, second = whole[..., :half], whole[..., half:]
        return jnp.where(lower, first, second), jnp.where(lower, second, first)

    kv_own = keyval_weight[0].T
    sources = [[2 * j, 2 * j + 1, shards // 2 + 2 * j, shards // 2 + 2 * j + 1] for j in range(KVH)]
    turned = [
        lax.ppermute(
            kv_own,
            "tp",
            [
                (sources[j][(i + k) % kv_group], kv_group * j + i)
                for j in range(KVH)
                for i in range(kv_group)
            ],
        )
        for k in range(kv_group)
    ]

    entering = jnp.stack(
        [carried_acts[0]] + [stashed_acts[0, :, k] for k in range(ticks)] + [carried_grads[0]]
    ).reshape(ticks + 2, 2 * row_count, width)
    own, other = halves(entering)
    arrived = lax.ppermute(other, "section", mirror)
    held = jnp.concatenate(
        [jnp.where(lower, own, arrived), jnp.where(lower, arrived, own)], axis=1
    )

    def gather(local):
        count = local.shape[0]
        spread = jnp.broadcast_to(local.reshape(1, count * rows, half), (shards, count * rows, half))
        full = lax.all_to_all(spread, "tp", split_axis=0, concat_axis=0, tiled=True)
        full = full.reshape(shards, count, rows, half)
        return [full[:, i].reshape(tokens, half) for i in range(count)]

    gathered = gather(held)
    acts, stash, cots = gathered[0], gathered[1 : 1 + ticks], gathered[1 + ticks]

    stacked_blocks = jnp.stack(turned)
    place = me % kv_group
    kv_mat = jnp.concatenate(
        [
            lax.dynamic_index_in_dim(stacked_blocks, (m - place) % kv_group, 0, keepdims=False)
            for m in range(kv_group)
        ],
        axis=0,
    )

    mask = pair_mask(tokens)
    my_rows = lambda full: lax.dynamic_slice_in_dim(full, me * rows, rows, 0)

    def summed_projections(act_list, cot):
        partials, squares = [], []
        for act in act_list:
            wide = act.astype(F32)
            scaled = (wide * gain).astype(BF)
            partials += [mm(scaled, query_mat), mm_t(scaled, kv_mat)]
            squares.append(jnp.sum(wide * wide, axis=-1, keepdims=True))
        partials.append(mm_t(cot, output_mat))
        square_mat = jnp.concatenate(squares, axis=1)
        high, low = split_f32(square_mat)
        count = len(act_list)
        filler = jnp.zeros((tokens, HD - 2 * count), BF)
        message = jnp.concatenate([p.astype(BF) for p in partials] + [high, low, filler], axis=1)
        other_half = lax.ppermute(message, "section", mirror).astype(F32)
        at = 0
        totals = []
        for p in partials:
            totals.append(p + other_half[:, at : at + p.shape[1]])
            at += p.shape[1]
        square_total = (
            square_mat + other_half[:, at : at + count] + other_half[:, at + count : at + 2 * count]
        )
        inverse = lax.rsqrt(square_total / width + EPSILON)
        out = []
        for i in range(count):
            inv = inverse[:, i : i + 1]
            out.append((totals[2 * i] * inv, totals[2 * i + 1] * inv, inv))
        return out, totals[-1].astype(BF)

    def forward_part(projected):
        queries, keyvals, _ = projected
        probs, mixed = attention(queries.astype(BF), keyvals.astype(BF), mask)
        return probs, mixed

    kv_index = [(d % 2) + 2 * (d // (shards // 2)) for d in range(shards)]
    kv_head_of = [(d % (shards // 2)) // 2 for d in range(shards)]
    my_head = me // kv_group

    def backward_part(act, projected, probs, back_mixed):
        queries, keyvals, inverse = projected
        query_back, keyval_back = attention_back(
            queries.astype(BF), keyvals.astype(BF), probs, back_mixed
        )
        back_normed = mm_t(query_back, query_mat) + mm(keyval_back, kv_mat)
        along = jnp.sum(query_back.astype(F32) * queries, axis=-1, keepdims=True) + jnp.sum(
            keyval_back.astype(F32) * keyvals, axis=-1, keepdims=True
        )
        unit = act.astype(F32) * inverse
        partial = inverse * (back_normed * gain - unit * (along / width))
        gain_part = jnp.sum(back_normed * unit, axis=0)
        normed = (unit * gain).astype(BF)
        return query_back, keyval_back, partial.astype(BF), gain_part, normed

    def scatter_sum(pieces):
        block = jnp.concatenate(pieces, axis=1)
        received = lax.all_to_all(block, "tp", split_axis=0, concat_axis=0, tiled=True)
        total = jnp.sum(received.astype(F32), axis=0)
        sizes = [p.shape[1] for p in pieces]
        at, out = 0, []
        for size in sizes:
            out.append(total[at : at + size])
            at += size
        return out

    def kv_blocks(keyval_back):
        turned_back = keyval_back.T.reshape(kv_group, -1, half)
        return jnp.stack(
            [
                jnp.where(kv_head_of[d] == my_head, turned_back[kv_index[d]], jnp.zeros((), BF))
                for d in range(shards)
            ]
        )

    act_rows, cot_rows = held[0], held[1 + ticks]
    projected, back_mixed = summed_projections([acts] + stash, cots)
    stash_projected = projected[1:]
    stash_forward = [forward_part(p) for p in stash_projected]
    forward_projected = projected[0]
    gain_total = jnp.zeros((half,), F32)
    out_rows, back_rows = [], []
    all_normed, all_query_back, all_kv_back, all_cots, all_mixed = [], [], [], [], []
    last = sections // 2 - 1
    ahead = [(i, i + 1) for i in range(last)] + [
        (sections - 1 - i, sections - 2 - i) for i in range(last)
    ]
    behind = [(b, a) for a, b in ahead]
    first_layer = (section == 0) | (section == sections - 1)
    last_layer = (section == last) | (section == last + 1)

    for k in range(ticks):
        _, mixed = forward_part(forward_projected)
        out_part = mm(mixed, output_mat).astype(BF)
        probs, kept_mixed = stash_forward[k]
        query_back, keyval_back, back_part, gain_part, normed = backward_part(
            stash[k], stash_projected[k], probs, back_mixed
        )
        gain_total = gain_total + gain_part
        pieces = [
            out_part.reshape(shards, rows, half),
            back_part.reshape(shards, rows, half),
            kv_blocks(keyval_back),
        ]
        if k + 1 == ticks:
            both = jnp.stack(split_f32(gain_total))[None]
            pieces.append(jnp.broadcast_to(both, (shards, 2, half)))
        sums = scatter_sum(pieces)
        layer_out = (act_rows.astype(F32) + sums[0]).astype(BF)
        back_input = (cot_rows.astype(F32) + sums[1]).astype(BF)
        out_rows.append(layer_out)
        back_rows.append(back_input)
        all_kv_back.append(sums[2].astype(BF).reshape(-1, tokens))
        all_normed.append(normed)
        all_query_back.append(query_back)
        all_cots.append(cots)
        all_mixed.append(kept_mixed)
        if k + 1 < ticks:
            f = layer_out.reshape(2, 2, row_count, half)
            b = back_input.reshape(2, 2, row_count, half)
            going_up = jnp.stack([f[0, 0], f[1, 1], b[1, 0], b[0, 1]])
            going_down = jnp.stack([f[1, 0], f[0, 1], b[0, 0], b[1, 1]])
            from_below = lax.ppermute(going_up, "section", ahead)
            from_above = lax.ppermute(going_down, "section", behind)
            fresh = jnp.stack(
                [fresh_acts[0, k], fresh_acts[1, k], fresh_grads[0, k], fresh_grads[1, k]]
            )
            fresh = halves(fresh)[0]
            lo = jnp.where(first_layer, fresh, from_below)
            hi = jnp.where(last_layer, going_up, from_above)
            act_rows = jnp.concatenate([lo[0], hi[1], hi[0], lo[1]], axis=0)
            cot_rows = jnp.concatenate([hi[2], lo[3], lo[2], hi[3]], axis=0)
            acts, cots = gather(jnp.stack([act_rows, cot_rows]))
            projected, back_mixed = summed_projections([acts], cots)
            forward_projected = projected[0]

    normed = jnp.concatenate(all_normed, axis=0)
    grad_query = t_mm(normed, jnp.concatenate(all_query_back, axis=0)).astype(BF)
    grad_keyval = mm(jnp.concatenate(all_kv_back, axis=1), normed).astype(BF).T
    grad_output = t_mm(
        jnp.concatenate(all_cots, axis=0), jnp.concatenate(all_mixed, axis=0)
    ).astype(BF)
    grad_gain = (sums[3][0] + sums[3][1]).astype(BF)

    leaving = jnp.stack(out_rows + back_rows).reshape(2 * ticks, 2, 2 * row_count, half)
    lo_rows, hi_rows = leaving[:, 0], leaving[:, 1]
    mine, theirs = jnp.where(lower, lo_rows, hi_rows), jnp.where(lower, hi_rows, lo_rows)
    returned = lax.ppermute(theirs, "section", mirror)
    whole = jnp.concatenate(
        [jnp.where(lower, mine, returned), jnp.where(lower, returned, mine)], axis=2
    ).reshape(2, ticks, 2, row_count, width)
    whole = whole.transpose(0, 2, 1, 3, 4)
    return (
        whole[0][None],
        whole[1][None],
        grad_query[None],
        grad_keyval[None],
        grad_output[None],
        grad_gain[None],
    )


def solution(mesh):
    in_specs = (
        P("section", None, "tp", None),
        P(None, None, "tp", None),
        P("section", None, None, "tp", None),
        P("section", None, "tp", None),
        P(None, None, "tp", None),
        P("section", None),
        P("section", None, "tp"),
        P("section", None, "tp"),
        P("section", "tp", None),
    )
    out_specs = (
        P("section", None, None, "tp", None),
        P("section", None, None, "tp", None),
        P("section", None, "tp"),
        P("section", None, "tp"),
        P("section", None, "tp"),
        P("section", None),
    )
    return jax.shard_map(
        on_device, mesh=mesh, in_specs=in_specs, out_specs=out_specs, check_vma=False
    )
```

time: 983 us -> 376 us (0.38)
  the two profiles are of different devices: /device:TPU:78 before, /device:TPU:30 now
where the time goes in v1:
time: 376 us; the launch traced here: 371 us
  waiting for transfers between devices  139 us (37%)
  local copies, waits for them, and re-layouts  91.1 us (24%)
  starting transfers between devices  72 us (19%)
  other arithmetic  33.2 us (9%)
  matrix products  32.6 us (9%)
    ppermute x4, waiting for transfers between devices, on_device(): lax.ppermute(kv_own, 'tp', [(sources[j][(i + k) % kv_group], kv_group * j...  40.5 us
    select_n x32, local copies, waits for them, and re-layouts, kv_blocks(): jnp.where(kv_head_of[d] == my_head, turned_back[kv_index[d]], jnp.zeros((...  37.1 us
    all_to_all x2, waiting for transfers between devices, scatter_sum(): lax.all_to_all(block, 'tp', split_axis=0, concat_axis=0, tiled=True)  34.5 us
    ppermute x2, waiting for transfers between devices, summed_projections(): other_half = lax.ppermute(message, 'section', mirror).astype(F32)  33.6 us
    dot_general x35, matrix products, mm(): lax.dot_general(left, right, (dims, ((), ())), preferred_element_type=F32)  32.6 us
    concatenate x2, local copies, waits for them, and re-layouts, summed_projections(): jnp.concatenate([p.astype(BF) for p in partials] + [high, low, filler], a...  20.1 us
    ppermute x2, starting transfers between devices, summed_projections(): other_half = lax.ppermute(message, 'section', mirror).astype(F32)  14.6 us
    unnamed x217, local copies, waits for them, and re-layouts  14.6 us
  transfers between devices with their start and end apart: 14, of which 13 were waited for; matrix products, arithmetic and copies ran while one was open for 5% of the time, Pallas kernels for 0%

profile of v1, /device:TPU:30, one launch (start us, length us, event | category | flops | bytes accessed | tf_op | source)
XLA Modules:
  0.0 370.9 jit_solution(3102688516569809535)
XLA Ops:
  3.3 13.2 %collective-permute-start = (bf16[4,4,2048]{2,1,0:T(4,128)(2,1)S(1)}, bf16[4,4,2048]{2,1,0:T(4,128)(2,1)S(1)}, u32[]{:S(2)}, u32[]{:S(2)}) collective-permute-start(bf16[4,4,2048]{2,1,0:T(4,128)(2,1)S(1)} %broadcast_select_fusion.6), channel_id=1, source_target_pairs={{0,496},{16,480},{32,464},{48,448},{64,432},{80,416},{96,400},{112... | collective-permute-start | bytes 196616 | tf_op jit(solution)/shard_map/ppermute | solution.py:125
  16.5 4.6 %collective-permute-done = bf16[4,4,2048]{2,1,0:T(4,128)(2,1)S(1)} collective-permute-done((bf16[4,4,2048]{2,1,0:T(4,128)(2,1)S(1)}, bf16[4,4,2048]{2,1,0:T(4,128)(2,1)S(1)}, u32[]{:S(2)}, u32[]{:S(2)}) %collective-permute-start) | collective-permute-done | bytes 65568 | tf_op jit(solution)/shard_map/ppermute | solution.py:125
  22.8 5.8 %all-to-all-start = ((bf16[16,32,2048]{2,1,0:T(8,128)(2,1)}), bf16[16,32,2048]{2,1,0:T(8,128)(2,1)S(1)}, u32[]{:S(2)}, u32[]{:S(2)}) async-start(bf16[16,32,2048]{2,1,0:T(8,128)(2,1)} %broadcast_in_dim.111), calls=%async_computation | async-start | bytes 4194304 | tf_op jit(solution)/shard_map/all_to_all | solution.py:133
  28.6 3.4 collective-permute-start.4
  34.0 2.6 collective-permute-start.2
  36.7 3.4 collective-permute-start.1
  41.3 24.2 %collective-permute-done.4 = bf16[64,2048]{1,0:T(8,128)(2,1)S(1)} collective-permute-done((bf16[64,2048]{1,0:T(8,128)(2,1)}, bf16[64,2048]{1,0:T(8,128)(2,1)S(1)}, u32[]{:S(2)}, u32[]{:S(2)}) %collective-permute-start.4) | collective-permute-done | bytes 262176 | tf_op jit(solution)/shard_map/ppermute | solution.py:109
  66.6 9.1 %collective-permute-done.2 = bf16[64,2048]{1,0:T(8,128)(2,1)} collective-permute-done((bf16[64,2048]{1,0:T(8,128)(2,1)}, bf16[64,2048]{1,0:T(8,128)(2,1)}, u32[]{:S(2)}, u32[]{:S(2)}) %collective-permute-start.2) | collective-permute-done | bytes 262176 | tf_op jit(solution)/shard_map/ppermute | solution.py:109
  75.7 6.1 %collective-permute-done.1 = bf16[64,2048]{1,0:T(8,128)(2,1)} collective-permute-done((bf16[64,2048]{1,0:T(8,128)(2,1)}, bf16[64,2048]{1,0:T(8,128)(2,1)}, u32[]{:S(2)}, u32[]{:S(2)}) %collective-permute-start.1) | collective-permute-done | bytes 262176 | tf_op jit(solution)/shard_map/ppermute | solution.py:109
  97.7 2.3 fusion.235
  100.6 13.0 %concatenate.101 = bf16[128,1920]{0,1:T(8,128)(2,1)} concatenate(bf16[128,256]{0,1:T(8,128)(2,1)} %get-tuple-element.147, bf16[128,256]{0,1:T(8,128)(2,1)} %get-tuple-element.149, bf16[128,256]{0,1:T(8,128)(2,1)} %get-tuple-element.151, bf16[128,256]{0,1:T(8,128)(2,1)} %get-tuple-element.153, bf16[128,256]{0,1:T(8,128)(2,1)} %get-tuple-element.155, ...), dimensions={1} | concatenate | bytes 983040 | tf_op jit(solution)/shard_map/concatenate | solution.py:165
  113.6 7.1 %collective-permute-start.5 = (bf16[128,1920]{0,1:T(8,128)(2,1)}, bf16[128,1920]{0,1:T(8,128)(2,1)}, u32[]{:S(2)}, u32[]{:S(2)}) collective-permute-start(bf16[128,1920]{0,1:T(8,128)(2,1)} %concatenate.101), channel_id=1, source_target_pairs={{0,496},{16,480},{32,464},{48,448},{64,432},{80,416},{96,400},{112... | collective-permute-start | bytes 1474568 | tf_op jit(solution)/shard_map/ppermute | solution.py:166
  122.2 21.1 %collective-permute-done.5 = bf16[128,1920]{0,1:T(8,128)(2,1)} collective-permute-done((bf16[128,1920]{0,1:T(8,128)(2,1)}, bf16[128,1920]{0,1:T(8,128)(2,1)}, u32[]{:S(2)}, u32[]{:S(2)}) %collective-permute-start.5) | collective-permute-done | bytes 491552 | tf_op jit(solution)/shard_map/ppermute | solution.py:166
  174.3 2.3 fusion.158
  179.7 4.7 %all-to-all-start.1 = ((bf16[16,20,2048]{2,1,0:T(8,128)(2,1)}), bf16[16,20,2048]{2,1,0:T(8,128)(2,1)}, u32[]{:S(2)}, u32[]{:S(2)}) async-start(bf16[16,20,2048]{2,1,0:T(8,128)(2,1)} %pad_maximum_fusion), calls=%async_computation.1 | async-start | bytes 3145728 | tf_op jit(solution)/shard_map/all_to_all | solution.py:208
  185.0 21.4 %all-to-all-done.1 = bf16[16,20,2048]{2,1,0:T(8,128)(2,1)} async-done(((bf16[16,20,2048]{2,1,0:T(8,128)(2,1)}), bf16[16,20,2048]{2,1,0:T(8,128)(2,1)}, u32[]{:S(2)}, u32[]{:S(2)}) %all-to-all-start.1) | async-done | bytes 1310752 | tf_op jit(solution)/shard_map/all_to_all | solution.py:208
  213.2 4.1 %collective-permute-done.7 = bf16[4,2,2048]{2,1,0:T(2,128)(2,1)S(1)} collective-permute-done((bf16[4,2,2048]{2,1,0:T(2,128)(2,1)S(1)}, bf16[4,2,2048]{2,1,0:T(2,128)(2,1)S(1)}, u32[]{:S(2)}, u32[]{:S(2)}) %collective-permute-start.7) | collective-permute-done | bytes 32800 | tf_op jit(solution)/shard_map/ppermute | solution.py:274
  218.1 3.1 collective-permute-start.6
  221.4 5.6 %collective-permute-done.6 = bf16[4,2,2048]{2,1,0:T(2,128)(2,1)S(1)} collective-permute-done((bf16[4,2,2048]{2,1,0:T(2,128)(2,1)S(1)}, bf16[4,2,2048]{2,1,0:T(2,128)(2,1)S(1)}, u32[]{:S(2)}, u32[]{:S(2)}) %collective-permute-start.6) | collective-permute-done | bytes 32800 | tf_op jit(solution)/shard_map/ppermute | solution.py:273
  228.8 4.6 %all-to-all-start.2 = ((bf16[16,16,2048]{2,1,0:T(8,128)(2,1)}), bf16[16,16,2048]{2,1,0:T(8,128)(2,1)}, u32[]{:S(2)}, u32[]{:S(2)}) async-start(bf16[16,16,2048]{2,1,0:T(8,128)(2,1)} %broadcast_in_dim.119), calls=%async_computation.2 | async-start | bytes 2097152 | tf_op jit(solution)/shard_map/all_to_all | solution.py:133
  234.0 14.4 %all-to-all-done.2 = bf16[16,16,2048]{2,1,0:T(8,128)(2,1)} async-done(((bf16[16,16,2048]{2,1,0:T(8,128)(2,1)}), bf16[16,16,2048]{2,1,0:T(8,128)(2,1)}, u32[]{:S(2)}, u32[]{:S(2)}) %all-to-all-start.2) | async-done | bytes 1048608 | tf_op jit(solution)/shard_map/all_to_all | solution.py:133
  248.4 2.6 fusion.239
  251.0 2.2 fusion.238
  253.2 2.1 fusion.240
  260.3 7.1 %concatenate.111 = bf16[128,896]{0,1:T(8,128)(2,1)} concatenate(bf16[128,256]{0,1:T(8,128)(2,1)} %get-tuple-element.167, bf16[128,256]{0,1:T(8,128)(2,1)} %get-tuple-element.169, bf16[128,256]{0,1:T(8,128)(2,1)} %get-tuple-element.171, bf16[128,1]{0,1:T(2,128)(2,1)} %get-tuple-element.146, bf16[128,1]{0,1:T(2,128)(2,1)} %get-tuple-element.145, bf16[128,126]{0,1:T(8,128)(2,1)} %broadcast_in_dim.120), dimensions={1} | concatenate | bytes 458752 | tf_op jit(solution)/shard_map/concatenate | solution.py:165
  267.4 7.6 %collective-permute-start.8 = (bf16[128,896]{0,1:T(8,128)(2,1)}, bf16[128,896]{0,1:T(8,128)(2,1)S(1)}, u32[]{:S(2)}, u32[]{:S(2)}) collective-permute-start(bf16[128,896]{0,1:T(8,128)(2,1)} %concatenate.111), channel_id=1, source_target_pairs={{0,496},{16,480},{32,464},{48,448},{64,432},{80,416},{96,400},{112... | collective-permute-start | bytes 688136 | tf_op jit(solution)/shard_map/ppermute | solution.py:166
  276.1 12.5 %collective-permute-done.8 = bf16[128,896]{0,1:T(8,128)(2,1)S(1)} collective-permute-done((bf16[128,896]{0,1:T(8,128)(2,1)}, bf16[128,896]{0,1:T(8,128)(2,1)S(1)}, u32[]{:S(2)}, u32[]{:S(2)}) %collective-permute-start.8) | collective-permute-done | bytes 229408 | tf_op jit(solution)/shard_map/ppermute | solution.py:166
  328.7 5.5 %all-to-all-start.3 = ((bf16[16,22,2048]{2,1,0:T(8,128)(2,1)}), bf16[16,22,2048]{2,1,0:T(8,128)(2,1)}, u32[]{:S(2)}, u32[]{:S(2)}) async-start(bf16[16,22,2048]{2,1,0:T(8,128)(2,1)} %pad_maximum_fusion.1), calls=%async_computation.3 | async-start | bytes 3145728 | tf_op jit(solution)/shard_map/all_to_all | solution.py:208
  340.7 2.6 fusion
  343.3 13.1 %all-to-all-done.3 = bf16[16,22,2048]{2,1,0:T(8,128)(2,1)} async-done(((bf16[16,22,2048]{2,1,0:T(8,128)(2,1)}), bf16[16,22,2048]{2,1,0:T(8,128)(2,1)}, u32[]{:S(2)}, u32[]{:S(2)}) %all-to-all-start.3) | async-done | bytes 1441824 | tf_op jit(solution)/shard_map/all_to_all | solution.py:208
  358.4 7.0 %collective-permute-start.9 = (bf16[4,4,2048]{2,1,0:T(4,128)(2,1)S(1)}, bf16[4,4,2048]{2,1,0:T(4,128)(2,1)S(1)}, u32[]{:S(2)}, u32[]{:S(2)}) collective-permute-start(bf16[4,4,2048]{2,1,0:T(4,128)(2,1)S(1)} %select_bitcast_fusion), channel_id=1, source_target_pairs={{0,496},{16,480},{32,464},{48,448},{64,432},{80,416},{96,400},{112... | collective-permute-start | bytes 196616 | tf_op jit(solution)/shard_map/ppermute | solution.py:298
  367.1 2.1 collective-permute-done.9
  (392 shorter events, 128.0 us)
Async XLA Ops:
  0.6 83.4 %copy-start = (bf16[1,2048,256]{2,1,0:T(8,128)(2,1)S(1)}, bf16[1,2048,256]{2,1,0:T(8,128)(2,1)}, u32[]{:S(2)}) copy-start(bf16[1,2048,256]{2,1,0:T(8,128)(2,1)} %param.15) | copy-start | bytes 3145732
  3.3 17.8 %collective-permute-start = (bf16[4,4,2048]{2,1,0:T(4,128)(2,1)S(1)}, bf16[4,4,2048]{2,1,0:T(4,128)(2,1)S(1)}, u32[]{:S(2)}, u32[]{:S(2)}) collective-permute-start(bf16[4,4,2048]{2,1,0:T(4,128)(2,1)S(1)} %broadcast_select_fusion.6), channel_id=1, source_target_pairs={{0,496},{16,480},{32,464},{48,448},{64,432},{80,416},{96,400},{112... | collective-permute-start | bytes 196616 | tf_op jit(solution)/shard_map/ppermute | solution.py:125
  22.8 61.2 %all-to-all-start = ((bf16[16,32,2048]{2,1,0:T(8,128)(2,1)}), bf16[16,32,2048]{2,1,0:T(8,128)(2,1)S(1)}, u32[]{:S(2)}, u32[]{:S(2)}) async-start(bf16[16,32,2048]{2,1,0:T(8,128)(2,1)} %broadcast_in_dim.111), calls=%async_computation | async-start | bytes 4194304 | tf_op jit(solution)/shard_map/all_to_all | solution.py:133
  28.6 36.9 %collective-permute-start.4 = (bf16[64,2048]{1,0:T(8,128)(2,1)}, bf16[64,2048]{1,0:T(8,128)(2,1)S(1)}, u32[]{:S(2)}, u32[]{:S(2)}) collective-permute-start(bf16[64,2048]{1,0:T(8,128)(2,1)} %bitcast.282), channel_id=1, source_target_pairs={{9,0},{0,1},{1,2},{8,3},{11,4},{2,5},{3,6},{10,7},{13,8},{4,9},{5,... | collective-permute-start | bytes 786440 | tf_op jit(solution)/shard_map/ppermute | solution.py:109
  32.0 34.5 %collective-permute-start.3 = (bf16[64,2048]{1,0:T(8,128)(2,1)}, bf16[64,2048]{1,0:T(8,128)(2,1)}, u32[]{:S(2)}, u32[]{:S(2)}) collective-permute-start(bf16[64,2048]{1,0:T(8,128)(2,1)} %bitcast.283), channel_id=1, source_target_pairs={{8,0},{9,1},{0,2},{1,3},{10,4},{11,5},{2,6},{3,7},{12,8},{13,9},{4... | collective-permute-start | bytes 786440 | tf_op jit(solution)/shard_map/ppermute | solution.py:109
  34.0 41.6 %collective-permute-start.2 = (bf16[64,2048]{1,0:T(8,128)(2,1)}, bf16[64,2048]{1,0:T(8,128)(2,1)}, u32[]{:S(2)}, u32[]{:S(2)}) collective-permute-start(bf16[64,2048]{1,0:T(8,128)(2,1)} %bitcast.284), channel_id=1, source_target_pairs={{1,0},{8,1},{9,2},{0,3},{3,4},{10,5},{11,6},{2,7},{5,8},{12,9},{13... | collective-permute-start | bytes 786440 | tf_op jit(solution)/shard_map/ppermute | solution.py:109
  36.7 45.1 %collective-permute-start.1 = (bf16[64,2048]{1,0:T(8,128)(2,1)}, bf16[64,2048]{1,0:T(8,128)(2,1)}, u32[]{:S(2)}, u32[]{:S(2)}) collective-permute-start(bf16[64,2048]{1,0:T(8,128)(2,1)} %bitcast.285), channel_id=1, source_target_pairs={{0,0},{1,1},{8,2},{9,3},{2,4},{3,5},{10,6},{11,7},{4,8},{5,9},{12,... | collective-permute-start | bytes 786440 | tf_op jit(solution)/shard_map/ppermute | solution.py:109
  97.7 46.8 %copy-start.77 = (f32[128,1]{0,1:T(1,128)S(1)}, f32[128,1]{0,1:T(1,128)}, u32[]{:S(2)}) copy-start(f32[128,1]{0,1:T(1,128)} %broadcast_in_dim.114) | copy-start | bytes 1540
  97.7 46.8 %copy-start.78 = (f32[128,1]{0,1:T(1,128)S(1)}, f32[128,1]{0,1:T(1,128)}, u32[]{:S(2)}) copy-start(f32[128,1]{0,1:T(1,128)} %broadcast_in_dim.113) | copy-start | bytes 1540
  113.6 29.7 %collective-permute-start.5 = (bf16[128,1920]{0,1:T(8,128)(2,1)}, bf16[128,1920]{0,1:T(8,128)(2,1)}, u32[]{:S(2)}, u32[]{:S(2)}) collective-permute-start(bf16[128,1920]{0,1:T(8,128)(2,1)} %concatenate.101), channel_id=1, source_target_pairs={{0,496},{16,480},{32,464},{48,448},{64,432},{80,416},{96,400},{112... | collective-permute-start | bytes 1474568 | tf_op jit(solution)/shard_map/ppermute | solution.py:166
  122.2 25.2 %copy-start.74 = (pred[128,128]{0,1:T(32,128)(4,1)}, pred[128,128]{0,1:T(32,128)(4,1)S(1)}, u32[]{:S(2)}) copy-start(pred[128,128]{0,1:T(32,128)(4,1)S(1)} %fusion.152) | copy-start | bytes 49156
  145.6 28.7 %copy-start.81 = (f32[128]{0:T(128)}, f32[128]{0:T(128)S(1)}, u32[]{:S(2)}) copy-start(f32[128]{0:T(128)S(1)} %get-tuple-element.142) | copy-start | bytes 1540
  145.6 31.9 %copy-start.79 = (f32[128]{0:T(128)}, f32[128]{0:T(128)S(1)}, u32[]{:S(2)}) copy-start(f32[128]{0:T(128)S(1)} %get-tuple-element.143) | copy-start | bytes 1540
  179.7 26.7 %all-to-all-start.1 = ((bf16[16,20,2048]{2,1,0:T(8,128)(2,1)}), bf16[16,20,2048]{2,1,0:T(8,128)(2,1)}, u32[]{:S(2)}, u32[]{:S(2)}) async-start(bf16[16,20,2048]{2,1,0:T(8,128)(2,1)} %pad_maximum_fusion), calls=%async_computation.1 | async-start | bytes 3145728 | tf_op jit(solution)/shard_map/all_to_all | solution.py:208
  208.8 20.0 %copy-start.21 = (bf16[8,2048]{1,0:T(8,128)(2,1)}, bf16[8,2048]{1,0:T(8,128)(2,1)S(1)}, u32[]{:S(2)}) copy-start(bf16[8,2048]{1,0:T(8,128)(2,1)S(1)} %get-tuple-element.56) | copy-start | bytes 98308
  208.8 20.0 %copy-start.23 = (bf16[8,2048]{1,0:T(8,128)(2,1)}, bf16[8,2048]{1,0:T(8,128)(2,1)S(1)}, u32[]{:S(2)}) copy-start(bf16[8,2048]{1,0:T(8,128)(2,1)S(1)} %get-tuple-element.57) | copy-start | bytes 98308
  209.5 23.9 %copy-start.37 = (bf16[128,256]{0,1:T(8,128)(2,1)S(1)}, bf16[128,256]{0,1:T(8,128)(2,1)}, u32[]{:S(2)}) copy-start(bf16[128,256]{0,1:T(8,128)(2,1)} %get-tuple-element.42) | copy-start | bytes 196612
  210.2 7.1 %collective-permute-start.7 = (bf16[4,2,2048]{2,1,0:T(2,128)(2,1)S(1)}, bf16[4,2,2048]{2,1,0:T(2,128)(2,1)S(1)}, u32[]{:S(2)}, u32[]{:S(2)}) collective-permute-start(bf16[4,2,2048]{2,1,0:T(2,128)(2,1)S(1)} %pad_maximum_fusion.30), channel_id=1, source_target_pairs={{16,0},{32,16},{48,32},{64,48},{80,64},{96,80},{112,96},{128,112},... | collective-permute-start | bytes 98312 | tf_op jit(solution)/shard_map/ppermute | solution.py:274
  218.1 8.8 %collective-permute-start.6 = (bf16[4,2,2048]{2,1,0:T(2,128)(2,1)S(1)}, bf16[4,2,2048]{2,1,0:T(2,128)(2,1)S(1)}, u32[]{:S(2)}, u32[]{:S(2)}) collective-permute-start(bf16[4,2,2048]{2,1,0:T(2,128)(2,1)S(1)} %get-tuple-element.34), channel_id=1, source_target_pairs={{0,16},{16,32},{32,48},{48,64},{64,80},{80,96},{96,112},{112,128},... | collective-permute-start | bytes 98312 | tf_op jit(solution)/shard_map/ppermute | solution.py:273
  228.8 19.6 %all-to-all-start.2 = ((bf16[16,16,2048]{2,1,0:T(8,128)(2,1)}), bf16[16,16,2048]{2,1,0:T(8,128)(2,1)}, u32[]{:S(2)}, u32[]{:S(2)}) async-start(bf16[16,16,2048]{2,1,0:T(8,128)(2,1)} %broadcast_in_dim.119), calls=%async_computation.2 | async-start | bytes 2097152 | tf_op jit(solution)/shard_map/all_to_all | solution.py:133
  267.4 23.7 %copy-start.39 = (bf16[128,256]{0,1:T(8,128)(2,1)S(1)}, bf16[128,256]{0,1:T(8,128)(2,1)}, u32[]{:S(2)}) copy-start(bf16[128,256]{0,1:T(8,128)(2,1)} %get-tuple-element.43) | copy-start | bytes 196612
  267.4 24.0 %copy-start.41 = (bf16[128,128]{0,1:T(8,128)(2,1)S(1)}, bf16[128,128]{0,1:T(8,128)(2,1)}, u32[]{:S(2)}) copy-start(bf16[128,128]{0,1:T(8,128)(2,1)} %get-tuple-element.91) | copy-start | bytes 98308
  267.4 24.0 %copy-start.42 = (bf16[128,128]{0,1:T(8,128)(2,1)S(1)}, bf16[128,128]{0,1:T(8,128)(2,1)}, u32[]{:S(2)}) copy-start(bf16[128,128]{0,1:T(8,128)(2,1)} %get-tuple-element.92) | copy-start | bytes 98308
  267.4 21.2 %collective-permute-start.8 = (bf16[128,896]{0,1:T(8,128)(2,1)}, bf16[128,896]{0,1:T(8,128)(2,1)S(1)}, u32[]{:S(2)}, u32[]{:S(2)}) collective-permute-start(bf16[128,896]{0,1:T(8,128)(2,1)} %concatenate.111), channel_id=1, source_target_pairs={{0,496},{16,480},{32,464},{48,448},{64,432},{80,416},{96,400},{112... | collective-permute-start | bytes 688136 | tf_op jit(solution)/shard_map/ppermute | solution.py:166
  328.7 27.6 %all-to-all-start.3 = ((bf16[16,22,2048]{2,1,0:T(8,128)(2,1)}), bf16[16,22,2048]{2,1,0:T(8,128)(2,1)}, u32[]{:S(2)}, u32[]{:S(2)}) async-start(bf16[16,22,2048]{2,1,0:T(8,128)(2,1)} %pad_maximum_fusion.1), calls=%async_computation.3 | async-start | bytes 3145728 | tf_op jit(solution)/shard_map/all_to_all | solution.py:208
  340.7 17.4 %copy-start.46 = (bf16[2,2048]{1,0:T(2,128)(2,1)S(1)}, bf16[2,2048]{1,0:T(2,128)(2,1)}, u32[]{:S(2)}) copy-start(bf16[2,2048]{1,0:T(2,128)(2,1)} %copy-done.45) | copy-start | bytes 24580
  340.7 17.4 %copy-start.48 = (bf16[2,2048]{1,0:T(2,128)(2,1)S(1)}, bf16[2,2048]{1,0:T(2,128)(2,1)}, u32[]{:S(2)}) copy-start(bf16[2,2048]{1,0:T(2,128)(2,1)} %copy-done.47) | copy-start | bytes 24580
  340.7 17.4 %copy-start.50 = (bf16[2,2048]{1,0:T(2,128)(2,1)S(1)}, bf16[2,2048]{1,0:T(2,128)(2,1)}, u32[]{:S(2)}) copy-start(bf16[2,2048]{1,0:T(2,128)(2,1)} %copy-done.49) | copy-start | bytes 24580
  340.7 17.4 %copy-start.52 = (bf16[2,2048]{1,0:T(2,128)(2,1)S(1)}, bf16[2,2048]{1,0:T(2,128)(2,1)}, u32[]{:S(2)}) copy-start(bf16[2,2048]{1,0:T(2,128)(2,1)} %copy-done.51) | copy-start | bytes 24580
  340.7 17.4 %copy-start.54 = (bf16[2,2048]{1,0:T(2,128)(2,1)S(1)}, bf16[2,2048]{1,0:T(2,128)(2,1)}, u32[]{:S(2)}) copy-start(bf16[2,2048]{1,0:T(2,128)(2,1)} %copy-done.53) | copy-start | bytes 24580
  340.7 25.4 %copy-start.90 = (bf16[128,2048]{1,0:T(8,128)(2,1)S(1)}, bf16[128,2048]{1,0:T(8,128)(2,1)}, u32[]{:S(2)}) copy-start(bf16[128,2048]{1,0:T(8,128)(2,1)} %get-tuple-element.37) | copy-start | bytes 1572868
  358.4 10.8 %collective-permute-start.9 = (bf16[4,4,2048]{2,1,0:T(4,128)(2,1)S(1)}, bf16[4,4,2048]{2,1,0:T(4,128)(2,1)S(1)}, u32[]{:S(2)}, u32[]{:S(2)}) collective-permute-start(bf16[4,4,2048]{2,1,0:T(4,128)(2,1)S(1)} %select_bitcast_fusion), channel_id=1, source_target_pairs={{0,496},{16,480},{32,464},{48,448},{64,432},{80,416},{96,400},{112... | collective-permute-start | bytes 196616 | tf_op jit(solution)/shard_map/ppermute | solution.py:298
  (73 other events, 322.4 us)

commit v2 on v1

v2 whole, which is shorter than its diff:
```python
import functools
import math

import jax
import jax.numpy as jnp
from jax import lax
from jax.experimental import pallas as pl
from jax.experimental.pallas import tpu as pltpu
from jax.sharding import PartitionSpec as P

HD = 128
KVH = 4
EPSILON = 1e-05
BF = jnp.bfloat16
F32 = jnp.float32


def mm(left, right, dims=((1,), (0,))):
    return lax.dot_general(left, right, (dims, ((), ())), preferred_element_type=F32)


def mm_t(left, right):
    return mm(left, right, ((1,), (1,)))


def t_mm(left, right):
    return mm(left, right, ((0,), (0,)))


def pair_mask(tokens, row_count):
    def parts(axis):
        i = lax.broadcasted_iota(jnp.int32, (tokens, tokens), axis)
        group = (i // row_count) % 4
        return group, (i // (4 * row_count)) * row_count + i % row_count

    (query_group, query_time), (key_group, key_time) = parts(0), parts(1)
    return (query_group == key_group) & (key_time <= query_time)


def array_of(gathered_ref, index, rows):
    at = (index // 2) * 2 * rows
    block = gathered_ref[:, at : at + 2 * rows, :].astype(F32)
    part = block[:, (index % 2) * rows : (index % 2 + 1) * rows]
    return part.reshape(part.shape[0] * rows, part.shape[2])


def lane_sum(block, lanes):
    lane = lax.broadcasted_iota(jnp.int32, block.shape, 1)
    chosen = functools.reduce(jnp.logical_or, [lane == i for i in lanes])
    return jnp.sum(jnp.where(chosen, block, 0.0), axis=1, keepdims=True)


def project_body(groups, rows, gathered, gain, query_mat, kv_mat, output_mat, *outs):
    gain_row = gain[...].astype(F32)
    for index, (acts, cot) in enumerate(groups):
        message, own = outs[2 * index], outs[2 * index + 1]
        tokens = own.shape[0]
        at = 0
        squares = []
        for act in acts:
            wide = array_of(gathered, act, rows)
            scaled = (wide * gain_row).astype(BF)
            squares.append(jnp.sum(wide * wide, axis=1, keepdims=True))
            for part in (mm(scaled, query_mat[...]), mm_t(scaled, kv_mat[...])):
                own[:, at : at + part.shape[1]] = part
                message[:, at : at + part.shape[1]] = part.astype(BF)
                at += part.shape[1]
        if cot is not None:
            part = mm_t(array_of(gathered, cot, rows).astype(BF), output_mat[...])
            own[:, at : at + part.shape[1]] = part
            message[:, at : at + part.shape[1]] = part.astype(BF)
            at += part.shape[1]
        lane = lax.broadcasted_iota(jnp.int32, (tokens, HD), 1)
        kept = jnp.zeros((tokens, HD), F32)
        sent = jnp.zeros((tokens, HD), F32)
        for i, square in enumerate(squares):
            high = square.astype(BF).astype(F32)
            kept = jnp.where(lane == i, square, kept)
            sent = jnp.where(lane == i, high, sent)
            sent = jnp.where(lane == len(squares) + i, square - high, sent)
        own[:, at : at + HD] = kept
        message[:, at : at + HD] = sent.astype(BF)


def stack_heads(columns):
    return jnp.concatenate([columns[:, i : i + HD] for i in range(0, columns.shape[1], HD)], axis=0)


def unstack_heads(stacked, tokens):
    return jnp.concatenate(
        [stacked[i : i + tokens] for i in range(0, stacked.shape[0], tokens)], axis=1
    )


def softmax_of(stacked, keys, mask):
    scores = mm_t(stacked, keys) / math.sqrt(HD)
    scores = jnp.where(mask, scores, -jnp.inf)
    weights = jnp.exp(scores - jnp.max(scores, axis=1, keepdims=True))
    return weights / jnp.sum(weights, axis=1, keepdims=True)


def attend_body(
    plan, head, own_x, got_x, own_s, got_s, gathered, gain, query_mat, kv_mat, output_mat, *rest
):
    last = plan["last"]
    if last:
        gain_before, rest = rest[0], rest[1:]
    block, normed_out, query_back_out, mixed_out = rest[:4]
    rows, columns = plan["rows"], query_mat.shape[1]
    shards = block.shape[0]
    tokens, half = shards * rows, query_mat.shape[0]
    eval_columns = columns + 2 * HD
    heads = columns // HD

    def total(own, got, at, size):
        return own[:, at : at + size] + got[:, at : at + size].astype(F32)

    def projected(own, got, place, count, has_cot):
        at = count * eval_columns + (columns if has_cot else 0)
        square = lane_sum(total(own, got, at, HD), (place, count + place))
        inverse = lax.rsqrt(square / (2 * half) + EPSILON)
        start = place * eval_columns
        queries = total(own, got, start, columns) * inverse
        keyvals = total(own, got, start + columns, 2 * HD) * inverse
        return queries, keyvals, inverse

    mask = pair_mask(tokens, rows // 4)
    mask = jnp.concatenate([mask.astype(jnp.int32)] * heads, axis=0) == 1

    queries, keyvals, _ = projected(own_x, got_x, 0, plan["count_x"], True)
    keys, values = keyvals[:, :HD].astype(BF), keyvals[:, HD:].astype(BF)
    probs = softmax_of(stack_heads(queries).astype(BF), keys, mask)
    mixed = unstack_heads(mm(probs.astype(BF), values), tokens).astype(BF)
    out_part = mm(mixed, output_mat[...])

    back_mixed = total(own_x, got_x, plan["count_x"] * eval_columns, columns)
    queries, keyvals, inverse = projected(
        own_s, got_s, plan["place_s"], plan["count_s"], plan["cot_s"]
    )
    keys, values = keyvals[:, :HD].astype(BF), keyvals[:, HD:].astype(BF)
    stacked = stack_heads(queries).astype(BF)
    probs = softmax_of(stacked, keys, mask)
    mixed_out[...] = unstack_heads(mm(probs.astype(BF), values), tokens).astype(BF)
    back = stack_heads(back_mixed).astype(BF)
    back_probs = mm_t(back, values)
    inner = jnp.sum(probs * back_probs, axis=1, keepdims=True)
    back_scores = probs * (back_probs - inner) / math.sqrt(HD)
    query_back = unstack_heads(mm(back_scores.astype(BF), keys), tokens).astype(BF)
    query_back_out[...] = query_back
    key_back = mm(back_scores.T.astype(BF), stacked)
    value_back = mm(probs.T.astype(BF), back)
    keyval_wide = jnp.concatenate([key_back, value_back], axis=1)
    keyval_back = keyval_wide.astype(BF)

    back_normed = mm_t(query_back, query_mat[...]) + mm(keyval_back, kv_mat[...])
    along = jnp.sum(query_back.astype(F32) * queries, axis=1, keepdims=True) + jnp.sum(
        keyval_back.astype(F32) * keyvals, axis=1, keepdims=True
    )
    gain_row = gain[...].astype(F32)
    unit = array_of(gathered, plan["stash"], rows) * inverse
    normed_out[...] = (unit * gain_row).astype(BF)
    back_part = inverse * (back_normed * gain_row - unit * (along / (2 * half)))
    gain_part = jnp.sum(back_normed * unit, axis=0, keepdims=True)

    both = jnp.concatenate(
        [out_part.reshape(shards, rows, half), back_part.reshape(shards, rows, half)], axis=1
    )
    block[:, :, :half] = both.astype(BF)

    turned = jnp.concatenate([key_back.T, value_back.T], axis=0)
    deep = 2 * rows
    per_block = turned.shape[0] // 4
    my_head = head[0]
    pieces = []
    for k in range(4):
        piece = turned[k * per_block : (k + 1) * per_block]
        pieces.append(
            jnp.concatenate([piece[i : i + deep] for i in range(0, per_block, deep)], axis=1)
        )
    wide_lanes = pieces[0].shape[1]
    for d in range(shards):
        k = (d % 2) + 2 * (d // (shards // 2))
        kept = jnp.where(my_head == (d % (shards // 2)) // 2, pieces[k], 0.0)
        block[d, :, half : half + wide_lanes] = kept.astype(BF)

    if last:
        gain_part = gain_part + gain_before[...]
        high = gain_part.astype(BF).astype(F32)
        width = half // rows
        spread = jnp.concatenate(
            [part[:, i * width : (i + 1) * width] for part in (high, gain_part - high) for i in range(rows)],
            axis=0,
        ).astype(BF)
        for d in range(shards):
            block[d, :, half + wide_lanes :] = spread
    else:
        rest[4][...] = gain_part


VMEM = pl.BlockSpec(memory_space=pltpu.VMEM)
SMEM = pl.BlockSpec(memory_space=pltpu.SMEM)
PARAMS = pltpu.CompilerParams(vmem_limit_bytes=44 * 2**20)


def on_device(
    carried_acts,
    fresh_acts,
    stashed_acts,
    carried_grads,
    fresh_grads,
    norm_gain,
    query_weight,
    keyval_weight,
    output_weight,
):
    sections = lax.axis_size("section")
    shards = lax.axis_size("tp")
    section = lax.axis_index("section")
    me = lax.axis_index("tp")
    lower = section < sections // 2
    ticks = stashed_acts.shape[2]
    width = carried_acts.shape[3]
    half = width // 2
    row_count = carried_acts.shape[2]
    rows = 4 * row_count
    tokens = rows * shards
    query_mat, output_mat = query_weight[0], output_weight[0]
    columns = query_mat.shape[1]
    mirror = [(i, sections - 1 - i) for i in range(sections)]
    kv_group = shards // KVH

    def halves(whole):
        first, second = whole[..., :half], whole[..., half:]
        return jnp.where(lower, first, second), jnp.where(lower, second, first)

    entering = jnp.stack(
        [carried_acts[0]] + [stashed_acts[0, :, k] for k in range(ticks)] + [carried_grads[0]]
    ).reshape(ticks + 2, 2 * row_count, width)
    own, other = halves(entering)
    arrived = lax.ppermute(other, "section", mirror)
    held = jnp.concatenate(
        [jnp.where(lower, own, arrived), jnp.where(lower, arrived, own)], axis=1
    )

    kv_own = keyval_weight[0].T
    sources = [[2 * j, 2 * j + 1, shards // 2 + 2 * j, shards // 2 + 2 * j + 1] for j in range(KVH)]
    fetched = [
        lax.ppermute(
            kv_own,
            "tp",
            [
                (sources[j][(i + 2 * k) % kv_group], kv_group * j + i)
                for j in range(KVH)
                for i in range(kv_group)
            ],
        )
        for k in range(2)
    ]
    second_chip = (me // 2) % 2 == 1
    mine = jnp.stack(
        [
            jnp.where(second_chip, fetched[1], fetched[0]),
            jnp.where(second_chip, fetched[0], fetched[1]),
        ]
    )
    swapped = lax.ppermute(mine, "tp", [(i, i ^ 1) for i in range(shards)])
    even = me % 2 == 0
    kv_mat = jnp.stack(
        [jnp.where(even, mine, swapped), jnp.where(even, swapped, mine)], axis=1
    ).reshape(2 * HD, half)

    def gather(local):
        count = local.shape[0]
        spread = jnp.broadcast_to(local.reshape(1, count * rows, half), (shards, count * rows, half))
        return lax.all_to_all(spread, "tp", split_axis=0, concat_axis=0, tiled=True)

    eval_columns = columns + 2 * HD

    def project(gathered, groups):
        shapes = []
        for acts, cot in groups:
            size = len(acts) * eval_columns + (0 if cot is None else columns) + HD
            shapes += [
                jax.ShapeDtypeStruct((tokens, size), BF),
                jax.ShapeDtypeStruct((tokens, size), F32),
            ]
        outs = pl.pallas_call(
            functools.partial(project_body, groups, rows),
            out_shape=shapes,
            in_specs=[VMEM] * 5,
            out_specs=[VMEM] * len(shapes),
            compiler_params=PARAMS,
        )(gathered, norm_gain, query_mat, kv_mat, output_mat)
        return [(outs[2 * i], outs[2 * i + 1]) for i in range(len(groups))]

    def exchange(message):
        return lax.ppermute(message, "section", mirror)

    my_head = (me // kv_group).astype(jnp.int32).reshape(1)
    kv_lanes = 2 * HD // 4 // (2 * rows) * tokens

    def attend(plan, pieces, gathered, gain_before):
        last = plan["last"]
        lanes = half + kv_lanes + (half // rows if last else 0)
        shapes = [
            jax.ShapeDtypeStruct((shards, 2 * rows, lanes), BF),
            jax.ShapeDtypeStruct((tokens, half), BF),
            jax.ShapeDtypeStruct((tokens, columns), BF),
            jax.ShapeDtypeStruct((tokens, columns), BF),
        ]
        if not last:
            shapes.append(jax.ShapeDtypeStruct((1, half), F32))
        extra = [gain_before] if last else []
        return pl.pallas_call(
            functools.partial(attend_body, plan),
            out_shape=shapes,
            in_specs=[SMEM] + [VMEM] * (9 + len(extra)),
            out_specs=[VMEM] * len(shapes),
            compiler_params=PARAMS,
        )(my_head, *pieces, gathered, norm_gain, query_mat, kv_mat, output_mat, *extra)

    def reduce_blocks(block):
        received = lax.all_to_all(block, "tp", split_axis=0, concat_axis=0, tiled=True)
        return jnp.sum(received.astype(F32), axis=0)

    def kv_rows(total):
        part = total[:, half : half + kv_lanes]
        return jnp.concatenate(
            [part[:, i : i + tokens] for i in range(0, kv_lanes, tokens)], axis=0
        ).astype(BF)

    def all_tokens(gathered, index):
        return gathered[:, index * rows : (index + 1) * rows].reshape(tokens, half)

    last = sections // 2 - 1
    ahead = [(i, i + 1) for i in range(last)] + [
        (sections - 1 - i, sections - 2 - i) for i in range(last)
    ]
    behind = [(b, a) for a, b in ahead]
    first_layer = (section == 0) | (section == sections - 1)
    last_layer = (section == last) | (section == last + 1)

    gathered = gather(held)
    kept = gathered
    cot_index = ticks + 1
    all_cots = [all_tokens(gathered, cot_index)]
    projected = project(gathered, [((0, 1), cot_index)] + [((k,), None) for k in range(2, 1 + ticks)])
    (message, own_x), later = projected[0], projected[1:]
    got_x = exchange(message)
    own_s, got_s = own_x, got_x
    act_rows, cot_rows = held[0], held[cot_index]
    gain_total = None
    out_rows, back_rows = [], []
    all_normed, all_query_back, all_kv_back, all_mixed = [], [], [], []
    for k in range(ticks):
        plan = {
            "last": k + 1 == ticks,
            "rows": rows,
            "count_x": 2 if k == 0 else 1,
            "place_s": 1 if k == 0 else 0,
            "count_s": 2 if k == 0 else 1,
            "cot_s": k == 0,
            "stash": 1 + k,
        }
        block, normed, query_back, mixed, *rest = attend(
            plan, (own_x, got_x, own_s, got_s), kept, gain_total
        )
        if k + 1 < ticks:
            gain_total = rest[0] if gain_total is None else gain_total + rest[0]
            block, message_s = lax.optimization_barrier((block, later[k][0]))
            own_s, got_s = later[k][1], exchange(message_s)
        total = reduce_blocks(block)
        layer_out = (act_rows.astype(F32) + total[:rows, :half]).astype(BF)
        back_input = (cot_rows.astype(F32) + total[rows:, :half]).astype(BF)
        out_rows.append(layer_out)
        back_rows.append(back_input)
        all_kv_back.append(kv_rows(total))
        all_normed.append(normed)
        all_query_back.append(query_back)
        all_mixed.append(mixed)
        if k + 1 < ticks:
            f = layer_out.reshape(2, 2, row_count, half)
            b = back_input.reshape(2, 2, row_count, half)
            going_up = jnp.stack([f[0, 0], f[1, 1], b[1, 0], b[0, 1]])
            going_down = jnp.stack([f[1, 0], f[0, 1], b[0, 0], b[1, 1]])
            going_up, going_down = lax.optimization_barrier((going_up, going_down))
            from_below = lax.ppermute(going_up, "section", ahead)
            from_above = lax.ppermute(going_down, "section", behind)
            from_below, from_above = lax.optimization_barrier((from_below, from_above))
            fresh = jnp.stack(
                [fresh_acts[0, k], fresh_acts[1, k], fresh_grads[0, k], fresh_grads[1, k]]
            )
            fresh = halves(fresh)[0]
            lo = jnp.where(first_layer, fresh, from_below)
            hi = jnp.where(last_layer, going_up, from_above)
            act_rows = jnp.concatenate([lo[0], hi[1], hi[0], lo[1]], axis=0)
            cot_rows = jnp.concatenate([hi[2], lo[3], lo[2], hi[3]], axis=0)
            gathered = gather(jnp.stack([act_rows, cot_rows]))
            all_cots.append(all_tokens(gathered, 1))
            ((message, own_x),) = project(gathered, [((0,), 1)])
            got_x = exchange(message)

    normed = jnp.concatenate(all_normed, axis=0)
    grad_query = t_mm(normed, jnp.concatenate(all_query_back, axis=0)).astype(BF)
    grad_keyval = mm(jnp.concatenate(all_kv_back, axis=1), normed).astype(BF).T
    grad_output = t_mm(
        jnp.concatenate(all_cots, axis=0), jnp.concatenate(all_mixed, axis=0)
    ).astype(BF)
    gain_lanes = total[:, half + kv_lanes :]
    grad_gain = (gain_lanes[:rows] + gain_lanes[rows:]).astype(BF).reshape(half)

    leaving = jnp.stack(out_rows + back_rows).reshape(2 * ticks, 2, 2 * row_count, half)
    lo_rows, hi_rows = leaving[:, 0], leaving[:, 1]
    mine, theirs = jnp.where(lower, lo_rows, hi_rows), jnp.where(lower, hi_rows, lo_rows)
    returned = lax.ppermute(theirs, "section", mirror)
    whole = jnp.concatenate(
        [jnp.where(lower, mine, returned), jnp.where(lower, returned, mine)], axis=2
    ).reshape(2, ticks, 2, row_count, width)
    whole = whole.transpose(0, 2, 1, 3, 4)
    return (
        whole[0][None],
        whole[1][None],
        grad_query[None],
        grad_keyval[None],
        grad_output[None],
        grad_gain[None],
    )


def solution(mesh):
    in_specs = (
        P("section", None, "tp", None),
        P(None, None, "tp", None),
        P("section", None, None, "tp", None),
        P("section", None, "tp", None),
        P(None, None, "tp", None),
        P("section", None),
        P("section", None, "tp"),
        P("section", None, "tp"),
        P("section", "tp", None),
    )
    out_specs = (
        P("section", None, None, "tp", None),
        P("section", None, None, "tp", None),
        P("section", None, "tp"),
        P("section", None, "tp"),
        P("section", None, "tp"),
        P("section", None),
    )
    return jax.shard_map(
        on_device, mesh=mesh, in_specs=in_specs, out_specs=out_specs, check_vma=False
    )
```

time: 376 us -> 251 us (0.67)
  the two profiles are of different devices: /device:TPU:30 before, /device:TPU:31 now
where the time goes in v2:
time: 251 us; the launch traced here: 249 us
  waiting for transfers between devices  115 us (46%)
  starting transfers between devices  68.6 us (27%)
  local copies, waits for them, and re-layouts  24.6 us (10%)
  blocking collectives  19.9 us (8%)
  Pallas kernels  7.67 us (3%)
  other arithmetic  6.66 us (3%)
  matrix products  4.96 us (2%)
    ppermute x3, waiting for transfers between devices, exchange(): return lax.ppermute(message, 'section', mirror)  37.4 us
    ppermute x2, waiting for transfers between devices, on_device(): lax.ppermute(kv_own, 'tp', [(sources[j][(i + 2 * k) % kv_group], kv_group...  34.3 us
    all_to_all x2, waiting for transfers between devices, reduce_blocks(): lax.all_to_all(block, 'tp', split_axis=0, concat_axis=0, tiled=True)  31.2 us
    all_to_all x1, blocking collectives, gather(): return lax.all_to_all(spread, 'tp', split_axis=0, concat_axis=0, tiled=True)  19.9 us
    unnamed x103, local copies, waits for them, and re-layouts  17.6 us
    ppermute x3, starting transfers between devices, exchange(): return lax.ppermute(message, 'section', mirror)  16.3 us
    ppermute x1, starting transfers between devices, on_device(): arrived = lax.ppermute(other, 'section', mirror)  12.9 us
    all_to_all x2, starting transfers between devices, reduce_blocks(): lax.all_to_all(block, 'tp', split_axis=0, concat_axis=0, tiled=True)  12.7 us
  transfers between devices with their start and end apart: 13, of which 10 were waited for; matrix products, arithmetic and copies ran while one was open for 4% of the time, Pallas kernels for 0%

profile of v2, /device:TPU:31, one launch (start us, length us, event | category | flops | bytes accessed | tf_op | source)
XLA Modules:
  0.0 249.3 jit_solution(572627701964666593)
XLA Ops:
  3.2 12.9 %collective-permute-start = (bf16[4,4,2048]{2,1,0:T(4,128)(2,1)S(1)}, bf16[4,4,2048]{2,1,0:T(4,128)(2,1)S(1)}, u32[]{:S(2)}, u32[]{:S(2)}) collective-permute-start(bf16[4,4,2048]{2,1,0:T(4,128)(2,1)S(1)} %broadcast_select_fusion.6), channel_id=1, source_target_pairs={{0,496},{16,480},{32,464},{48,448},{64,432},{80,416},{96,400},{112... | collective-permute-start | bytes 196616 | tf_op jit(solution)/shard_map/ppermute | solution.py:240
  16.1 4.4 %collective-permute-done = bf16[4,4,2048]{2,1,0:T(4,128)(2,1)S(1)} collective-permute-done((bf16[4,4,2048]{2,1,0:T(4,128)(2,1)S(1)}, bf16[4,4,2048]{2,1,0:T(4,128)(2,1)S(1)}, u32[]{:S(2)}, u32[]{:S(2)}) %collective-permute-start) | collective-permute-done | bytes 65568 | tf_op jit(solution)/shard_map/ppermute | solution.py:240
  20.7 1.6 broadcast_in_dim.24
  22.3 6.6 %all-to-all-start = ((bf16[16,32,2048]{2,1,0:T(8,128)(2,1)}), bf16[16,32,2048]{2,1,0:T(8,128)(2,1)S(1)}, u32[]{:S(2)}, u32[]{:S(2)}) async-start(bf16[16,32,2048]{2,1,0:T(8,128)(2,1)} %broadcast_in_dim.24), calls=%async_computation | async-start | bytes 4194304 | tf_op jit(solution)/shard_map/all_to_all | solution.py:275
  28.9 3.4 %collective-permute-start.2 = (bf16[64,2048]{1,0:T(8,128)(2,1)S(1)}, bf16[64,2048]{1,0:T(8,128)(2,1)S(1)}, u32[]{:S(2)}, u32[]{:S(2)}) collective-permute-start(bf16[64,2048]{1,0:T(8,128)(2,1)S(1)} %bitcast.121), channel_id=1, source_target_pairs={{0,0},{1,1},{8,2},{9,3},{2,4},{3,5},{10,6},{11,7},{4,8},{5,9},{12,... | collective-permute-start | bytes 786440 | tf_op jit(solution)/shard_map/ppermute | solution.py:248
  32.3 1.9 collective-permute-start.1
  34.2 30.3 %collective-permute-done.2 = bf16[64,2048]{1,0:T(8,128)(2,1)S(1)} collective-permute-done((bf16[64,2048]{1,0:T(8,128)(2,1)S(1)}, bf16[64,2048]{1,0:T(8,128)(2,1)S(1)}, u32[]{:S(2)}, u32[]{:S(2)}) %collective-permute-start.2) | collective-permute-done | bytes 262176 | tf_op jit(solution)/shard_map/ppermute | solution.py:248
  64.5 3.9 %collective-permute-done.1 = bf16[64,2048]{1,0:T(8,128)(2,1)S(1)} collective-permute-done((bf16[64,2048]{1,0:T(8,128)(2,1)S(1)}, bf16[64,2048]{1,0:T(8,128)(2,1)S(1)}, u32[]{:S(2)}, u32[]{:S(2)}) %collective-permute-start.1) | collective-permute-done | bytes 262176 | tf_op jit(solution)/shard_map/ppermute | solution.py:248
  69.4 2.8 %collective-permute-start.3 = (bf16[2,64,2048]{2,1,0:T(8,128)(2,1)}, bf16[2,64,2048]{2,1,0:T(8,128)(2,1)S(1)}, u32[]{:S(2)}, u32[]{:S(2)}) collective-permute-start(bf16[2,64,2048]{2,1,0:T(8,128)(2,1)} %pad_maximum_fusion.1), channel_id=1, source_target_pairs={{0,1},{1,0},{2,3},{3,2},{4,5},{5,4},{6,7},{7,6},{8,9},{9,8},{10,11... | collective-permute-start | bytes 1572872 | tf_op jit(solution)/shard_map/ppermute | solution.py:266
  72.2 1.7 collective-permute-done.3
  77.2 2.6 %shard_map.136 = (bf16[128,1408]{1,0:T(8,128)(2,1)}, f32[128,1408]{1,0:T(8,128)S(1)}, bf16[128,640]{1,0:T(8,128)(2,1)S(1)}, f32[128,640]{1,0:T(8,128)S(1)}) custom-call(bf16[16,32,2048]{2,1,0:T(8,128)(2,1)S(1)} %all-to-all-done.gathered, bf16[1,2048]{1,0:T(2,128)(2,1)S(1)} %copy-done.17, bf16[2048,256]{1,0:T(8,128)(2,1)S(1)} %bitcast.105, ...), custom_call_target="tpu_custom_call" | custom-call | tf_op jit(solution)/shard_map/pallas_call | solution.py:287
  82.0 6.8 %collective-permute-start.4 = (bf16[128,1408]{1,0:T(8,128)(2,1)}, bf16[128,1408]{1,0:T(8,128)(2,1)S(1)}, u32[]{:S(2)}, u32[]{:S(2)}) collective-permute-start(bf16[128,1408]{1,0:T(8,128)(2,1)} %get-tuple-element.28), channel_id=1, source_target_pairs={{0,496},{16,480},{32,464},{48,448},{64,432},{80,416},{96,400},{112... | collective-permute-start | bytes 1081352 | tf_op jit(solution)/shard_map/ppermute | solution.py:297
  88.8 19.3 %collective-permute-done.4.got_x.got_s = bf16[128,1408]{1,0:T(8,128)(2,1)S(1)} collective-permute-done((bf16[128,1408]{1,0:T(8,128)(2,1)}, bf16[128,1408]{1,0:T(8,128)(2,1)S(1)}, u32[]{:S(2)}, u32[]{:S(2)}) %collective-permute-start.4) | collective-permute-done | bytes 360480 | tf_op jit(solution)/shard_map/ppermute | solution.py:297
  111.7 2.0 shard_map.137
  116.9 6.1 %all-to-all-start.1 = ((bf16[16,16,2560]{2,1,0:T(8,128)(2,1)}), bf16[16,16,2560]{2,1,0:T(8,128)(2,1)}, u32[]{:S(2)}, u32[]{:S(2)}) async-start(bf16[16,16,2560]{2,1,0:T(8,128)(2,1)} %copy-done.11), calls=%async_computation.1 | async-start | bytes 2621440 | tf_op jit(solution)/shard_map/all_to_all | solution.py:323
  123.6 17.8 %all-to-all-done.1 = bf16[16,16,2560]{2,1,0:T(8,128)(2,1)} async-done(((bf16[16,16,2560]{2,1,0:T(8,128)(2,1)}), bf16[16,16,2560]{2,1,0:T(8,128)(2,1)}, u32[]{:S(2)}, u32[]{:S(2)}) %all-to-all-start.1) | async-done | bytes 1310752 | tf_op jit(solution)/shard_map/all_to_all | solution.py:323
  141.4 1.5 convert_reduce_fusion.1
  143.3 2.1 collective-permute-start.6
  145.3 4.1 %collective-permute-start.5 = (bf16[4,2,2048]{2,1,0:T(2,128)(2,1)S(1)}, bf16[4,2,2048]{2,1,0:T(2,128)(2,1)}, u32[]{:S(2)}, u32[]{:S(2)}) collective-permute-start(bf16[4,2,2048]{2,1,0:T(2,128)(2,1)S(1)} %get-tuple-element.32), channel_id=1, source_target_pairs={{0,16},{16,32},{32,48},{48,64},{64,80},{80,96},{96,112},{112,128},... | collective-permute-start | bytes 98312 | tf_op jit(solution)/shard_map/ppermute | solution.py:387
  150.4 3.0 %collective-permute-done.5 = bf16[4,2,2048]{2,1,0:T(2,128)(2,1)} collective-permute-done((bf16[4,2,2048]{2,1,0:T(2,128)(2,1)S(1)}, bf16[4,2,2048]{2,1,0:T(2,128)(2,1)}, u32[]{:S(2)}, u32[]{:S(2)}) %collective-permute-start.5) | collective-permute-done | bytes 32800 | tf_op jit(solution)/shard_map/ppermute | solution.py:387
  155.1 19.9 %all_to_all.20.gathered = bf16[16,16,2048]{2,1,0:T(8,128)(2,1)S(1)} all-to-all(bf16[16,16,2048]{2,1,0:T(8,128)(2,1)S(1)} %broadcast_in_dim.26), channel_id=1, replica_groups=mesh['section'=32,'tp'=16] {'tp'}, dimensions={0} | all-to-all | bytes 2097152 | tf_op jit(solution)/shard_map/all_to_all | solution.py:275
  176.1 6.2 %collective-permute-start.7 = (bf16[128,896]{1,0:T(8,128)(2,1)S(1)}, bf16[128,896]{1,0:T(8,128)(2,1)S(1)}, u32[]{:S(2)}, u32[]{:S(2)}) collective-permute-start(bf16[128,896]{1,0:T(8,128)(2,1)S(1)} %get-tuple-element.37), channel_id=1, source_target_pairs={{0,496},{16,480},{32,464},{48,448},{64,432},{80,416},{96,400},{112... | collective-permute-start | bytes 688136 | tf_op jit(solution)/shard_map/ppermute | solution.py:297
  182.3 3.3 %collective-permute-start.8 = (bf16[128,640]{1,0:T(8,128)(2,1)S(1)}, bf16[128,640]{1,0:T(8,128)(2,1)S(1)}, u32[]{:S(2)}, u32[]{:S(2)}) collective-permute-start(bf16[128,640]{1,0:T(8,128)(2,1)S(1)} %copy-done.21), channel_id=1, source_target_pairs={{0,496},{16,480},{32,464},{48,448},{64,432},{80,416},{96,400},{112... | collective-permute-start | bytes 491528 | tf_op jit(solution)/shard_map/ppermute | solution.py:297
  185.6 18.1 %collective-permute-done.8.got_s = bf16[128,640]{1,0:T(8,128)(2,1)S(1)} collective-permute-done((bf16[128,640]{1,0:T(8,128)(2,1)S(1)}, bf16[128,640]{1,0:T(8,128)(2,1)S(1)}, u32[]{:S(2)}, u32[]{:S(2)}) %collective-permute-start.8) | collective-permute-done | bytes 163872 | tf_op jit(solution)/shard_map/ppermute | solution.py:297
  203.7 2.1 shard_map.139
  207.7 6.6 %all-to-all-start.3 = ((bf16[16,16,2816]{2,1,0:T(8,128)(2,1)}), bf16[16,16,2816]{2,1,0:T(8,128)(2,1)}, u32[]{:S(2)}, u32[]{:S(2)}) async-start(bf16[16,16,2816]{2,1,0:T(8,128)(2,1)} %copy-done.10), calls=%async_computation.3 | async-start | bytes 2883584 | tf_op jit(solution)/shard_map/all_to_all | solution.py:323
  217.2 2.5 %fusion.1 = bf16[1,2048,256]{2,1,0:T(8,128)(2,1)} fusion(bf16[128,2048]{1,0:T(8,128)(2,1)S(1)} %slice_bitcast_fusion, bf16[128,2048]{1,0:T(8,128)(2,1)} %slice_bitcast_fusion.1, bf16[128,256]{1,0:T(8,128)(2,1)S(1)} %get-tuple-element.47, bf16[128,256]{1,0:T(8,128)(2,1)S(1)} %copy-done.23), kind=kOutput, calls=%fused_computation.5 | convolution fusion | flops 271319040 | bytes 2228224 | tf_op jit(solution)/shard_map/dot_general | solution.py:19
  219.9 1.5 fusion
  221.3 13.4 %all-to-all-done.3 = bf16[16,16,2816]{2,1,0:T(8,128)(2,1)} async-done(((bf16[16,16,2816]{2,1,0:T(8,128)(2,1)}), bf16[16,16,2816]{2,1,0:T(8,128)(2,1)}, u32[]{:S(2)}, u32[]{:S(2)}) %all-to-all-start.3) | async-done | bytes 1441824 | tf_op jit(solution)/shard_map/all_to_all | solution.py:323
  234.7 1.6 convert_reduce_fusion
  236.7 5.9 %collective-permute-start.9 = (bf16[4,4,2048]{2,1,0:T(4,128)(2,1)S(1)}, bf16[4,4,2048]{2,1,0:T(4,128)(2,1)S(1)}, u32[]{:S(2)}, u32[]{:S(2)}) collective-permute-start(bf16[4,4,2048]{2,1,0:T(4,128)(2,1)S(1)} %select_bitcast_fusion.4), channel_id=1, source_target_pairs={{0,496},{16,480},{32,464},{48,448},{64,432},{80,416},{96,400},{112... | collective-permute-start | bytes 196616 | tf_op jit(solution)/shard_map/ppermute | solution.py:415
  244.2 3.4 %collective-permute-done.9 = bf16[4,4,2048]{2,1,0:T(4,128)(2,1)S(1)} collective-permute-done((bf16[4,4,2048]{2,1,0:T(4,128)(2,1)S(1)}, bf16[4,4,2048]{2,1,0:T(4,128)(2,1)S(1)}, u32[]{:S(2)}, u32[]{:S(2)}) %collective-permute-start.9) | collective-permute-done | bytes 65568 | tf_op jit(solution)/shard_map/ppermute | solution.py:415
  (157 shorter events, 28.6 us)
Async XLA Ops:
  3.2 17.3 %collective-permute-start = (bf16[4,4,2048]{2,1,0:T(4,128)(2,1)S(1)}, bf16[4,4,2048]{2,1,0:T(4,128)(2,1)S(1)}, u32[]{:S(2)}, u32[]{:S(2)}) collective-permute-start(bf16[4,4,2048]{2,1,0:T(4,128)(2,1)S(1)} %broadcast_select_fusion.6), channel_id=1, source_target_pairs={{0,496},{16,480},{32,464},{48,448},{64,432},{80,416},{96,400},{112... | collective-permute-start | bytes 196616 | tf_op jit(solution)/shard_map/ppermute | solution.py:240
  22.3 51.9 %all-to-all-start = ((bf16[16,32,2048]{2,1,0:T(8,128)(2,1)}), bf16[16,32,2048]{2,1,0:T(8,128)(2,1)S(1)}, u32[]{:S(2)}, u32[]{:S(2)}) async-start(bf16[16,32,2048]{2,1,0:T(8,128)(2,1)} %broadcast_in_dim.24), calls=%async_computation | async-start | bytes 4194304 | tf_op jit(solution)/shard_map/all_to_all | solution.py:275
  28.9 35.7 %collective-permute-start.2 = (bf16[64,2048]{1,0:T(8,128)(2,1)S(1)}, bf16[64,2048]{1,0:T(8,128)(2,1)S(1)}, u32[]{:S(2)}, u32[]{:S(2)}) collective-permute-start(bf16[64,2048]{1,0:T(8,128)(2,1)S(1)} %bitcast.121), channel_id=1, source_target_pairs={{0,0},{1,1},{8,2},{9,3},{2,4},{3,5},{10,6},{11,7},{4,8},{5,9},{12,... | collective-permute-start | bytes 786440 | tf_op jit(solution)/shard_map/ppermute | solution.py:248
  32.3 36.2 %collective-permute-start.1 = (bf16[64,2048]{1,0:T(8,128)(2,1)S(1)}, bf16[64,2048]{1,0:T(8,128)(2,1)S(1)}, u32[]{:S(2)}, u32[]{:S(2)}) collective-permute-start(bf16[64,2048]{1,0:T(8,128)(2,1)S(1)} %bitcast.122), channel_id=1, source_target_pairs={{8,0},{9,1},{0,2},{1,3},{10,4},{11,5},{2,6},{3,7},{12,8},{13,9},{4... | collective-permute-start | bytes 786440 | tf_op jit(solution)/shard_map/ppermute | solution.py:248
  69.4 4.6 %collective-permute-start.3 = (bf16[2,64,2048]{2,1,0:T(8,128)(2,1)}, bf16[2,64,2048]{2,1,0:T(8,128)(2,1)S(1)}, u32[]{:S(2)}, u32[]{:S(2)}) collective-permute-start(bf16[2,64,2048]{2,1,0:T(8,128)(2,1)} %pad_maximum_fusion.1), channel_id=1, source_target_pairs={{0,1},{1,0},{2,3},{3,2},{4,5},{5,4},{6,7},{7,6},{8,9},{9,8},{10,11... | collective-permute-start | bytes 1572872 | tf_op jit(solution)/shard_map/ppermute | solution.py:266
  82.0 26.1 %collective-permute-start.4 = (bf16[128,1408]{1,0:T(8,128)(2,1)}, bf16[128,1408]{1,0:T(8,128)(2,1)S(1)}, u32[]{:S(2)}, u32[]{:S(2)}) collective-permute-start(bf16[128,1408]{1,0:T(8,128)(2,1)} %get-tuple-element.28), channel_id=1, source_target_pairs={{0,496},{16,480},{32,464},{48,448},{64,432},{80,416},{96,400},{112... | collective-permute-start | bytes 1081352 | tf_op jit(solution)/shard_map/ppermute | solution.py:297
  116.9 26.1 %copy-start.25 = (bf16[4,4,2048]{2,1,0:T(4,128)(2,1)S(1)}, bf16[4,4,2048]{2,1,0:T(4,128)(2,1)}, u32[]{:S(2)}) copy-start(bf16[4,4,2048]{2,1,0:T(4,128)(2,1)} %copy-done.24) | copy-start | bytes 196612
  116.9 26.1 %copy-start.27 = (bf16[4,4,2048]{2,1,0:T(4,128)(2,1)S(1)}, bf16[4,4,2048]{2,1,0:T(4,128)(2,1)}, u32[]{:S(2)}) copy-start(bf16[4,4,2048]{2,1,0:T(4,128)(2,1)} %copy-done.26) | copy-start | bytes 196612
  116.9 24.6 %all-to-all-start.1 = ((bf16[16,16,2560]{2,1,0:T(8,128)(2,1)}), bf16[16,16,2560]{2,1,0:T(8,128)(2,1)}, u32[]{:S(2)}, u32[]{:S(2)}) async-start(bf16[16,16,2560]{2,1,0:T(8,128)(2,1)} %copy-done.11), calls=%async_computation.1 | async-start | bytes 2621440 | tf_op jit(solution)/shard_map/all_to_all | solution.py:323
  143.0 32.0 %copy-start.28 = (bf16[8,2048]{1,0:T(8,128)(2,1)}, bf16[8,2048]{1,0:T(8,128)(2,1)S(1)}, u32[]{:S(2)}) copy-start(bf16[8,2048]{1,0:T(8,128)(2,1)S(1)} %get-tuple-element.58) | copy-start | bytes 98308
  143.3 7.1 %collective-permute-start.6 = (bf16[4,2,2048]{2,1,0:T(2,128)(2,1)S(1)}, bf16[4,2,2048]{2,1,0:T(2,128)(2,1)S(1)}, u32[]{:S(2)}, u32[]{:S(2)}) collective-permute-start(bf16[4,2,2048]{2,1,0:T(2,128)(2,1)S(1)} %get-tuple-element.33), channel_id=1, source_target_pairs={{16,0},{32,16},{48,32},{64,48},{80,64},{96,80},{112,96},{128,112},... | collective-permute-start | bytes 98312 | tf_op jit(solution)/shard_map/ppermute | solution.py:388
  145.3 8.0 %collective-permute-start.5 = (bf16[4,2,2048]{2,1,0:T(2,128)(2,1)S(1)}, bf16[4,2,2048]{2,1,0:T(2,128)(2,1)}, u32[]{:S(2)}, u32[]{:S(2)}) collective-permute-start(bf16[4,2,2048]{2,1,0:T(2,128)(2,1)S(1)} %get-tuple-element.32), channel_id=1, source_target_pairs={{0,16},{16,32},{32,48},{48,64},{64,80},{80,96},{96,112},{112,128},... | collective-permute-start | bytes 98312 | tf_op jit(solution)/shard_map/ppermute | solution.py:387
  150.4 24.6 %copy-start.2 = (bf16[1,2048,256]{2,1,0:T(8,128)(2,1)S(1)}, bf16[1,2048,256]{2,1,0:T(8,128)(2,1)}, u32[]{:S(2)}) copy-start(bf16[1,2048,256]{2,1,0:T(8,128)(2,1)} %param.15) | copy-start | bytes 3145732
  150.4 24.6 %copy-start.5 = (bf16[1,256,2048]{2,1,0:T(8,128)(2,1)S(1)}, bf16[1,256,2048]{2,1,0:T(8,128)(2,1)}, u32[]{:S(2)}) copy-start(bf16[1,256,2048]{2,1,0:T(8,128)(2,1)} %param.17) | copy-start | bytes 3145732
  153.4 22.6 %copy-start.31 = (bf16[2,2048]{1,0:T(2,128)(2,1)}, bf16[2,2048]{1,0:T(2,128)(2,1)S(1)}, u32[]{:S(2)}) copy-start(bf16[2,2048]{1,0:T(2,128)(2,1)S(1)} %get-tuple-element.83) | copy-start | bytes 24580
  153.4 22.6 %copy-start.33 = (bf16[2,2048]{1,0:T(2,128)(2,1)}, bf16[2,2048]{1,0:T(2,128)(2,1)S(1)}, u32[]{:S(2)}) copy-start(bf16[2,2048]{1,0:T(2,128)(2,1)S(1)} %get-tuple-element.84) | copy-start | bytes 24580
  153.4 22.6 %copy-start.35 = (bf16[2,2048]{1,0:T(2,128)(2,1)}, bf16[2,2048]{1,0:T(2,128)(2,1)S(1)}, u32[]{:S(2)}) copy-start(bf16[2,2048]{1,0:T(2,128)(2,1)S(1)} %get-tuple-element.85) | copy-start | bytes 24580
  154.3 21.7 %copy-start.37 = (bf16[2,2048]{1,0:T(2,128)(2,1)}, bf16[2,2048]{1,0:T(2,128)(2,1)S(1)}, u32[]{:S(2)}) copy-start(bf16[2,2048]{1,0:T(2,128)(2,1)S(1)} %get-tuple-element.78) | copy-start | bytes 24580
  175.1 28.6 %copy-start.16 = (f32[128,640]{1,0:T(8,128)S(1)}, f32[128,640]{1,0:T(8,128)}, u32[]{:S(2)}) copy-start(f32[128,640]{1,0:T(8,128)} %copy-done.15) | copy-start | bytes 983044
  176.1 27.6 %collective-permute-start.7 = (bf16[128,896]{1,0:T(8,128)(2,1)S(1)}, bf16[128,896]{1,0:T(8,128)(2,1)S(1)}, u32[]{:S(2)}, u32[]{:S(2)}) collective-permute-start(bf16[128,896]{1,0:T(8,128)(2,1)S(1)} %get-tuple-element.37), channel_id=1, source_target_pairs={{0,496},{16,480},{32,464},{48,448},{64,432},{80,416},{96,400},{112... | collective-permute-start | bytes 688136 | tf_op jit(solution)/shard_map/ppermute | solution.py:297
  182.3 21.4 %collective-permute-start.8 = (bf16[128,640]{1,0:T(8,128)(2,1)S(1)}, bf16[128,640]{1,0:T(8,128)(2,1)S(1)}, u32[]{:S(2)}, u32[]{:S(2)}) collective-permute-start(bf16[128,640]{1,0:T(8,128)(2,1)S(1)} %copy-done.21), channel_id=1, source_target_pairs={{0,496},{16,480},{32,464},{48,448},{64,432},{80,416},{96,400},{112... | collective-permute-start | bytes 491528 | tf_op jit(solution)/shard_map/ppermute | solution.py:297
  207.7 9.4 %copy-start.7 = (bf16[16,16,2048]{2,1,0:T(8,128)(2,1)S(1)}, bf16[16,16,2048]{2,1,0:T(8,128)(2,1)}, u32[]{:S(2)}) copy-start(bf16[16,16,2048]{2,1,0:T(8,128)(2,1)} %copy-done.6) | copy-start | bytes 3145732
  207.7 27.0 %all-to-all-start.3 = ((bf16[16,16,2816]{2,1,0:T(8,128)(2,1)}), bf16[16,16,2816]{2,1,0:T(8,128)(2,1)}, u32[]{:S(2)}, u32[]{:S(2)}) async-start(bf16[16,16,2816]{2,1,0:T(8,128)(2,1)} %copy-done.10), calls=%async_computation.3 | async-start | bytes 2883584 | tf_op jit(solution)/shard_map/all_to_all | solution.py:323
  219.8 16.5 %copy-start.30 = (bf16[2,2048]{1,0:T(2,128)(2,1)S(1)}, bf16[2,2048]{1,0:T(2,128)(2,1)}, u32[]{:S(2)}) copy-start(bf16[2,2048]{1,0:T(2,128)(2,1)} %copy-done.29) | copy-start | bytes 24580
  219.8 16.5 %copy-start.32 = (bf16[2,2048]{1,0:T(2,128)(2,1)S(1)}, bf16[2,2048]{1,0:T(2,128)(2,1)}, u32[]{:S(2)}) copy-start(bf16[2,2048]{1,0:T(2,128)(2,1)} %copy-done.31) | copy-start | bytes 24580
  219.8 16.5 %copy-start.34 = (bf16[2,2048]{1,0:T(2,128)(2,1)S(1)}, bf16[2,2048]{1,0:T(2,128)(2,1)}, u32[]{:S(2)}) copy-start(bf16[2,2048]{1,0:T(2,128)(2,1)} %copy-done.33) | copy-start | bytes 24580
  219.8 16.5 %copy-start.36 = (bf16[2,2048]{1,0:T(2,128)(2,1)S(1)}, bf16[2,2048]{1,0:T(2,128)(2,1)}, u32[]{:S(2)}) copy-start(bf16[2,2048]{1,0:T(2,128)(2,1)} %copy-done.35) | copy-start | bytes 24580
  219.8 16.5 %copy-start.38 = (bf16[2,2048]{1,0:T(2,128)(2,1)S(1)}, bf16[2,2048]{1,0:T(2,128)(2,1)}, u32[]{:S(2)}) copy-start(bf16[2,2048]{1,0:T(2,128)(2,1)} %copy-done.37) | copy-start | bytes 24580
  219.8 16.5 %copy-start.40 = (bf16[2,2048]{1,0:T(2,128)(2,1)S(1)}, bf16[2,2048]{1,0:T(2,128)(2,1)}, u32[]{:S(2)}) copy-start(bf16[2,2048]{1,0:T(2,128)(2,1)} %copy-done.39) | copy-start | bytes 24580
  219.8 16.5 %copy-start.42 = (bf16[2,2048]{1,0:T(2,128)(2,1)S(1)}, bf16[2,2048]{1,0:T(2,128)(2,1)}, u32[]{:S(2)}) copy-start(bf16[2,2048]{1,0:T(2,128)(2,1)} %copy-done.41) | copy-start | bytes 24580
  219.9 16.5 %copy-start.44 = (bf16[2,2048]{1,0:T(2,128)(2,1)S(1)}, bf16[2,2048]{1,0:T(2,128)(2,1)}, u32[]{:S(2)}) copy-start(bf16[2,2048]{1,0:T(2,128)(2,1)} %copy-done.43) | copy-start | bytes 24580
  236.7 10.9 %collective-permute-start.9 = (bf16[4,4,2048]{2,1,0:T(4,128)(2,1)S(1)}, bf16[4,4,2048]{2,1,0:T(4,128)(2,1)S(1)}, u32[]{:S(2)}, u32[]{:S(2)}) collective-permute-start(bf16[4,4,2048]{2,1,0:T(4,128)(2,1)S(1)} %select_bitcast_fusion.4), channel_id=1, source_target_pairs={{0,496},{16,480},{32,464},{48,448},{64,432},{80,416},{96,400},{112... | collective-permute-start | bytes 196616 | tf_op jit(solution)/shard_map/ppermute | solution.py:415
  (29 other events, 56.3 us)

commit v3 on v2

--- a/solution.py
+++ b/solution.py
@@ -38,9 +38,7 @@
 
 
 def array_of(gathered_ref, index, rows):
-    at = (index // 2) * 2 * rows
-    block = gathered_ref[:, at : at + 2 * rows, :].astype(F32)
-    part = block[:, (index % 2) * rows : (index % 2 + 1) * rows]
+    part = gathered_ref[...].astype(F32)[:, index * rows : (index + 1) * rows]
     return part.reshape(part.shape[0] * rows, part.shape[2])
 
 
@@ -100,12 +98,12 @@
 
 
 def attend_body(
-    plan, head, own_x, got_x, own_s, got_s, gathered, gain, query_mat, kv_mat, output_mat, *rest
+    plan, own_x, got_x, own_s, got_s, gathered, gain, query_mat, kv_mat, output_mat, *rest
 ):
     last = plan["last"]
     if last:
         gain_before, rest = rest[0], rest[1:]
-    block, normed_out, query_back_out, mixed_out = rest[:4]
+    block, normed_out, query_back_out, mixed_out, keyval_back_out = rest[:5]
     rows, columns = plan["rows"], query_mat.shape[1]
     shards = block.shape[0]
     tokens, half = shards * rows, query_mat.shape[0]
@@ -149,8 +147,7 @@
     query_back_out[...] = query_back
     key_back = mm(back_scores.T.astype(BF), stacked)
     value_back = mm(probs.T.astype(BF), back)
-    keyval_wide = jnp.concatenate([key_back, value_back], axis=1)
-    keyval_back = keyval_wide.astype(BF)
+    keyval_back = jnp.concatenate([key_back, value_back], axis=1).astype(BF)
 
     back_normed = mm_t(query_back, query_mat[...]) + mm(keyval_back, kv_mat[...])
     along = jnp.sum(query_back.astype(F32) * queries, axis=1, keepdims=True) + jnp.sum(
@@ -167,21 +164,7 @@
     )
     block[:, :, :half] = both.astype(BF)
 
-    turned = jnp.concatenate([key_back.T, value_back.T], axis=0)
-    deep = 2 * rows
-    per_block = turned.shape[0] // 4
-    my_head = head[0]
-    pieces = []
-    for k in range(4):
-        piece = turned[k * per_block : (k + 1) * per_block]
-        pieces.append(
-            jnp.concatenate([piece[i : i + deep] for i in range(0, per_block, deep)], axis=1)
-        )
-    wide_lanes = pieces[0].shape[1]
-    for d in range(shards):
-        k = (d % 2) + 2 * (d // (shards // 2))
-        kept = jnp.where(my_head == (d % (shards // 2)) // 2, pieces[k], 0.0)
-        block[d, :, half : half + wide_lanes] = kept.astype(BF)
+    keyval_back_out[...] = jnp.concatenate([key_back.T, value_back.T], axis=0).astype(BF)
 
     if last:
         gain_part = gain_part + gain_before[...]
@@ -192,14 +175,13 @@
             axis=0,
         ).astype(BF)
         for d in range(shards):
-            block[d, :, half + wide_lanes :] = spread
+            block[d, :, half:] = spread
     else:
-        rest[4][...] = gain_part
+        rest[5][...] = gain_part
 
 
 VMEM = pl.BlockSpec(memory_space=pltpu.VMEM)
-SMEM = pl.BlockSpec(memory_space=pltpu.SMEM)
-PARAMS = pltpu.CompilerParams(vmem_limit_bytes=44 * 2**20)
+PARAMS = pltpu.CompilerParams(vmem_limit_bytes=24 * 2**20)
 
 
 def on_device(
@@ -234,7 +216,7 @@
         return jnp.where(lower, first, second), jnp.where(lower, second, first)
 
     entering = jnp.stack(
-        [carried_acts[0]] + [stashed_acts[0, :, k] for k in range(ticks)] + [carried_grads[0]]
+        [carried_acts[0], carried_grads[0]] + [stashed_acts[0, :, k] for k in range(ticks)]
     ).reshape(ticks + 2, 2 * row_count, width)
     own, other = halves(entering)
     arrived = lax.ppermute(other, "section", mirror)
@@ -244,18 +226,17 @@
 
     kv_own = keyval_weight[0].T
     sources = [[2 * j, 2 * j + 1, shards // 2 + 2 * j, shards // 2 + 2 * j + 1] for j in range(KVH)]
-    fetched = [
-        lax.ppermute(
-            kv_own,
-            "tp",
-            [
-                (sources[j][(i + 2 * k) % kv_group], kv_group * j + i)
-                for j in range(KVH)
-                for i in range(kv_group)
-            ],
-        )
+    kv_routes = [
+        [
+            (sources[j][(i + 2 * k) % kv_group], kv_group * j + i)
+            for j in range(KVH)
+            for i in range(kv_group)
+        ]
         for k in range(2)
     ]
+    swap_cores = [(i, i ^ 1) for i in range(shards)]
+    fetched = [lax.ppermute(kv_own, "tp", route) for route in kv_routes]
+    held, fetched = lax.optimization_barrier((held, fetched))
     second_chip = (me // 2) % 2 == 1
     mine = jnp.stack(
         [
@@ -263,7 +244,7 @@
             jnp.where(second_chip, fetched[0], fetched[1]),
         ]
     )
-    swapped = lax.ppermute(mine, "tp", [(i, i ^ 1) for i in range(shards)])
+    swapped = lax.ppermute(mine, "tp", swap_cores)
     even = me % 2 == 0
     kv_mat = jnp.stack(
         [jnp.where(even, mine, swapped), jnp.where(even, swapped, mine)], axis=1
@@ -296,17 +277,15 @@
     def exchange(message):
         return lax.ppermute(message, "section", mirror)
 
-    my_head = (me // kv_group).astype(jnp.int32).reshape(1)
-    kv_lanes = 2 * HD // 4 // (2 * rows) * tokens
-
     def attend(plan, pieces, gathered, gain_before):
         last = plan["last"]
-        lanes = half + kv_lanes + (half // rows if last else 0)
+        lanes = half + (half // rows if last else 0)
         shapes = [
             jax.ShapeDtypeStruct((shards, 2 * rows, lanes), BF),
             jax.ShapeDtypeStruct((tokens, half), BF),
             jax.ShapeDtypeStruct((tokens, columns), BF),
             jax.ShapeDtypeStruct((tokens, columns), BF),
+            jax.ShapeDtypeStruct((2 * HD, tokens), BF),
         ]
         if not last:
             shapes.append(jax.ShapeDtypeStruct((1, half), F32))
@@ -314,20 +293,29 @@
         return pl.pallas_call(
             functools.partial(attend_body, plan),
             out_shape=shapes,
-            in_specs=[SMEM] + [VMEM] * (9 + len(extra)),
+            in_specs=[VMEM] * (9 + len(extra)),
             out_specs=[VMEM] * len(shapes),
             compiler_params=PARAMS,
-        )(my_head, *pieces, gathered, norm_gain, query_mat, kv_mat, output_mat, *extra)
+        )(*pieces, gathered, norm_gain, query_mat, kv_mat, output_mat, *extra)
 
     def reduce_blocks(block):
         received = lax.all_to_all(block, "tp", split_axis=0, concat_axis=0, tiled=True)
         return jnp.sum(received.astype(F32), axis=0)
 
-    def kv_rows(total):
-        part = total[:, half : half + kv_lanes]
-        return jnp.concatenate(
-            [part[:, i : i + tokens] for i in range(0, kv_lanes, tokens)], axis=0
-        ).astype(BF)
+    def reduce_kv(blocks):
+        parts = blocks.reshape(2, 2, HD // 2, -1)
+        low, high = parts[:, 0], parts[:, 1]
+        got = lax.ppermute(jnp.where(even, high, low), "tp", swap_cores)
+        chip = (jnp.where(even, low, high).astype(F32) + got.astype(F32)).astype(BF)
+        sends = (
+            jnp.where(second_chip, chip[1], chip[0]),
+            jnp.where(second_chip, chip[0], chip[1]),
+        )
+        arrived = [
+            lax.ppermute(send, "tp", [(b, a) for a, b in route])
+            for send, route in zip(sends, kv_routes)
+        ]
+        return (arrived[0].astype(F32) + arrived[1].astype(F32)).astype(BF)
 
     def all_tokens(gathered, index):
         return gathered[:, index * rows : (index + 1) * rows].reshape(tokens, half)
@@ -340,41 +328,41 @@
     first_layer = (section == 0) | (section == sections - 1)
     last_layer = (section == last) | (section == last + 1)
 
-    gathered = gather(held)
-    kept = gathered
-    cot_index = ticks + 1
-    all_cots = [all_tokens(gathered, cot_index)]
-    projected = project(gathered, [((0, 1), cot_index)] + [((k,), None) for k in range(2, 1 + ticks)])
-    (message, own_x), later = projected[0], projected[1:]
+    gathered = gather(held[:3])
+    all_cots = [all_tokens(gathered, 1)]
+    ((message, own_x),) = project(gathered, [((0, 2), 1)])
+    message, later_rows = lax.optimization_barrier((message, held[3:]))
     got_x = exchange(message)
+    later = gather(later_rows)
+    got_x, later = lax.optimization_barrier((got_x, later))
+    later_projected = project(later, [((i,), None) for i in range(ticks - 1)])
     own_s, got_s = own_x, got_x
-    act_rows, cot_rows = held[0], held[cot_index]
+    act_rows, cot_rows = held[0], held[1]
     gain_total = None
     out_rows, back_rows = [], []
     all_normed, all_query_back, all_kv_back, all_mixed = [], [], [], []
     for k in range(ticks):
+        first = k == 0
         plan = {
             "last": k + 1 == ticks,
             "rows": rows,
-            "count_x": 2 if k == 0 else 1,
-            "place_s": 1 if k == 0 else 0,
-            "count_s": 2 if k == 0 else 1,
-            "cot_s": k == 0,
-            "stash": 1 + k,
+            "count_x": 2 if first else 1,
+            "place_s": 1 if first else 0,
+            "count_s": 2 if first else 1,
+            "cot_s": first,
+            "stash": 2 if first else k - 1,
         }
-        block, normed, query_back, mixed, *rest = attend(
-            plan, (own_x, got_x, own_s, got_s), kept, gain_total
+        block, normed, query_back, mixed, kv_back, *rest = attend(
+            plan, (own_x, got_x, own_s, got_s), gathered if first else later, gain_total
         )
         if k + 1 < ticks:
             gain_total = rest[0] if gain_total is None else gain_total + rest[0]
-            block, message_s = lax.optimization_barrier((block, later[k][0]))
-            own_s, got_s = later[k][1], exchange(message_s)
         total = reduce_blocks(block)
         layer_out = (act_rows.astype(F32) + total[:rows, :half]).astype(BF)
         back_input = (cot_rows.astype(F32) + total[rows:, :half]).astype(BF)
         out_rows.append(layer_out)
         back_rows.append(back_input)
-        all_kv_back.append(kv_rows(total))
+        all_kv_back.append(kv_back)
         all_normed.append(normed)
         all_query_back.append(query_back)
         all_mixed.append(mixed)
@@ -395,18 +383,22 @@
             hi = jnp.where(last_layer, going_up, from_above)
             act_rows = jnp.concatenate([lo[0], hi[1], hi[0], lo[1]], axis=0)
             cot_rows = jnp.concatenate([hi[2], lo[3], lo[2], hi[3]], axis=0)
-            gathered = gather(jnp.stack([act_rows, cot_rows]))
-            all_cots.append(all_tokens(gathered, 1))
-            ((message, own_x),) = project(gathered, [((0,), 1)])
+            entering = jnp.stack([act_rows, cot_rows])
+            entering, message_s = lax.optimization_barrier((entering, later_projected[k][0]))
+            own_s, got_s = later_projected[k][1], exchange(message_s)
+            moved = gather(entering)
+            moved, got_s = lax.optimization_barrier((moved, got_s))
+            all_cots.append(all_tokens(moved, 1))
+            ((message, own_x),) = project(moved, [((0,), 1)])
             got_x = exchange(message)
 
     normed = jnp.concatenate(all_normed, axis=0)
     grad_query = t_mm(normed, jnp.concatenate(all_query_back, axis=0)).astype(BF)
-    grad_keyval = mm(jnp.concatenate(all_kv_back, axis=1), normed).astype(BF).T
+    grad_keyval = mm(reduce_kv(jnp.concatenate(all_kv_back, axis=1)), normed).astype(BF).T
     grad_output = t_mm(
         jnp.concatenate(all_cots, axis=0), jnp.concatenate(all_mixed, axis=0)
     ).astype(BF)
-    gain_lanes = total[:, half + kv_lanes :]
+    gain_lanes = total[:, half:]
     grad_gain = (gain_lanes[:rows] + gain_lanes[rows:]).astype(BF).reshape(half)
 
     leaving = jnp.stack(out_rows + back_rows).reshape(2 * ticks, 2, 2 * row_count, half)

time: 251 us -> 239 us (0.952)
  the two profiles are of different devices: /device:TPU:31 before, /device:TPU:8 now
where the time goes in v3:
time: 239 us; the launch traced here: 237 us
  waiting for transfers between devices  97.2 us (41%)
  starting transfers between devices  92.8 us (39%)
  local copies, waits for them, and re-layouts  22 us (9%)
  Pallas kernels  13.4 us (6%)
  other arithmetic  6.25 us (3%)
  matrix products  3.92 us (2%)
    ppermute x3, waiting for transfers between devices, exchange(): return lax.ppermute(message, 'section', mirror)  46 us
    all_to_all x3, waiting for transfers between devices, gather(): return lax.all_to_all(spread, 'tp', split_axis=0, concat_axis=0, tiled=True)  20 us
    all_to_all x3, starting transfers between devices, gather(): return lax.all_to_all(spread, 'tp', split_axis=0, concat_axis=0, tiled=True)  19.3 us
    all_to_all x2, waiting for transfers between devices, reduce_blocks(): lax.all_to_all(block, 'tp', split_axis=0, concat_axis=0, tiled=True)  17.6 us
    ppermute x3, starting transfers between devices, exchange(): return lax.ppermute(message, 'section', mirror)  15.2 us
    ppermute x1, starting transfers between devices, on_device(): arrived = lax.ppermute(other, 'section', mirror)  14.5 us
    unnamed x105, local copies, waits for them, and re-layouts  13.4 us
    all_to_all x2, starting transfers between devices, reduce_blocks(): lax.all_to_all(block, 'tp', split_axis=0, concat_axis=0, tiled=True)  11.7 us
  transfers between devices with their start and end apart: 18, of which 11 were waited for; matrix products, arithmetic and copies ran while one was open for 3% of the time, Pallas kernels for 1%

profile of v3, /device:TPU:8, one launch (start us, length us, event | category | flops | bytes accessed | tf_op | source)
XLA Modules:
  0.0 237.2 jit_solution(12761453060551184521)
XLA Ops:
  3.2 14.5 %collective-permute-start = (bf16[4,4,2048]{2,1,0:T(4,128)(2,1)S(1)}, bf16[4,4,2048]{2,1,0:T(4,128)(2,1)S(1)}, u32[]{:S(2)}, u32[]{:S(2)}) collective-permute-start(bf16[4,4,2048]{2,1,0:T(4,128)(2,1)S(1)} %broadcast_select_fusion.6), channel_id=1, source_target_pairs={{0,496},{16,480},{32,464},{48,448},{64,432},{80,416},{96,400},{112... | collective-permute-start | bytes 196616 | tf_op jit(solution)/shard_map/ppermute | solution.py:222
  17.7 3.4 %collective-permute-start.2 = (bf16[64,2048]{1,0:T(8,128)(2,1)}, bf16[64,2048]{1,0:T(8,128)(2,1)S(1)}, u32[]{:S(2)}, u32[]{:S(2)}) collective-permute-start(bf16[64,2048]{1,0:T(8,128)(2,1)} %bitcast.145), channel_id=1, source_target_pairs={{8,0},{9,1},{0,2},{1,3},{10,4},{11,5},{2,6},{3,7},{12,8},{13,9},{4... | collective-permute-start | bytes 786440 | tf_op jit(solution)/shard_map/ppermute | solution.py:238
  21.2 1.6 collective-permute-start.1
  22.9 5.5 %collective-permute-done.2 = bf16[64,2048]{1,0:T(8,128)(2,1)S(1)} collective-permute-done((bf16[64,2048]{1,0:T(8,128)(2,1)}, bf16[64,2048]{1,0:T(8,128)(2,1)S(1)}, u32[]{:S(2)}, u32[]{:S(2)}) %collective-permute-start.2) | collective-permute-done | bytes 262176 | tf_op jit(solution)/shard_map/ppermute | solution.py:238
  29.8 10.7 %all-to-all-start = ((bf16[16,24,2048]{2,1,0:T(8,128)(2,1)}), bf16[16,24,2048]{2,1,0:T(8,128)(2,1)}, u32[]{:S(2)}, u32[]{:S(2)}) async-start(bf16[16,24,2048]{2,1,0:T(8,128)(2,1)} %broadcast_in_dim.31), calls=%async_computation | async-start | bytes 3145728 | tf_op jit(solution)/shard_map/all_to_all | solution.py:256
  40.7 2.2 collective-permute-start.3
  43.0 1.5 collective-permute-done.3
  44.8 18.4 %all-to-all-done.gathered = bf16[16,24,2048]{2,1,0:T(8,128)(2,1)} async-done(((bf16[16,24,2048]{2,1,0:T(8,128)(2,1)}), bf16[16,24,2048]{2,1,0:T(8,128)(2,1)}, u32[]{:S(2)}, u32[]{:S(2)}) %all-to-all-start) | async-done | bytes 1572896 | tf_op jit(solution)/shard_map/all_to_all | solution.py:256
  63.2 2.9 %shard_map.136 = (bf16[128,1408]{1,0:T(8,128)(2,1)S(1)}, f32[128,1408]{1,0:T(8,128)S(1)}) custom-call(bf16[16,24,2048]{2,1,0:T(8,128)(2,1)} %all-to-all-done.gathered, bf16[1,2048]{1,0:T(2,128)(2,1)S(1)} %copy-done.10, bf16[2048,256]{1,0:T(8,128)(2,1)S(1)} %bitcast.126, bf16[256,2048]{1,0:T(8,128)(2,1)S(1)} %bitcast.121, bf16[256,2048]{1,0:T(8,128)(2,1)S(1)} %bitcast.131), custom_call_target="tpu_custom_call" | custom-call | tf_op jit(solution)/shard_map/pallas_call | solution.py:268
  68.6 4.3 %all-to-all-start.1 = ((bf16[16,8,2048]{2,1,0:T(8,128)(2,1)}), bf16[16,8,2048]{2,1,0:T(8,128)(2,1)}, u32[]{:S(2)}, u32[]{:S(2)}) async-start(bf16[16,8,2048]{2,1,0:T(8,128)(2,1)} %broadcast_in_dim.33), calls=%async_computation.1 | async-start | bytes 1048576 | tf_op jit(solution)/shard_map/all_to_all | solution.py:256
  72.9 3.6 %collective-permute-start.4 = (bf16[128,1408]{1,0:T(8,128)(2,1)}, bf16[128,1408]{1,0:T(8,128)(2,1)S(1)}, u32[]{:S(2)}, u32[]{:S(2)}) collective-permute-start(bf16[128,1408]{1,0:T(8,128)(2,1)} %copy-done.21), channel_id=1, source_target_pairs={{0,496},{16,480},{32,464},{48,448},{64,432},{80,416},{96,400},{112... | collective-permute-start | bytes 1081352 | tf_op jit(solution)/shard_map/ppermute | solution.py:278
  76.4 22.2 %collective-permute-done.4.got_x.got_s = bf16[128,1408]{1,0:T(8,128)(2,1)S(1)} collective-permute-done((bf16[128,1408]{1,0:T(8,128)(2,1)}, bf16[128,1408]{1,0:T(8,128)(2,1)S(1)}, u32[]{:S(2)}, u32[]{:S(2)}) %collective-permute-start.4) | collective-permute-done | bytes 360480 | tf_op jit(solution)/shard_map/ppermute | solution.py:278
  99.8 3.5 %shard_map.137 = (bf16[16,16,2048]{2,1,0:T(8,128)(2,1)S(1)}, bf16[128,2048]{1,0:T(8,128)(2,1)S(1)}, bf16[128,256]{1,0:T(8,128)(2,1)S(1)}, bf16[128,256]{1,0:T(8,...) custom-call(f32[128,1408]{1,0:T(8,128)S(1)} %copy-done.3, ...), custom_call_target="tpu_custom_call" | custom-call | tf_op jit(solution)/shard_map/pallas_call | solution.py:293
  106.9 6.3 %all-to-all-start.2 = ((bf16[16,16,2048]{2,1,0:T(8,128)(2,1)}), bf16[16,16,2048]{2,1,0:T(8,128)(2,1)}, u32[]{:S(2)}, u32[]{:S(2)}) async-start(bf16[16,16,2048]{2,1,0:T(8,128)(2,1)} %copy-done.5), calls=%async_computation.2 | async-start | bytes 2097152 | tf_op jit(solution)/shard_map/all_to_all | solution.py:302
  113.3 16.6 %all-to-all-done.2 = bf16[16,16,2048]{2,1,0:T(8,128)(2,1)} async-done(((bf16[16,16,2048]{2,1,0:T(8,128)(2,1)}), bf16[16,16,2048]{2,1,0:T(8,128)(2,1)}, u32[]{:S(2)}, u32[]{:S(2)}) %all-to-all-start.2) | async-done | bytes 1048608 | tf_op jit(solution)/shard_map/all_to_all | solution.py:302
  132.2 1.9 collective-permute-start.6
  134.1 4.8 %collective-permute-start.5 = (bf16[4,2,2048]{2,1,0:T(2,128)(2,1)}, bf16[4,2,2048]{2,1,0:T(2,128)(2,1)}, u32[]{:S(2)}, u32[]{:S(2)}) collective-permute-start(bf16[4,2,2048]{2,1,0:T(2,128)(2,1)} %get-tuple-element.47), channel_id=1, source_target_pairs={{0,16},{16,32},{32,48},{48,64},{64,80},{80,96},{96,112},{112,128},... | collective-permute-start | bytes 98312 | tf_op jit(solution)/shard_map/ppermute | solution.py:375
  139.1 1.7 shard_map.138
  141.4 1.8 collective-permute-done.5
  146.7 4.3 %all-to-all-start.3 = ((bf16[16,16,2048]{2,1,0:T(8,128)(2,1)}), bf16[16,16,2048]{2,1,0:T(8,128)(2,1)}, u32[]{:S(2)}, u32[]{:S(2)}) async-start(bf16[16,16,2048]{2,1,0:T(8,128)(2,1)} %broadcast_in_dim.35), calls=%async_computation.3 | async-start | bytes 2097152 | tf_op jit(solution)/shard_map/all_to_all | solution.py:256
  151.1 5.8 %collective-permute-start.7 = (bf16[128,640]{1,0:T(8,128)(2,1)}, bf16[128,640]{1,0:T(8,128)(2,1)S(1)}, u32[]{:S(2)}, u32[]{:S(2)}) collective-permute-start(bf16[128,640]{1,0:T(8,128)(2,1)} %copy-done.22), channel_id=1, source_target_pairs={{0,496},{16,480},{32,464},{48,448},{64,432},{80,416},{96,400},{112... | collective-permute-start | bytes 491528 | tf_op jit(solution)/shard_map/ppermute | solution.py:278
  156.9 12.0 %collective-permute-done.7.got_s = bf16[128,640]{1,0:T(8,128)(2,1)S(1)} collective-permute-done((bf16[128,640]{1,0:T(8,128)(2,1)}, bf16[128,640]{1,0:T(8,128)(2,1)S(1)}, u32[]{:S(2)}, u32[]{:S(2)}) %collective-permute-start.7) | collective-permute-done | bytes 163872 | tf_op jit(solution)/shard_map/ppermute | solution.py:278
  169.6 1.6 all-to-all-done.3.gathered
  171.1 2.2 shard_map.139
  173.4 5.8 %collective-permute-start.8 = (bf16[128,896]{1,0:T(8,128)(2,1)S(1)}, bf16[128,896]{1,0:T(8,128)(2,1)S(1)}, u32[]{:S(2)}, u32[]{:S(2)}) collective-permute-start(bf16[128,896]{1,0:T(8,128)(2,1)S(1)} %get-tuple-element.57), channel_id=1, source_target_pairs={{0,496},{16,480},{32,464},{48,448},{64,432},{80,416},{96,400},{112... | collective-permute-start | bytes 688136 | tf_op jit(solution)/shard_map/ppermute | solution.py:278
  179.2 11.7 %collective-permute-done.8.got_x = bf16[128,896]{1,0:T(8,128)(2,1)S(1)} collective-permute-done((bf16[128,896]{1,0:T(8,128)(2,1)S(1)}, bf16[128,896]{1,0:T(8,128)(2,1)S(1)}, u32[]{:S(2)}, u32[]{:S(2)}) %collective-permute-start.8) | collective-permute-done | bytes 229408 | tf_op jit(solution)/shard_map/ppermute | solution.py:278
  190.9 3.1 %shard_map.140 = (bf16[16,16,2304]{2,1,0:T(8,128)(2,1)S(1)}, bf16[128,2048]{1,0:T(8,128)(2,1)S(1)}, bf16[128,256]{1,0:T(8,128)(2,1)S(1)}, bf16[128,256]{1,0:T(8,128)(2,1)S(1)}, bf16[256,128]{1,0:T(8,128)(2,1)S(1)}) custom-call(f32[128,896]{1,0:T(8,128)S(1)} %get-tuple-element.56.own_x, bf16[128,896]{1,0:T(8,128)(2,1)S(1)} %collective-permute-done.8.got_x, ...), custom_call_target="tpu_custom_call" | custom-call | tf_op jit(solution)/shard_map/pallas_call | solution.py:293
  197.1 5.3 %all-to-all-start.4 = ((bf16[16,16,2304]{2,1,0:T(8,128)(2,1)}), bf16[16,16,2304]{2,1,0:T(8,128)(2,1)}, u32[]{:S(2)}, u32[]{:S(2)}) async-start(bf16[16,16,2304]{2,1,0:T(8,128)(2,1)} %copy-done.4), calls=%async_computation.4 | async-start | bytes 2359296 | tf_op jit(solution)/shard_map/all_to_all | solution.py:302
  205.0 2.3 collective-permute-start.10
  209.6 7.8 %collective-permute-start.12 = (bf16[64,256]{1,0:T(8,128)(2,1)S(1)}, bf16[64,256]{1,0:T(8,128)(2,1)S(1)}, u32[]{:S(2)}, u32[]{:S(2)}) collective-permute-start(bf16[64,256]{1,0:T(8,128)(2,1)S(1)} %get-tuple-element.91), channel_id=1, source_target_pairs={{0,8},{1,9},{2,0},{3,1},{4,10},{5,11},{6,2},{7,3},{8,12},{9,13},{1... | collective-permute-start | bytes 98312 | tf_op jit(solution)/shard_map/ppermute | solution.py:315
  222.8 7.3 %collective-permute-start.9 = (bf16[4,4,2048]{2,1,0:T(4,128)(2,1)S(1)}, bf16[4,4,2048]{2,1,0:T(4,128)(2,1)S(1)}, u32[]{:S(2)}, u32[]{:S(2)}) collective-permute-start(bf16[4,4,2048]{2,1,0:T(4,128)(2,1)S(1)} %select_bitcast_fusion.4), channel_id=1, source_target_pairs={{0,496},{16,480},{32,464},{48,448},{64,432},{80,416},{96,400},{112... | collective-permute-start | bytes 196616 | tf_op jit(solution)/shard_map/ppermute | solution.py:407
  230.8 4.7 %collective-permute-done.9 = bf16[4,4,2048]{2,1,0:T(4,128)(2,1)S(1)} collective-permute-done((bf16[4,4,2048]{2,1,0:T(4,128)(2,1)S(1)}, bf16[4,4,2048]{2,1,0:T(4,128)(2,1)S(1)}, u32[]{:S(2)}, u32[]{:S(2)}) %collective-permute-start.9) | collective-permute-done | bytes 65568 | tf_op jit(solution)/shard_map/ppermute | solution.py:407
  (173 shorter events, 33.9 us)
Async XLA Ops:
  3.2 19.5 %collective-permute-start = (bf16[4,4,2048]{2,1,0:T(4,128)(2,1)S(1)}, bf16[4,4,2048]{2,1,0:T(4,128)(2,1)S(1)}, u32[]{:S(2)}, u32[]{:S(2)}) collective-permute-start(bf16[4,4,2048]{2,1,0:T(4,128)(2,1)S(1)} %broadcast_select_fusion.6), channel_id=1, source_target_pairs={{0,496},{16,480},{32,464},{48,448},{64,432},{80,416},{96,400},{112... | collective-permute-start | bytes 196616 | tf_op jit(solution)/shard_map/ppermute | solution.py:222
  17.7 10.7 %collective-permute-start.2 = (bf16[64,2048]{1,0:T(8,128)(2,1)}, bf16[64,2048]{1,0:T(8,128)(2,1)S(1)}, u32[]{:S(2)}, u32[]{:S(2)}) collective-permute-start(bf16[64,2048]{1,0:T(8,128)(2,1)} %bitcast.145), channel_id=1, source_target_pairs={{8,0},{9,1},{0,2},{1,3},{10,4},{11,5},{2,6},{3,7},{12,8},{13,9},{4... | collective-permute-start | bytes 786440 | tf_op jit(solution)/shard_map/ppermute | solution.py:238
  21.2 7.3 %collective-permute-start.1 = (bf16[64,2048]{1,0:T(8,128)(2,1)}, bf16[64,2048]{1,0:T(8,128)(2,1)S(1)}, u32[]{:S(2)}, u32[]{:S(2)}) collective-permute-start(bf16[64,2048]{1,0:T(8,128)(2,1)} %bitcast.146), channel_id=1, source_target_pairs={{0,0},{1,1},{8,2},{9,3},{2,4},{3,5},{10,6},{11,7},{4,8},{5,9},{12,... | collective-permute-start | bytes 786440 | tf_op jit(solution)/shard_map/ppermute | solution.py:238
  22.9 20.1 %copy-start.25 = (bf16[4,8,2048]{2,1,0:T(8,128)(2,1)}, bf16[4,8,2048]{2,1,0:T(8,128)(2,1)S(1)}, u32[]{:S(2)}) copy-start(bf16[4,8,2048]{2,1,0:T(8,128)(2,1)S(1)} %pad_maximum_fusion.2) | copy-start | bytes 393220
  29.8 33.4 %all-to-all-start = ((bf16[16,24,2048]{2,1,0:T(8,128)(2,1)}), bf16[16,24,2048]{2,1,0:T(8,128)(2,1)}, u32[]{:S(2)}, u32[]{:S(2)}) async-start(bf16[16,24,2048]{2,1,0:T(8,128)(2,1)} %broadcast_in_dim.31), calls=%async_computation | async-start | bytes 3145728 | tf_op jit(solution)/shard_map/all_to_all | solution.py:256
  40.7 3.8 %collective-permute-start.3 = (bf16[2,64,2048]{2,1,0:T(8,128)(2,1)S(1)}, bf16[2,64,2048]{2,1,0:T(8,128)(2,1)S(1)}, u32[]{:S(2)}, u32[]{:S(2)}) collective-permute-start(bf16[2,64,2048]{2,1,0:T(8,128)(2,1)S(1)} %pad_maximum_fusion.1), channel_id=1, source_target_pairs={{0,1},{1,0},{2,3},{3,2},{4,5},{5,4},{6,7},{7,6},{8,9},{9,8},{10,11... | collective-permute-start | bytes 1572872 | tf_op jit(solution)/shard_map/ppermute | solution.py:247
  44.6 18.6 %copy-start.10 = (bf16[1,2048]{1,0:T(2,128)(2,1)S(1)}, bf16[1,2048]{1,0:T(2,128)(2,1)}, u32[]{:S(2)}) copy-start(bf16[1,2048]{1,0:T(2,128)(2,1)} %gain.9) | copy-start | bytes 12292
  44.7 18.5 %copy-start = (bf16[1,2048,256]{2,1,0:T(8,128)(2,1)S(1)}, bf16[1,2048,256]{2,1,0:T(8,128)(2,1)}, u32[]{:S(2)}) copy-start(bf16[1,2048,256]{2,1,0:T(8,128)(2,1)} %param.15) | copy-start | bytes 3145732
  44.7 18.5 %copy-start.1 = (bf16[1,256,2048]{2,1,0:T(8,128)(2,1)S(1)}, bf16[1,256,2048]{2,1,0:T(8,128)(2,1)}, u32[]{:S(2)}) copy-start(bf16[1,256,2048]{2,1,0:T(8,128)(2,1)} %param.17) | copy-start | bytes 3145732
  63.2 4.5 %slice-start = ((bf16[4,8,2048]{2,1,0:T(8,128)(2,1)}), bf16[1,8,2048]{2,1,0:T(8,128)(2,1)S(1)}, s32[]{:S(2)}) async-start(bf16[4,8,2048]{2,1,0:T(8,128)(2,1)} %copy-done.25), calls=%async_computation.5 | async-start | bytes 65536 | tf_op jit(solution)/shard_map/slice | solution.py:334
  68.6 30.1 %all-to-all-start.1 = ((bf16[16,8,2048]{2,1,0:T(8,128)(2,1)}), bf16[16,8,2048]{2,1,0:T(8,128)(2,1)}, u32[]{:S(2)}, u32[]{:S(2)}) async-start(bf16[16,8,2048]{2,1,0:T(8,128)(2,1)} %broadcast_in_dim.33), calls=%async_computation.1 | async-start | bytes 1048576 | tf_op jit(solution)/shard_map/all_to_all | solution.py:256
  72.9 25.8 %collective-permute-start.4 = (bf16[128,1408]{1,0:T(8,128)(2,1)}, bf16[128,1408]{1,0:T(8,128)(2,1)S(1)}, u32[]{:S(2)}, u32[]{:S(2)}) collective-permute-start(bf16[128,1408]{1,0:T(8,128)(2,1)} %copy-done.21), channel_id=1, source_target_pairs={{0,496},{16,480},{32,464},{48,448},{64,432},{80,416},{96,400},{112... | collective-permute-start | bytes 1081352 | tf_op jit(solution)/shard_map/ppermute | solution.py:278
  106.9 6.3 %copy-start.47 = (bf16[2,1,2,4096]{3,2,1,0:T(2,128)(2,1)S(1)}, bf16[2,1,2,4096]{3,2,1,0:T(2,128)(2,1)}, u32[]{:S(2)}) copy-start(bf16[2,1,2,4096]{3,2,1,0:T(2,128)(2,1)} %param.13) | copy-start | bytes 98308
  106.9 6.3 %copy-start.48 = (bf16[2,1,2,4096]{3,2,1,0:T(2,128)(2,1)S(1)}, bf16[2,1,2,4096]{3,2,1,0:T(2,128)(2,1)}, u32[]{:S(2)}) copy-start(bf16[2,1,2,4096]{3,2,1,0:T(2,128)(2,1)} %param.10) | copy-start | bytes 98308
  106.9 24.4 %copy-start.26 = (bf16[4,8,2048]{2,1,0:T(8,128)(2,1)S(1)}, bf16[4,8,2048]{2,1,0:T(8,128)(2,1)}, u32[]{:S(2)}) copy-start(bf16[4,8,2048]{2,1,0:T(8,128)(2,1)} %copy-done.25) | copy-start | bytes 393220
  106.9 23.0 %all-to-all-start.2 = ((bf16[16,16,2048]{2,1,0:T(8,128)(2,1)}), bf16[16,16,2048]{2,1,0:T(8,128)(2,1)}, u32[]{:S(2)}, u32[]{:S(2)}) async-start(bf16[16,16,2048]{2,1,0:T(8,128)(2,1)} %copy-done.5), calls=%async_computation.2 | async-start | bytes 2097152 | tf_op jit(solution)/shard_map/all_to_all | solution.py:302
  131.3 7.8 %copy-start.27 = (bf16[8,2048]{1,0:T(8,128)(2,1)}, bf16[8,2048]{1,0:T(8,128)(2,1)S(1)}, u32[]{:S(2)}) copy-start(bf16[8,2048]{1,0:T(8,128)(2,1)S(1)} %get-tuple-element.81) | copy-start | bytes 98308
  131.3 7.8 %copy-start.29 = (bf16[8,2048]{1,0:T(8,128)(2,1)}, bf16[8,2048]{1,0:T(8,128)(2,1)S(1)}, u32[]{:S(2)}) copy-start(bf16[8,2048]{1,0:T(8,128)(2,1)S(1)} %get-tuple-element.80) | copy-start | bytes 98308
  132.2 9.3 %collective-permute-start.6 = (bf16[4,2,2048]{2,1,0:T(2,128)(2,1)}, bf16[4,2,2048]{2,1,0:T(2,128)(2,1)}, u32[]{:S(2)}, u32[]{:S(2)}) collective-permute-start(bf16[4,2,2048]{2,1,0:T(2,128)(2,1)} %get-tuple-element.48), channel_id=1, source_target_pairs={{16,0},{32,16},{48,32},{64,48},{80,64},{96,80},{112,96},{128,112},... | collective-permute-start | bytes 98312 | tf_op jit(solution)/shard_map/ppermute | solution.py:376
  134.1 9.1 %collective-permute-start.5 = (bf16[4,2,2048]{2,1,0:T(2,128)(2,1)}, bf16[4,2,2048]{2,1,0:T(2,128)(2,1)}, u32[]{:S(2)}, u32[]{:S(2)}) collective-permute-start(bf16[4,2,2048]{2,1,0:T(2,128)(2,1)} %get-tuple-element.47), channel_id=1, source_target_pairs={{0,16},{16,32},{32,48},{48,64},{64,80},{80,96},{96,112},{112,128},... | collective-permute-start | bytes 98312 | tf_op jit(solution)/shard_map/ppermute | solution.py:375
  146.7 24.4 %all-to-all-start.3 = ((bf16[16,16,2048]{2,1,0:T(8,128)(2,1)}), bf16[16,16,2048]{2,1,0:T(8,128)(2,1)}, u32[]{:S(2)}, u32[]{:S(2)}) async-start(bf16[16,16,2048]{2,1,0:T(8,128)(2,1)} %broadcast_in_dim.35), calls=%async_computation.3 | async-start | bytes 2097152 | tf_op jit(solution)/shard_map/all_to_all | solution.py:256
  151.1 17.8 %collective-permute-start.7 = (bf16[128,640]{1,0:T(8,128)(2,1)}, bf16[128,640]{1,0:T(8,128)(2,1)S(1)}, u32[]{:S(2)}, u32[]{:S(2)}) collective-permute-start(bf16[128,640]{1,0:T(8,128)(2,1)} %copy-done.22), channel_id=1, source_target_pairs={{0,496},{16,480},{32,464},{48,448},{64,432},{80,416},{96,400},{112... | collective-permute-start | bytes 491528 | tf_op jit(solution)/shard_map/ppermute | solution.py:278
  171.1 19.8 %copy-start.12 = (bf16[128,640]{1,0:T(8,128)(2,1)S(1)}, bf16[128,640]{1,0:T(8,128)(2,1)}, u32[]{:S(2)}) copy-start(bf16[128,640]{1,0:T(8,128)(2,1)} %copy-done.11) | copy-start | bytes 491524
  173.4 17.6 %collective-permute-start.8 = (bf16[128,896]{1,0:T(8,128)(2,1)S(1)}, bf16[128,896]{1,0:T(8,128)(2,1)S(1)}, u32[]{:S(2)}, u32[]{:S(2)}) collective-permute-start(bf16[128,896]{1,0:T(8,128)(2,1)S(1)} %get-tuple-element.57), channel_id=1, source_target_pairs={{0,496},{16,480},{32,464},{48,448},{64,432},{80,416},{96,400},{112... | collective-permute-start | bytes 688136 | tf_op jit(solution)/shard_map/ppermute | solution.py:278
  197.1 6.5 %copy-start.7 = (bf16[128,2048]{1,0:T(8,128)(2,1)S(1)}, bf16[128,2048]{1,0:T(8,128)(2,1)}, u32[]{:S(2)}) copy-start(bf16[128,2048]{1,0:T(8,128)(2,1)} %copy-done.6) | copy-start | bytes 1572868
  197.1 23.8 %all-to-all-start.4 = ((bf16[16,16,2304]{2,1,0:T(8,128)(2,1)}), bf16[16,16,2304]{2,1,0:T(8,128)(2,1)}, u32[]{:S(2)}, u32[]{:S(2)}) async-start(bf16[16,16,2304]{2,1,0:T(8,128)(2,1)} %copy-done.4), calls=%async_computation.4 | async-start | bytes 2359296 | tf_op jit(solution)/shard_map/all_to_all | solution.py:302
  203.7 3.6 %copy-start.9 = (bf16[128,2048]{1,0:T(8,128)(2,1)S(1)}, bf16[128,2048]{1,0:T(8,128)(2,1)}, u32[]{:S(2)}) copy-start(bf16[128,2048]{1,0:T(8,128)(2,1)} %copy-done.8) | copy-start | bytes 1572868
  205.0 3.8 %collective-permute-start.10 = (bf16[2,64,256]{2,1,0:T(8,128)(2,1)S(1)}, bf16[2,64,256]{2,1,0:T(8,128)(2,1)S(1)}, u32[]{:S(2)}, u32[]{:S(2)}) collective-permute-start(bf16[2,64,256]{2,1,0:T(8,128)(2,1)S(1)} %fusion.13), channel_id=1, source_target_pairs={{0,1},{1,0},{2,3},{3,2},{4,5},{5,4},{6,7},{7,6},{8,9},{9,8},{10,11... | collective-permute-start | bytes 196616 | tf_op jit(solution)/shard_map/ppermute | solution.py:308
  207.3 10.0 %copy-start.24 = (bf16[128,256]{1,0:T(8,128)(2,1)S(1)}, bf16[128,256]{1,0:T(8,128)(2,1)}, u32[]{:S(2)}) copy-start(bf16[128,256]{1,0:T(8,128)(2,1)} %copy-done.23) | copy-start | bytes 196612
  208.9 10.0 %collective-permute-start.11 = (bf16[64,256]{1,0:T(8,128)(2,1)S(1)}, bf16[64,256]{1,0:T(8,128)(2,1)S(1)}, u32[]{:S(2)}, u32[]{:S(2)}) collective-permute-start(bf16[64,256]{1,0:T(8,128)(2,1)S(1)} %get-tuple-element.90), channel_id=1, source_target_pairs={{0,0},{1,1},{2,8},{3,9},{4,2},{5,3},{6,10},{7,11},{8,4},{9,5},{10,... | collective-permute-start | bytes 98312 | tf_op jit(solution)/shard_map/ppermute | solution.py:315
  209.6 9.4 %collective-permute-start.12 = (bf16[64,256]{1,0:T(8,128)(2,1)S(1)}, bf16[64,256]{1,0:T(8,128)(2,1)S(1)}, u32[]{:S(2)}, u32[]{:S(2)}) collective-permute-start(bf16[64,256]{1,0:T(8,128)(2,1)S(1)} %get-tuple-element.91), channel_id=1, source_target_pairs={{0,8},{1,9},{2,0},{3,1},{4,10},{5,11},{6,2},{7,3},{8,12},{9,13},{1... | collective-permute-start | bytes 98312 | tf_op jit(solution)/shard_map/ppermute | solution.py:315
  222.8 12.7 %collective-permute-start.9 = (bf16[4,4,2048]{2,1,0:T(4,128)(2,1)S(1)}, bf16[4,4,2048]{2,1,0:T(4,128)(2,1)S(1)}, u32[]{:S(2)}, u32[]{:S(2)}) collective-permute-start(bf16[4,4,2048]{2,1,0:T(4,128)(2,1)S(1)} %select_bitcast_fusion.4), channel_id=1, source_target_pairs={{0,496},{16,480},{32,464},{48,448},{64,432},{80,416},{96,400},{112... | collective-permute-start | bytes 196616 | tf_op jit(solution)/shard_map/ppermute | solution.py:407
  (36 other events, 61.7 us)

commit v4 on v3

--- a/solution.py
+++ b/solution.py
@@ -48,7 +48,22 @@
     return jnp.sum(jnp.where(chosen, block, 0.0), axis=1, keepdims=True)
 
 
-def project_body(groups, rows, gathered, gain, query_mat, kv_mat, output_mat, *outs):
+def project_body(groups, kept_arrays, far, rows, gathered, gain, query_mat, kv_mat, output_mat, *rest):
+    results, buffers, sems = rest[: len(far)], rest[len(far) : -1], rest[-1]
+    places = [i for i, is_far in enumerate(far) if is_far]
+    outs = [buffers[places.index(i)] if is_far else results[i] for i, is_far in enumerate(far)]
+    copies = []
+
+    def send(index):
+        if far[index]:
+            place = places.index(index)
+            copies.append(pltpu.make_async_copy(buffers[place], results[index], sems.at[place]))
+            copies[-1].start()
+
+    for i, kept_array in enumerate(kept_arrays):
+        index = 2 * len(groups) + i
+        outs[index][...] = array_of(gathered, kept_array, rows).astype(BF)
+        send(index)
     gain_row = gain[...].astype(F32)
     for index, (acts, cot) in enumerate(groups):
         message, own = outs[2 * index], outs[2 * index + 1]
@@ -78,6 +93,10 @@
             sent = jnp.where(lane == len(squares) + i, square - high, sent)
         own[:, at : at + HD] = kept
         message[:, at : at + HD] = sent.astype(BF)
+        send(2 * index)
+        send(2 * index + 1)
+    for copy in copies:
+        copy.wait()
 
 
 def stack_heads(columns):
@@ -98,12 +117,27 @@
 
 
 def attend_body(
-    plan, own_x, got_x, own_s, got_s, gathered, gain, query_mat, kv_mat, output_mat, *rest
+    plan, pieces, own_x, got_x, *rest
 ):
     last = plan["last"]
+    own_s, got_s = (own_x, got_x) if pieces == 2 else rest[: pieces - 2]
+    stash, gain, query_mat, kv_mat, output_mat, *rest = rest[pieces - 2 :]
     if last:
         gain_before, rest = rest[0], rest[1:]
-    block, normed_out, query_back_out, mixed_out, keyval_back_out = rest[:5]
+    outs, block, sems = rest[: plan["outs"]], rest[plan["outs"]], rest[-1]
+    leaving = []
+
+    def leave(index, value):
+        buffer = rest[plan["outs"] + index]
+        buffer[...] = value
+        send(index)
+
+    def send(index):
+        copy = pltpu.make_async_copy(
+            rest[plan["outs"] + index], outs[index], sems.at[index]
+        )
+        copy.start()
+        leaving.append(copy)
     rows, columns = plan["rows"], query_mat.shape[1]
     shards = block.shape[0]
     tokens, half = shards * rows, query_mat.shape[0]
@@ -138,24 +172,25 @@
     keys, values = keyvals[:, :HD].astype(BF), keyvals[:, HD:].astype(BF)
     stacked = stack_heads(queries).astype(BF)
     probs = softmax_of(stacked, keys, mask)
-    mixed_out[...] = unstack_heads(mm(probs.astype(BF), values), tokens).astype(BF)
+    leave(3, unstack_heads(mm(probs.astype(BF), values), tokens).astype(BF))
     back = stack_heads(back_mixed).astype(BF)
     back_probs = mm_t(back, values)
     inner = jnp.sum(probs * back_probs, axis=1, keepdims=True)
     back_scores = probs * (back_probs - inner) / math.sqrt(HD)
     query_back = unstack_heads(mm(back_scores.astype(BF), keys), tokens).astype(BF)
-    query_back_out[...] = query_back
+    leave(2, query_back)
     key_back = mm(back_scores.T.astype(BF), stacked)
     value_back = mm(probs.T.astype(BF), back)
     keyval_back = jnp.concatenate([key_back, value_back], axis=1).astype(BF)
+    leave(4, jnp.concatenate([key_back.T, value_back.T], axis=0).astype(BF))
 
     back_normed = mm_t(query_back, query_mat[...]) + mm(keyval_back, kv_mat[...])
     along = jnp.sum(query_back.astype(F32) * queries, axis=1, keepdims=True) + jnp.sum(
         keyval_back.astype(F32) * keyvals, axis=1, keepdims=True
     )
     gain_row = gain[...].astype(F32)
-    unit = array_of(gathered, plan["stash"], rows) * inverse
-    normed_out[...] = (unit * gain_row).astype(BF)
+    unit = stash[...].astype(F32) * inverse
+    leave(1, (unit * gain_row).astype(BF))
     back_part = inverse * (back_normed * gain_row - unit * (along / (2 * half)))
     gain_part = jnp.sum(back_normed * unit, axis=0, keepdims=True)
 
@@ -163,8 +198,6 @@
         [out_part.reshape(shards, rows, half), back_part.reshape(shards, rows, half)], axis=1
     )
     block[:, :, :half] = both.astype(BF)
-
-    keyval_back_out[...] = jnp.concatenate([key_back.T, value_back.T], axis=0).astype(BF)
 
     if last:
         gain_part = gain_part + gain_before[...]
@@ -177,10 +210,14 @@
         for d in range(shards):
             block[d, :, half:] = spread
     else:
-        rest[5][...] = gain_part
+        leave(5, gain_part)
+    send(0)
+    for copy in leaving:
+        copy.wait()
 
 
 VMEM = pl.BlockSpec(memory_space=pltpu.VMEM)
+HBM = pl.BlockSpec(memory_space=pltpu.HBM)
 PARAMS = pltpu.CompilerParams(vmem_limit_bytes=24 * 2**20)
 
 
@@ -255,29 +292,48 @@
         spread = jnp.broadcast_to(local.reshape(1, count * rows, half), (shards, count * rows, half))
         return lax.all_to_all(spread, "tp", split_axis=0, concat_axis=0, tiled=True)
 
+    def gather_two_level(local):
+        count, chips = local.shape[0], shards // 2
+        spread = jnp.broadcast_to(local.reshape(1, count * rows, half), (chips, count * rows, half))
+        groups = [[2 * chip + core for chip in range(chips)] for core in range(2)]
+        mine = lax.all_to_all(
+            spread, "tp", split_axis=0, concat_axis=0, axis_index_groups=groups, tiled=True
+        )
+        other = lax.ppermute(mine, "tp", swap_cores)
+        both = jnp.stack(
+            [jnp.where(even, mine, other), jnp.where(even, other, mine)], axis=1
+        )
+        return both.reshape(shards, count * rows, half)
+
     eval_columns = columns + 2 * HD
 
-    def project(gathered, groups):
-        shapes = []
-        for acts, cot in groups:
+    def project(gathered, groups, kept_arrays):
+        shapes, far = [], []
+        for i, (acts, cot) in enumerate(groups):
             size = len(acts) * eval_columns + (0 if cot is None else columns) + HD
-            shapes += [
-                jax.ShapeDtypeStruct((tokens, size), BF),
-                jax.ShapeDtypeStruct((tokens, size), F32),
-            ]
+            shapes += [((tokens, size), BF), ((tokens, size), F32)]
+            far += [i > 0] * 2
+        shapes += [((tokens, half), BF)] * len(kept_arrays)
+        far += [True] * len(kept_arrays)
         outs = pl.pallas_call(
-            functools.partial(project_body, groups, rows),
-            out_shape=shapes,
+            functools.partial(project_body, groups, kept_arrays, far, rows),
+            out_shape=[
+                pltpu.HBM(*shape) if is_far else jax.ShapeDtypeStruct(*shape)
+                for shape, is_far in zip(shapes, far)
+            ],
             in_specs=[VMEM] * 5,
-            out_specs=[VMEM] * len(shapes),
+            out_specs=[HBM if is_far else VMEM for is_far in far],
+            scratch_shapes=[pltpu.VMEM(*shape) for shape, is_far in zip(shapes, far) if is_far]
+            + [pltpu.SemaphoreType.DMA((sum(far),))],
             compiler_params=PARAMS,
         )(gathered, norm_gain, query_mat, kv_mat, output_mat)
-        return [(outs[2 * i], outs[2 * i + 1]) for i in range(len(groups))]
+        pairs = [(outs[2 * i], outs[2 * i + 1]) for i in range(len(groups))]
+        return pairs, outs[2 * len(groups) :]
 
     def exchange(message):
         return lax.ppermute(message, "section", mirror)
 
-    def attend(plan, pieces, gathered, gain_before):
+    def attend(plan, pieces, stash, gain_before):
         last = plan["last"]
         lanes = half + (half // rows if last else 0)
         shapes = [
@@ -291,12 +347,14 @@
             shapes.append(jax.ShapeDtypeStruct((1, half), F32))
         extra = [gain_before] if last else []
         return pl.pallas_call(
-            functools.partial(attend_body, plan),
-            out_shape=shapes,
-            in_specs=[VMEM] * (9 + len(extra)),
-            out_specs=[VMEM] * len(shapes),
+            functools.partial(attend_body, {**plan, "outs": len(shapes)}, len(pieces)),
+            out_shape=[pltpu.HBM(shape.shape, shape.dtype) for shape in shapes],
+            in_specs=[VMEM] * (5 + len(pieces) + len(extra)),
+            out_specs=[HBM] * len(shapes),
+            scratch_shapes=[pltpu.VMEM(shape.shape, shape.dtype) for shape in shapes]
+            + [pltpu.SemaphoreType.DMA((len(shapes),))],
             compiler_params=PARAMS,
-        )(*pieces, gathered, norm_gain, query_mat, kv_mat, output_mat, *extra)
+        )(*pieces, stash, norm_gain, query_mat, kv_mat, output_mat, *extra)
 
     def reduce_blocks(block):
         received = lax.all_to_all(block, "tp", split_axis=0, concat_axis=0, tiled=True)
@@ -317,9 +375,6 @@
         ]
         return (arrived[0].astype(F32) + arrived[1].astype(F32)).astype(BF)
 
-    def all_tokens(gathered, index):
-        return gathered[:, index * rows : (index + 1) * rows].reshape(tokens, half)
-
     last = sections // 2 - 1
     ahead = [(i, i + 1) for i in range(last)] + [
         (sections - 1 - i, sections - 2 - i) for i in range(last)
@@ -328,15 +383,13 @@
     first_layer = (section == 0) | (section == sections - 1)
     last_layer = (section == last) | (section == last + 1)
 
-    gathered = gather(held[:3])
-    all_cots = [all_tokens(gathered, 1)]
-    ((message, own_x),) = project(gathered, [((0, 2), 1)])
-    message, later_rows = lax.optimization_barrier((message, held[3:]))
+    gathered = gather_two_level(held)
+    kept_arrays = tuple(range(1, 2 + ticks))
+    groups = [((0, 2), 1)] + [((2 + k,), None) for k in range(1, ticks)]
+    projected, (cots, *stash) = project(gathered, groups, kept_arrays)
+    (message, own_x), later = projected[0], projected[1:]
     got_x = exchange(message)
-    later = gather(later_rows)
-    got_x, later = lax.optimization_barrier((got_x, later))
-    later_projected = project(later, [((i,), None) for i in range(ticks - 1)])
-    own_s, got_s = own_x, got_x
+    all_cots = [cots]
     act_rows, cot_rows = held[0], held[1]
     gain_total = None
     out_rows, back_rows = [], []
@@ -350,10 +403,12 @@
             "place_s": 1 if first else 0,
             "count_s": 2 if first else 1,
             "cot_s": first,
-            "stash": 2 if first else k - 1,
         }
         block, normed, query_back, mixed, kv_back, *rest = attend(
-            plan, (own_x, got_x, own_s, got_s), gathered if first else later, gain_total
+            plan,
+            (own_x, got_x) if first else (own_x, got_x, own_s, got_s),
+            stash[k],
+            gain_total,
         )
         if k + 1 < ticks:
             gain_total = rest[0] if gain_total is None else gain_total + rest[0]
@@ -384,12 +439,13 @@
             act_rows = jnp.concatenate([lo[0], hi[1], hi[0], lo[1]], axis=0)
             cot_rows = jnp.concatenate([hi[2], lo[3], lo[2], hi[3]], axis=0)
             entering = jnp.stack([act_rows, cot_rows])
-            entering, message_s = lax.optimization_barrier((entering, later_projected[k][0]))
-            own_s, got_s = later_projected[k][1], exchange(message_s)
+            entering, message_s = lax.optimization_barrier((entering, later[k][0]))
+            own_s, got_s = later[k][1], exchange(message_s)
+            act_rows, cot_rows = entering[0], entering[1]
             moved = gather(entering)
             moved, got_s = lax.optimization_barrier((moved, got_s))
-            all_cots.append(all_tokens(moved, 1))
-            ((message, own_x),) = project(moved, [((0,), 1)])
+            ((message, own_x),), (cots,) = project(moved, [((0,), 1)], (1,))
+            all_cots.append(cots)
             got_x = exchange(message)
 
     normed = jnp.concatenate(all_normed, axis=0)

time: 239 us -> 217 us (0.908)
  the two profiles are of different devices: /device:TPU:8 before, /device:TPU:26 now
where the time goes in v4:
time: 217 us; the launch traced here: 216 us
  waiting for transfers between devices  93.6 us (43%)
  starting transfers between devices  88.3 us (41%)
  Pallas kernels  12.4 us (6%)
  local copies, waits for them, and re-layouts  10.4 us (5%)
  other arithmetic  5.09 us (2%)
  matrix products  4.76 us (2%)
    ppermute x3, waiting for transfers between devices, exchange(): return lax.ppermute(message, 'section', mirror)  47.2 us
    ppermute x3, starting transfers between devices, exchange(): return lax.ppermute(message, 'section', mirror)  18.9 us
    all_to_all x2, waiting for transfers between devices, reduce_blocks(): lax.all_to_all(block, 'tp', split_axis=0, concat_axis=0, tiled=True)  13.5 us
    ppermute x1, starting transfers between devices, on_device(): arrived = lax.ppermute(other, 'section', mirror)  13.2 us
    all_to_all x1, waiting for transfers between devices, gather_two_level(): lax.all_to_all(spread, 'tp', split_axis=0, concat_axis=0, axis_index_grou...  11 us
    all_to_all x2, starting transfers between devices, reduce_blocks(): lax.all_to_all(block, 'tp', split_axis=0, concat_axis=0, tiled=True)  10.8 us
    ppermute x2, waiting for transfers between devices, on_device(): fetched = [lax.ppermute(kv_own, 'tp', route) for route in kv_routes]  8.79 us
    ppermute x1, starting transfers between devices, on_device(): returned = lax.ppermute(theirs, 'section', mirror)  7.38 us
  transfers between devices with their start and end apart: 18, of which 12 were waited for; matrix products, arithmetic and copies ran while one was open for 4% of the time, Pallas kernels for 0%

profile of v4, /device:TPU:26, one launch (start us, length us, event | category | flops | bytes accessed | tf_op | source)
XLA Modules:
  0.0 216.0 jit_solution(18172093853973717241)
XLA Ops:
  3.2 13.2 %collective-permute-start = (bf16[4,4,2048]{2,1,0:T(4,128)(2,1)S(1)}, bf16[4,4,2048]{2,1,0:T(4,128)(2,1)S(1)}, u32[]{:S(2)}, u32[]{:S(2)}) collective-permute-start(bf16[4,4,2048]{2,1,0:T(4,128)(2,1)S(1)} %broadcast_select_fusion.6), channel_id=1, source_target_pairs={{0,496},{16,480},{32,464},{48,448},{64,432},{80,416},{96,400},{112... | collective-permute-start | bytes 196616 | tf_op jit(solution)/shard_map/ppermute | solution.py:259
  16.4 4.0 %collective-permute-start.2 = (bf16[64,2048]{1,0:T(8,128)(2,1)}, bf16[64,2048]{1,0:T(8,128)(2,1)S(1)}, u32[]{:S(2)}, u32[]{:S(2)}) collective-permute-start(bf16[64,2048]{1,0:T(8,128)(2,1)} %bitcast.152), channel_id=1, source_target_pairs={{8,0},{9,1},{0,2},{1,3},{10,4},{11,5},{2,6},{3,7},{12,8},{13,9},{4... | collective-permute-start | bytes 786440 | tf_op jit(solution)/shard_map/ppermute | solution.py:275
  20.4 2.7 %collective-permute-start.1 = (bf16[64,2048]{1,0:T(8,128)(2,1)}, bf16[64,2048]{1,0:T(8,128)(2,1)S(1)}, u32[]{:S(2)}, u32[]{:S(2)}) collective-permute-start(bf16[64,2048]{1,0:T(8,128)(2,1)} %bitcast.153), channel_id=1, source_target_pairs={{0,0},{1,1},{8,2},{9,3},{2,4},{3,5},{10,6},{11,7},{4,8},{5,9},{12,... | collective-permute-start | bytes 786440 | tf_op jit(solution)/shard_map/ppermute | solution.py:275
  23.3 3.8 %collective-permute-done.2 = bf16[64,2048]{1,0:T(8,128)(2,1)S(1)} collective-permute-done((bf16[64,2048]{1,0:T(8,128)(2,1)}, bf16[64,2048]{1,0:T(8,128)(2,1)S(1)}, u32[]{:S(2)}, u32[]{:S(2)}) %collective-permute-start.2) | collective-permute-done | bytes 262176 | tf_op jit(solution)/shard_map/ppermute | solution.py:275
  27.2 5.0 %collective-permute-done.1 = bf16[64,2048]{1,0:T(8,128)(2,1)S(1)} collective-permute-done((bf16[64,2048]{1,0:T(8,128)(2,1)}, bf16[64,2048]{1,0:T(8,128)(2,1)S(1)}, u32[]{:S(2)}, u32[]{:S(2)}) %collective-permute-start.1) | collective-permute-done | bytes 262176 | tf_op jit(solution)/shard_map/ppermute | solution.py:275
  33.2 6.3 %all-to-all-start = ((bf16[8,32,2048]{2,1,0:T(8,128)(2,1)}), bf16[8,32,2048]{2,1,0:T(8,128)(2,1)S(1)}, u32[]{:S(2)}, u32[]{:S(2)}) async-start(bf16[8,32,2048]{2,1,0:T(8,128)(2,1)} %broadcast_in_dim.24), calls=%async_computation | async-start | bytes 2097152 | tf_op jit(solution)/shard_map/all_to_all | solution.py:299
  39.6 1.9 collective-permute-start.4
  41.5 11.0 %all-to-all-done = bf16[8,32,2048]{2,1,0:T(8,128)(2,1)S(1)} async-done(((bf16[8,32,2048]{2,1,0:T(8,128)(2,1)}), bf16[8,32,2048]{2,1,0:T(8,128)(2,1)S(1)}, u32[]{:S(2)}, u32[]{:S(2)}) %all-to-all-start) | async-done | bytes 1048608 | tf_op jit(solution)/shard_map/all_to_all | solution.py:299
  58.8 3.2 %shard_map.136 = (bf16[128,1408]{1,0:T(8,128)(2,1)S(1)}, f32[128,1408]{1,0:T(8,128)S(1)}, bf16[128,640]{1,0:T(8,128)(2,1)}, f32[128,640]{1,0:T(8,128)}, bf16[128...) custom-call(bf16[16,32,2048]{2,1,0:T(8,128)(2,1)S(1)} %bitcast.140, ...), custom_call_target="tpu_custom_call" | custom-call | tf_op jit(solution)/shard_map/pallas_call | solution.py:318
  61.9 3.2 %collective-permute-start.5 = (bf16[128,1408]{1,0:T(8,128)(2,1)S(1)}, bf16[128,1408]{1,0:T(8,128)(2,1)S(1)}, u32[]{:S(2)}, u32[]{:S(2)}) collective-permute-start(bf16[128,1408]{1,0:T(8,128)(2,1)S(1)} %get-tuple-element.42), channel_id=1, source_target_pairs={{0,496},{16,480},{32,464},{48,448},{64,432},{80,416},{96,400},{112... | collective-permute-start | bytes 1081352 | tf_op jit(solution)/shard_map/ppermute | solution.py:334
  65.1 22.9 %collective-permute-done.5.got_x = bf16[128,1408]{1,0:T(8,128)(2,1)S(1)} collective-permute-done((bf16[128,1408]{1,0:T(8,128)(2,1)S(1)}, bf16[128,1408]{1,0:T(8,128)(2,1)S(1)}, u32[]{:S(2)}, u32[]{:S(2)}) %collective-permute-start.5) | collective-permute-done | bytes 360480 | tf_op jit(solution)/shard_map/ppermute | solution.py:334
  89.0 3.1 %shard_map.137 = (bf16[16,16,2048]{2,1,0:T(8,128)(2,1)}, bf16[128,2048]{1,0:T(8,128)(2,1)}, bf16[128,256]{1,0:T(8,128)(2,1)}, bf16[128,256]{1,0:T(8,128)(2,1)}, ...) custom-call(f32[128,1408]{1,0:T(8,128)S(1)} %get-tuple-element.41.own_x, bf16[128,1408]{1,0:T(8,128)(2,1)S(1)} %collective-permute-done.5.got_x, ...), custom_call_target="tpu_custom_call" | custom-call | tf_op jit(solution)/shard_map/pallas_call | solution.py:349
  92.1 5.3 %all-to-all-start.1 = ((bf16[16,16,2048]{2,1,0:T(8,128)(2,1)}), bf16[16,16,2048]{2,1,0:T(8,128)(2,1)}, u32[]{:S(2)}, u32[]{:S(2)}) async-start(bf16[16,16,2048]{2,1,0:T(8,128)(2,1)} %get-tuple-element.44), calls=%async_computation.1 | async-start | bytes 2097152 | tf_op jit(solution)/shard_map/all_to_all | solution.py:360
  97.5 13.5 %all-to-all-done.1 = bf16[16,16,2048]{2,1,0:T(8,128)(2,1)} async-done(((bf16[16,16,2048]{2,1,0:T(8,128)(2,1)}), bf16[16,16,2048]{2,1,0:T(8,128)(2,1)}, u32[]{:S(2)}, u32[]{:S(2)}) %all-to-all-start.1) | async-done | bytes 1048608 | tf_op jit(solution)/shard_map/all_to_all | solution.py:360
  112.6 1.9 collective-permute-start.7
  114.6 4.8 %collective-permute-start.6 = (bf16[4,2,2048]{2,1,0:T(2,128)(2,1)S(1)}, bf16[4,2,2048]{2,1,0:T(2,128)(2,1)S(1)}, u32[]{:S(2)}, u32[]{:S(2)}) collective-permute-start(bf16[4,2,2048]{2,1,0:T(2,128)(2,1)S(1)} %get-tuple-element.45), channel_id=1, source_target_pairs={{0,16},{16,32},{32,48},{48,64},{64,80},{80,96},{96,112},{112,128},... | collective-permute-start | bytes 98312 | tf_op jit(solution)/shard_map/ppermute | solution.py:430
  119.5 4.2 %collective-permute-done.6 = bf16[4,2,2048]{2,1,0:T(2,128)(2,1)S(1)} collective-permute-done((bf16[4,2,2048]{2,1,0:T(2,128)(2,1)S(1)}, bf16[4,2,2048]{2,1,0:T(2,128)(2,1)S(1)}, u32[]{:S(2)}, u32[]{:S(2)}) %collective-permute-start.6) | collective-permute-done | bytes 32800 | tf_op jit(solution)/shard_map/ppermute | solution.py:430
  125.1 7.1 %all-to-all-start.2 = ((bf16[16,16,2048]{2,1,0:T(8,128)(2,1)}), bf16[16,16,2048]{2,1,0:T(8,128)(2,1)}, u32[]{:S(2)}, u32[]{:S(2)}) async-start(bf16[16,16,2048]{2,1,0:T(8,128)(2,1)} %broadcast_in_dim.26), calls=%async_computation.2 | async-start | bytes 2097152 | tf_op jit(solution)/shard_map/all_to_all | solution.py:293
  132.2 8.4 %collective-permute-start.8 = (bf16[128,640]{1,0:T(8,128)(2,1)}, bf16[128,640]{1,0:T(8,128)(2,1)S(1)}, u32[]{:S(2)}, u32[]{:S(2)}) collective-permute-start(bf16[128,640]{1,0:T(8,128)(2,1)} %get-tuple-element.51), channel_id=1, source_target_pairs={{0,496},{16,480},{32,464},{48,448},{64,432},{80,416},{96,400},{112... | collective-permute-start | bytes 491528 | tf_op jit(solution)/shard_map/ppermute | solution.py:334
  140.6 10.4 %collective-permute-done.8.rest_1_ = bf16[128,640]{1,0:T(8,128)(2,1)S(1)} collective-permute-done((bf16[128,640]{1,0:T(8,128)(2,1)}, bf16[128,640]{1,0:T(8,128)(2,1)S(1)}, u32[]{:S(2)}, u32[]{:S(2)}) %collective-permute-start.8) | collective-permute-done | bytes 163872 | tf_op jit(solution)/shard_map/ppermute | solution.py:334
  151.7 3.0 %shard_map.138 = (bf16[128,896]{1,0:T(8,128)(2,1)S(1)}, f32[128,896]{1,0:T(8,128)S(1)}, bf16[128,2048]{1,0:T(8,128)(2,1)}) custom-call(bf16[16,16,2048]{2,1,0:T(8,128)(2,1)} %all-to-all-done.2.gathered, bf16[1,2048]{1,0:T(2,128)(2,1)S(1)} %copy-done.7, bf16[2048,256]{1,0:T(8,128)(2,1)S(1)} %bitcast.134, bf16[256,2048]{1,0:T(8,128)(2,1)S(1)} %bitcast.130, ...), custom_call_target="tpu_custom_call" | custom-call | tf_op jit(solution)/shard_map/pallas_call | solution.py:318
  154.7 7.3 %collective-permute-start.9 = (bf16[128,896]{1,0:T(8,128)(2,1)S(1)}, bf16[128,896]{1,0:T(8,128)(2,1)S(1)}, u32[]{:S(2)}, u32[]{:S(2)}) collective-permute-start(bf16[128,896]{1,0:T(8,128)(2,1)S(1)} %get-tuple-element.54), channel_id=1, source_target_pairs={{0,496},{16,480},{32,464},{48,448},{64,432},{80,416},{96,400},{112... | collective-permute-start | bytes 688136 | tf_op jit(solution)/shard_map/ppermute | solution.py:334
  162.0 14.0 %collective-permute-done.9.got_x = bf16[128,896]{1,0:T(8,128)(2,1)S(1)} collective-permute-done((bf16[128,896]{1,0:T(8,128)(2,1)S(1)}, bf16[128,896]{1,0:T(8,128)(2,1)S(1)}, u32[]{:S(2)}, u32[]{:S(2)}) %collective-permute-start.9) | collective-permute-done | bytes 229408 | tf_op jit(solution)/shard_map/ppermute | solution.py:334
  176.0 3.2 %shard_map.139 = (bf16[16,16,2304]{2,1,0:T(8,128)(2,1)}, bf16[128,2048]{1,0:T(8,128)(2,1)}, bf16[128,256]{1,0:T(8,128)(2,1)}, bf16[128,256]{1,0:T(8,128)(2,1)}, bf16[256,128]{1,0:T(8,128)(2,1)}) custom-call(f32[128,896]{1,0:T(8,128)S(1)} %get-tuple-element.53.own_x, bf16[128,896]{1,0:T(8,128)(2,1)S(1)} %collective-permute-done.9.got_x, ...), custom_call_target="tpu_custom_call" | custom-call | tf_op jit(solution)/shard_map/pallas_call | solution.py:349
  179.2 5.5 %all-to-all-start.3 = ((bf16[16,16,2304]{2,1,0:T(8,128)(2,1)}), bf16[16,16,2304]{2,1,0:T(8,128)(2,1)S(1)}, u32[]{:S(2)}, u32[]{:S(2)}) async-start(bf16[16,16,2304]{2,1,0:T(8,128)(2,1)} %get-tuple-element.59), calls=%async_computation.3 | async-start | bytes 2359296 | tf_op jit(solution)/shard_map/all_to_all | solution.py:360
  185.9 2.1 collective-permute-start.11
  188.1 2.3 %fusion = bf16[1,2048,256]{2,1,0:T(8,128)(2,1)} fusion(bf16[256,2048]{1,0:T(8,128)(2,1)S(1)} %constant_dynamic-update-slice_fusion.4, bf16[128,256]{1,0:T(8,128)(2,1)} %get-tuple-element.63, bf16[128,256]{1,0:T(8,128)(2,1)S(1)} %copy-done.15), kind=kOutput, calls=%fused_computation.2 | convolution fusion | flops 269221888 | bytes 2228224 | tf_op jit(solution)/shard_map/dot_general | solution.py:19
  190.4 3.4 %collective-permute-start.12 = (bf16[64,256]{1,0:T(8,128)(2,1)S(1)}, bf16[64,256]{1,0:T(8,128)(2,1)S(1)}, u32[]{:S(2)}, u32[]{:S(2)}) collective-permute-start(bf16[64,256]{1,0:T(8,128)(2,1)S(1)} %get-tuple-element.92), channel_id=1, source_target_pairs={{0,0},{1,1},{2,8},{3,9},{4,2},{5,3},{6,10},{7,11},{8,4},{9,5},{10,... | collective-permute-start | bytes 98312 | tf_op jit(solution)/shard_map/ppermute | solution.py:373
  193.8 1.9 collective-permute-start.13
  197.2 3.9 %collective-permute-done.12 = bf16[64,256]{1,0:T(8,128)(2,1)S(1)} collective-permute-done((bf16[64,256]{1,0:T(8,128)(2,1)S(1)}, bf16[64,256]{1,0:T(8,128)(2,1)S(1)}, u32[]{:S(2)}, u32[]{:S(2)}) %collective-permute-start.12) | collective-permute-done | bytes 32800 | tf_op jit(solution)/shard_map/ppermute | solution.py:373
  202.9 7.4 %collective-permute-start.10 = (bf16[4,4,2048]{2,1,0:T(4,128)(2,1)S(1)}, bf16[4,4,2048]{2,1,0:T(4,128)(2,1)S(1)}, u32[]{:S(2)}, u32[]{:S(2)}) collective-permute-start(bf16[4,4,2048]{2,1,0:T(4,128)(2,1)S(1)} %select_bitcast_fusion.6), channel_id=1, source_target_pairs={{0,496},{16,480},{32,464},{48,448},{64,432},{80,416},{96,400},{112... | collective-permute-start | bytes 196616 | tf_op jit(solution)/shard_map/ppermute | solution.py:463
  210.9 3.4 %collective-permute-done.10 = bf16[4,4,2048]{2,1,0:T(4,128)(2,1)S(1)} collective-permute-done((bf16[4,4,2048]{2,1,0:T(4,128)(2,1)S(1)}, bf16[4,4,2048]{2,1,0:T(4,128)(2,1)S(1)}, u32[]{:S(2)}, u32[]{:S(2)}) %collective-permute-start.10) | collective-permute-done | bytes 65568 | tf_op jit(solution)/shard_map/ppermute | solution.py:463
  (114 shorter events, 21.5 us)
Async XLA Ops:
  3.2 19.9 %collective-permute-start = (bf16[4,4,2048]{2,1,0:T(4,128)(2,1)S(1)}, bf16[4,4,2048]{2,1,0:T(4,128)(2,1)S(1)}, u32[]{:S(2)}, u32[]{:S(2)}) collective-permute-start(bf16[4,4,2048]{2,1,0:T(4,128)(2,1)S(1)} %broadcast_select_fusion.6), channel_id=1, source_target_pairs={{0,496},{16,480},{32,464},{48,448},{64,432},{80,416},{96,400},{112... | collective-permute-start | bytes 196616 | tf_op jit(solution)/shard_map/ppermute | solution.py:259
  16.4 10.8 %collective-permute-start.2 = (bf16[64,2048]{1,0:T(8,128)(2,1)}, bf16[64,2048]{1,0:T(8,128)(2,1)S(1)}, u32[]{:S(2)}, u32[]{:S(2)}) collective-permute-start(bf16[64,2048]{1,0:T(8,128)(2,1)} %bitcast.152), channel_id=1, source_target_pairs={{8,0},{9,1},{0,2},{1,3},{10,4},{11,5},{2,6},{3,7},{12,8},{13,9},{4... | collective-permute-start | bytes 786440 | tf_op jit(solution)/shard_map/ppermute | solution.py:275
  20.4 11.7 %collective-permute-start.1 = (bf16[64,2048]{1,0:T(8,128)(2,1)}, bf16[64,2048]{1,0:T(8,128)(2,1)S(1)}, u32[]{:S(2)}, u32[]{:S(2)}) collective-permute-start(bf16[64,2048]{1,0:T(8,128)(2,1)} %bitcast.153), channel_id=1, source_target_pairs={{0,0},{1,1},{8,2},{9,3},{2,4},{3,5},{10,6},{11,7},{4,8},{5,9},{12,... | collective-permute-start | bytes 786440 | tf_op jit(solution)/shard_map/ppermute | solution.py:275
  33.2 19.3 %all-to-all-start = ((bf16[8,32,2048]{2,1,0:T(8,128)(2,1)}), bf16[8,32,2048]{2,1,0:T(8,128)(2,1)S(1)}, u32[]{:S(2)}, u32[]{:S(2)}) async-start(bf16[8,32,2048]{2,1,0:T(8,128)(2,1)} %broadcast_in_dim.24), calls=%async_computation | async-start | bytes 2097152 | tf_op jit(solution)/shard_map/all_to_all | solution.py:299
  39.6 14.8 %collective-permute-start.4 = (bf16[2,64,2048]{2,1,0:T(8,128)(2,1)S(1)}, bf16[2,64,2048]{2,1,0:T(8,128)(2,1)}, u32[]{:S(2)}, u32[]{:S(2)}) collective-permute-start(bf16[2,64,2048]{2,1,0:T(8,128)(2,1)S(1)} %pad_maximum_fusion.2), channel_id=1, source_target_pairs={{0,1},{1,0},{2,3},{3,2},{4,5},{5,4},{6,7},{7,6},{8,9},{9,8},{10,11... | collective-permute-start | bytes 1572872 | tf_op jit(solution)/shard_map/ppermute | solution.py:284
  52.5 4.5 %collective-permute-start.3 = (bf16[8,32,2048]{2,1,0:T(8,128)(2,1)S(1)}, bf16[8,32,2048]{2,1,0:T(8,128)(2,1)S(1)}, u32[]{:S(2)}, u32[]{:S(2)}) collective-permute-start(bf16[8,32,2048]{2,1,0:T(8,128)(2,1)S(1)} %all-to-all-done), channel_id=1, source_target_pairs={{0,1},{1,0},{2,3},{3,2},{4,5},{5,4},{6,7},{7,6},{8,9},{9,8},{10,11... | collective-permute-start | bytes 3145736 | tf_op jit(solution)/shard_map/ppermute | solution.py:302
  61.9 26.0 %collective-permute-start.5 = (bf16[128,1408]{1,0:T(8,128)(2,1)S(1)}, bf16[128,1408]{1,0:T(8,128)(2,1)S(1)}, u32[]{:S(2)}, u32[]{:S(2)}) collective-permute-start(bf16[128,1408]{1,0:T(8,128)(2,1)S(1)} %get-tuple-element.42), channel_id=1, source_target_pairs={{0,496},{16,480},{32,464},{48,448},{64,432},{80,416},{96,400},{112... | collective-permute-start | bytes 1081352 | tf_op jit(solution)/shard_map/ppermute | solution.py:334
  92.1 18.8 %all-to-all-start.1 = ((bf16[16,16,2048]{2,1,0:T(8,128)(2,1)}), bf16[16,16,2048]{2,1,0:T(8,128)(2,1)}, u32[]{:S(2)}, u32[]{:S(2)}) async-start(bf16[16,16,2048]{2,1,0:T(8,128)(2,1)} %get-tuple-element.44), calls=%async_computation.1 | async-start | bytes 2097152 | tf_op jit(solution)/shard_map/all_to_all | solution.py:360
  112.3 12.7 %copy-start.11 = (bf16[8,2048]{1,0:T(8,128)(2,1)}, bf16[8,2048]{1,0:T(8,128)(2,1)S(1)}, u32[]{:S(2)}) copy-start(bf16[8,2048]{1,0:T(8,128)(2,1)S(1)} %get-tuple-element.83) | copy-start | bytes 98308
  112.4 12.7 %copy-start.13 = (bf16[8,2048]{1,0:T(8,128)(2,1)}, bf16[8,2048]{1,0:T(8,128)(2,1)S(1)}, u32[]{:S(2)}) copy-start(bf16[8,2048]{1,0:T(8,128)(2,1)S(1)} %get-tuple-element.82) | copy-start | bytes 98308
  112.6 6.9 %collective-permute-start.7 = (bf16[4,2,2048]{2,1,0:T(2,128)(2,1)S(1)}, bf16[4,2,2048]{2,1,0:T(2,128)(2,1)S(1)}, u32[]{:S(2)}, u32[]{:S(2)}) collective-permute-start(bf16[4,2,2048]{2,1,0:T(2,128)(2,1)S(1)} %get-tuple-element.46), channel_id=1, source_target_pairs={{16,0},{32,16},{48,32},{64,48},{80,64},{96,80},{112,96},{128,112},... | collective-permute-start | bytes 98312 | tf_op jit(solution)/shard_map/ppermute | solution.py:431
  114.6 9.2 %collective-permute-start.6 = (bf16[4,2,2048]{2,1,0:T(2,128)(2,1)S(1)}, bf16[4,2,2048]{2,1,0:T(2,128)(2,1)S(1)}, u32[]{:S(2)}, u32[]{:S(2)}) collective-permute-start(bf16[4,2,2048]{2,1,0:T(2,128)(2,1)S(1)} %get-tuple-element.45), channel_id=1, source_target_pairs={{0,16},{16,32},{32,48},{48,64},{64,80},{80,96},{96,112},{112,128},... | collective-permute-start | bytes 98312 | tf_op jit(solution)/shard_map/ppermute | solution.py:430
  125.1 26.6 %all-to-all-start.2 = ((bf16[16,16,2048]{2,1,0:T(8,128)(2,1)}), bf16[16,16,2048]{2,1,0:T(8,128)(2,1)}, u32[]{:S(2)}, u32[]{:S(2)}) async-start(bf16[16,16,2048]{2,1,0:T(8,128)(2,1)} %broadcast_in_dim.26), calls=%async_computation.2 | async-start | bytes 2097152 | tf_op jit(solution)/shard_map/all_to_all | solution.py:293
  132.1 43.8 %copy-start.4 = (f32[128,640]{1,0:T(8,128)S(1)}, f32[128,640]{1,0:T(8,128)}, u32[]{:S(2)}) copy-start(f32[128,640]{1,0:T(8,128)} %get-tuple-element.55.rest_0_) | copy-start | bytes 983044
  132.1 43.8 %copy-start.8 = (f32[1,2048]{1,0:T(1,128)S(1)}, f32[1,2048]{1,0:T(1,128)}, u32[]{:S(2)}) copy-start(f32[1,2048]{1,0:T(1,128)} %get-tuple-element.58.rest_7_) | copy-start | bytes 24580
  132.2 18.8 %collective-permute-start.8 = (bf16[128,640]{1,0:T(8,128)(2,1)}, bf16[128,640]{1,0:T(8,128)(2,1)S(1)}, u32[]{:S(2)}, u32[]{:S(2)}) collective-permute-start(bf16[128,640]{1,0:T(8,128)(2,1)} %get-tuple-element.51), channel_id=1, source_target_pairs={{0,496},{16,480},{32,464},{48,448},{64,432},{80,416},{96,400},{112... | collective-permute-start | bytes 491528 | tf_op jit(solution)/shard_map/ppermute | solution.py:334
  151.7 24.3 %copy-start.2 = (bf16[128,2048]{1,0:T(8,128)(2,1)S(1)}, bf16[128,2048]{1,0:T(8,128)(2,1)}, u32[]{:S(2)}) copy-start(bf16[128,2048]{1,0:T(8,128)(2,1)} %get-tuple-element.57.rest_2_) | copy-start | bytes 1572868
  151.7 24.3 %copy-start.6 = (bf16[128,640]{1,0:T(8,128)(2,1)S(1)}, bf16[128,640]{1,0:T(8,128)(2,1)}, u32[]{:S(2)}) copy-start(bf16[128,640]{1,0:T(8,128)(2,1)} %copy-done.5) | copy-start | bytes 491524
  154.7 21.3 %collective-permute-start.9 = (bf16[128,896]{1,0:T(8,128)(2,1)S(1)}, bf16[128,896]{1,0:T(8,128)(2,1)S(1)}, u32[]{:S(2)}, u32[]{:S(2)}) collective-permute-start(bf16[128,896]{1,0:T(8,128)(2,1)S(1)} %get-tuple-element.54), channel_id=1, source_target_pairs={{0,496},{16,480},{32,464},{48,448},{64,432},{80,416},{96,400},{112... | collective-permute-start | bytes 688136 | tf_op jit(solution)/shard_map/ppermute | solution.py:334
  179.2 5.6 %copy-start.14 = (bf16[8,2048]{1,0:T(8,128)(2,1)S(1)}, bf16[8,2048]{1,0:T(8,128)(2,1)}, u32[]{:S(2)}) copy-start(bf16[8,2048]{1,0:T(8,128)(2,1)} %copy-done.13) | copy-start | bytes 98308
  179.2 5.7 %copy-start.12 = (bf16[8,2048]{1,0:T(8,128)(2,1)S(1)}, bf16[8,2048]{1,0:T(8,128)(2,1)}, u32[]{:S(2)}) copy-start(bf16[8,2048]{1,0:T(8,128)(2,1)} %copy-done.11) | copy-start | bytes 98308
  179.2 8.8 %copy-start.10 = (bf16[128,2048]{1,0:T(8,128)(2,1)S(1)}, bf16[128,2048]{1,0:T(8,128)(2,1)}, u32[]{:S(2)}) copy-start(bf16[128,2048]{1,0:T(8,128)(2,1)} %get-tuple-element.61) | copy-start | bytes 1572868
  179.2 8.9 %copy-start.15 = (bf16[128,256]{1,0:T(8,128)(2,1)S(1)}, bf16[128,256]{1,0:T(8,128)(2,1)}, u32[]{:S(2)}) copy-start(bf16[128,256]{1,0:T(8,128)(2,1)} %get-tuple-element.62) | copy-start | bytes 196612
  179.2 23.3 %all-to-all-start.3 = ((bf16[16,16,2304]{2,1,0:T(8,128)(2,1)}), bf16[16,16,2304]{2,1,0:T(8,128)(2,1)S(1)}, u32[]{:S(2)}, u32[]{:S(2)}) async-start(bf16[16,16,2304]{2,1,0:T(8,128)(2,1)} %get-tuple-element.59), calls=%async_computation.3 | async-start | bytes 2359296 | tf_op jit(solution)/shard_map/all_to_all | solution.py:360
  184.9 10.9 %copy-start.20 = (bf16[128,256]{1,0:T(8,128)(2,1)S(1)}, bf16[128,256]{1,0:T(8,128)(2,1)}, u32[]{:S(2)}) copy-start(bf16[128,256]{1,0:T(8,128)(2,1)} %get-tuple-element.68) | copy-start | bytes 196612
  184.9 10.9 %copy-start.21 = (bf16[128,256]{1,0:T(8,128)(2,1)S(1)}, bf16[128,256]{1,0:T(8,128)(2,1)}, u32[]{:S(2)}) copy-start(bf16[128,256]{1,0:T(8,128)(2,1)} %get-tuple-element.69) | copy-start | bytes 196612
  184.9 10.8 %copy-start.18 = (bf16[128,2048]{1,0:T(8,128)(2,1)S(1)}, bf16[128,2048]{1,0:T(8,128)(2,1)}, u32[]{:S(2)}) copy-start(bf16[128,2048]{1,0:T(8,128)(2,1)} %get-tuple-element.66) | copy-start | bytes 1572868
  184.9 10.8 %copy-start.19 = (bf16[128,2048]{1,0:T(8,128)(2,1)S(1)}, bf16[128,2048]{1,0:T(8,128)(2,1)}, u32[]{:S(2)}) copy-start(bf16[128,2048]{1,0:T(8,128)(2,1)} %get-tuple-element.67) | copy-start | bytes 1572868
  185.9 4.4 %collective-permute-start.11 = (bf16[2,64,256]{2,1,0:T(8,128)(2,1)S(1)}, bf16[2,64,256]{2,1,0:T(8,128)(2,1)S(1)}, u32[]{:S(2)}, u32[]{:S(2)}) collective-permute-start(bf16[2,64,256]{2,1,0:T(8,128)(2,1)S(1)} %fusion.13), channel_id=1, source_target_pairs={{0,1},{1,0},{2,3},{3,2},{4,5},{5,4},{6,7},{7,6},{8,9},{9,8},{10,11... | collective-permute-start | bytes 196616 | tf_op jit(solution)/shard_map/ppermute | solution.py:366
  190.4 10.7 %collective-permute-start.12 = (bf16[64,256]{1,0:T(8,128)(2,1)S(1)}, bf16[64,256]{1,0:T(8,128)(2,1)S(1)}, u32[]{:S(2)}, u32[]{:S(2)}) collective-permute-start(bf16[64,256]{1,0:T(8,128)(2,1)S(1)} %get-tuple-element.92), channel_id=1, source_target_pairs={{0,0},{1,1},{2,8},{3,9},{4,2},{5,3},{6,10},{7,11},{8,4},{9,5},{10,... | collective-permute-start | bytes 98312 | tf_op jit(solution)/shard_map/ppermute | solution.py:373
  193.8 7.7 %collective-permute-start.13 = (bf16[64,256]{1,0:T(8,128)(2,1)S(1)}, bf16[64,256]{1,0:T(8,128)(2,1)S(1)}, u32[]{:S(2)}, u32[]{:S(2)}) collective-permute-start(bf16[64,256]{1,0:T(8,128)(2,1)S(1)} %get-tuple-element.93), channel_id=1, source_target_pairs={{0,8},{1,9},{2,0},{3,1},{4,10},{5,11},{6,2},{7,3},{8,12},{9,13},{1... | collective-permute-start | bytes 98312 | tf_op jit(solution)/shard_map/ppermute | solution.py:373
  202.9 11.4 %collective-permute-start.10 = (bf16[4,4,2048]{2,1,0:T(4,128)(2,1)S(1)}, bf16[4,4,2048]{2,1,0:T(4,128)(2,1)S(1)}, u32[]{:S(2)}, u32[]{:S(2)}) collective-permute-start(bf16[4,4,2048]{2,1,0:T(4,128)(2,1)S(1)} %select_bitcast_fusion.6), channel_id=1, source_target_pairs={{0,496},{16,480},{32,464},{48,448},{64,432},{80,416},{96,400},{112... | collective-permute-start | bytes 196616 | tf_op jit(solution)/shard_map/ppermute | solution.py:463
  (8 other events, 22.2 us)

commit v5 on v4

--- a/solution.py
+++ b/solution.py
@@ -117,14 +117,15 @@
 
 
 def attend_body(
-    plan, pieces, own_x, got_x, *rest
+    plan, pieces, core, own_x, got_x, *rest
 ):
     last = plan["last"]
     own_s, got_s = (own_x, got_x) if pieces == 2 else rest[: pieces - 2]
     stash, gain, query_mat, kv_mat, output_mat, *rest = rest[pieces - 2 :]
     if last:
         gain_before, rest = rest[0], rest[1:]
-    outs, block, sems = rest[: plan["outs"]], rest[plan["outs"]], rest[-1]
+    outs, sems = rest[: plan["outs"]], rest[-1]
+    block, other_block = rest[plan["outs"]], rest[plan["outs"] + 1]
     leaving = []
 
     def leave(index, value):
@@ -139,7 +140,7 @@
         copy.start()
         leaving.append(copy)
     rows, columns = plan["rows"], query_mat.shape[1]
-    shards = block.shape[0]
+    shards = 2 * block.shape[0]
     tokens, half = shards * rows, query_mat.shape[0]
     eval_columns = columns + 2 * HD
     heads = columns // HD
@@ -172,17 +173,17 @@
     keys, values = keyvals[:, :HD].astype(BF), keyvals[:, HD:].astype(BF)
     stacked = stack_heads(queries).astype(BF)
     probs = softmax_of(stacked, keys, mask)
-    leave(3, unstack_heads(mm(probs.astype(BF), values), tokens).astype(BF))
+    leave(4, unstack_heads(mm(probs.astype(BF), values), tokens).astype(BF))
     back = stack_heads(back_mixed).astype(BF)
     back_probs = mm_t(back, values)
     inner = jnp.sum(probs * back_probs, axis=1, keepdims=True)
     back_scores = probs * (back_probs - inner) / math.sqrt(HD)
     query_back = unstack_heads(mm(back_scores.astype(BF), keys), tokens).astype(BF)
-    leave(2, query_back)
+    leave(3, query_back)
     key_back = mm(back_scores.T.astype(BF), stacked)
     value_back = mm(probs.T.astype(BF), back)
     keyval_back = jnp.concatenate([key_back, value_back], axis=1).astype(BF)
-    leave(4, jnp.concatenate([key_back.T, value_back.T], axis=0).astype(BF))
+    leave(5, jnp.concatenate([key_back.T, value_back.T], axis=0).astype(BF))
 
     back_normed = mm_t(query_back, query_mat[...]) + mm(keyval_back, kv_mat[...])
     along = jnp.sum(query_back.astype(F32) * queries, axis=1, keepdims=True) + jnp.sum(
@@ -190,14 +191,17 @@
     )
     gain_row = gain[...].astype(F32)
     unit = stash[...].astype(F32) * inverse
-    leave(1, (unit * gain_row).astype(BF))
+    leave(2, (unit * gain_row).astype(BF))
     back_part = inverse * (back_normed * gain_row - unit * (along / (2 * half)))
     gain_part = jnp.sum(back_normed * unit, axis=0, keepdims=True)
 
     both = jnp.concatenate(
         [out_part.reshape(shards, rows, half), back_part.reshape(shards, rows, half)], axis=1
     )
-    block[:, :, :half] = both.astype(BF)
+    both = both.reshape(shards // 2, 2, 2 * rows, half)
+    for target, parity in ((block, 0), (other_block, 1)):
+        part = jnp.where(core[0] == parity, both[:, 0], both[:, 1])
+        target[:, :, :half] = part.astype(BF)
 
     if last:
         gain_part = gain_part + gain_before[...]
@@ -207,16 +211,19 @@
             [part[:, i * width : (i + 1) * width] for part in (high, gain_part - high) for i in range(rows)],
             axis=0,
         ).astype(BF)
-        for d in range(shards):
+        for d in range(shards // 2):
             block[d, :, half:] = spread
+            other_block[d, :, half:] = spread
     else:
-        leave(5, gain_part)
+        leave(6, gain_part)
     send(0)
+    send(1)
     for copy in leaving:
         copy.wait()
 
 
 VMEM = pl.BlockSpec(memory_space=pltpu.VMEM)
+SMEM = pl.BlockSpec(memory_space=pltpu.SMEM)
 HBM = pl.BlockSpec(memory_space=pltpu.HBM)
 PARAMS = pltpu.CompilerParams(vmem_limit_bytes=24 * 2**20)
 
@@ -287,17 +294,13 @@
         [jnp.where(even, mine, swapped), jnp.where(even, swapped, mine)], axis=1
     ).reshape(2 * HD, half)
 
+    same_core = [[2 * chip + core for chip in range(shards // 2)] for core in range(2)]
+
     def gather(local):
-        count = local.shape[0]
-        spread = jnp.broadcast_to(local.reshape(1, count * rows, half), (shards, count * rows, half))
-        return lax.all_to_all(spread, "tp", split_axis=0, concat_axis=0, tiled=True)
-
-    def gather_two_level(local):
         count, chips = local.shape[0], shards // 2
         spread = jnp.broadcast_to(local.reshape(1, count * rows, half), (chips, count * rows, half))
-        groups = [[2 * chip + core for chip in range(chips)] for core in range(2)]
         mine = lax.all_to_all(
-            spread, "tp", split_axis=0, concat_axis=0, axis_index_groups=groups, tiled=True
+            spread, "tp", split_axis=0, concat_axis=0, axis_index_groups=same_core, tiled=True
         )
         other = lax.ppermute(mine, "tp", swap_cores)
         both = jnp.stack(
@@ -337,7 +340,8 @@
         last = plan["last"]
         lanes = half + (half // rows if last else 0)
         shapes = [
-            jax.ShapeDtypeStruct((shards, 2 * rows, lanes), BF),
+            jax.ShapeDtypeStruct((shards // 2, 2 * rows, lanes), BF),
+            jax.ShapeDtypeStruct((shards // 2, 2 * rows, lanes), BF),
             jax.ShapeDtypeStruct((tokens, half), BF),
             jax.ShapeDtypeStruct((tokens, columns), BF),
             jax.ShapeDtypeStruct((tokens, columns), BF),
@@ -349,16 +353,27 @@
         return pl.pallas_call(
             functools.partial(attend_body, {**plan, "outs": len(shapes)}, len(pieces)),
             out_shape=[pltpu.HBM(shape.shape, shape.dtype) for shape in shapes],
-            in_specs=[VMEM] * (5 + len(pieces) + len(extra)),
+            in_specs=[SMEM] + [VMEM] * (5 + len(pieces) + len(extra)),
             out_specs=[HBM] * len(shapes),
             scratch_shapes=[pltpu.VMEM(shape.shape, shape.dtype) for shape in shapes]
             + [pltpu.SemaphoreType.DMA((len(shapes),))],
             compiler_params=PARAMS,
-        )(*pieces, stash, norm_gain, query_mat, kv_mat, output_mat, *extra)
-
-    def reduce_blocks(block):
-        received = lax.all_to_all(block, "tp", split_axis=0, concat_axis=0, tiled=True)
-        return jnp.sum(received.astype(F32), axis=0)
+        )(core, *pieces, stash, norm_gain, query_mat, kv_mat, output_mat, *extra)
+
+    core = (me % 2).astype(jnp.int32).reshape(1)
+
+    def reduce_blocks(mine, other, beside=None):
+        got = lax.ppermute(other, "tp", swap_cores)
+        chip = (mine.astype(F32) + got.astype(F32)).astype(BF)
+        if beside is not None:
+            chip, beside = lax.optimization_barrier((chip, beside))
+            beside = exchange(beside)
+        received = lax.all_to_all(
+            chip, "tp", split_axis=0, concat_axis=0, axis_index_groups=same_core, tiled=True
+        )
+        if beside is not None:
+            received, beside = lax.optimization_barrier((received, beside))
+        return jnp.sum(received.astype(F32), axis=0), beside
 
     def reduce_kv(blocks):
         parts = blocks.reshape(2, 2, HD // 2, -1)
@@ -383,7 +398,7 @@
     first_layer = (section == 0) | (section == sections - 1)
     last_layer = (section == last) | (section == last + 1)
 
-    gathered = gather_two_level(held)
+    gathered = gather(held)
     kept_arrays = tuple(range(1, 2 + ticks))
     groups = [((0, 2), 1)] + [((2 + k,), None) for k in range(1, ticks)]
     projected, (cots, *stash) = project(gathered, groups, kept_arrays)
@@ -404,7 +419,7 @@
             "count_s": 2 if first else 1,
             "cot_s": first,
         }
-        block, normed, query_back, mixed, kv_back, *rest = attend(
+        mine, other, normed, query_back, mixed, kv_back, *rest = attend(
             plan,
             (own_x, got_x) if first else (own_x, got_x, own_s, got_s),
             stash[k],
@@ -412,7 +427,8 @@
         )
         if k + 1 < ticks:
             gain_total = rest[0] if gain_total is None else gain_total + rest[0]
-        total = reduce_blocks(block)
+        message_s = None if k + 1 == ticks else later[k][0]
+        total, arrived_s = reduce_blocks(mine, other, message_s)
         layer_out = (act_rows.astype(F32) + total[:rows, :half]).astype(BF)
         back_input = (cot_rows.astype(F32) + total[rows:, :half]).astype(BF)
         out_rows.append(layer_out)
@@ -439,16 +455,16 @@
             act_rows = jnp.concatenate([lo[0], hi[1], hi[0], lo[1]], axis=0)
             cot_rows = jnp.concatenate([hi[2], lo[3], lo[2], hi[3]], axis=0)
             entering = jnp.stack([act_rows, cot_rows])
-            entering, message_s = lax.optimization_barrier((entering, later[k][0]))
-            own_s, got_s = later[k][1], exchange(message_s)
+            own_s, got_s = later[k][1], arrived_s
             act_rows, cot_rows = entering[0], entering[1]
             moved = gather(entering)
-            moved, got_s = lax.optimization_barrier((moved, got_s))
             ((message, own_x),), (cots,) = project(moved, [((0,), 1)], (1,))
             all_cots.append(cots)
             got_x = exchange(message)
 
     normed = jnp.concatenate(all_normed, axis=0)
+    total, *late = lax.optimization_barrier((total, *all_query_back, *all_mixed))
+    all_query_back, all_mixed = late[:ticks], late[ticks:]
     grad_query = t_mm(normed, jnp.concatenate(all_query_back, axis=0)).astype(BF)
     grad_keyval = mm(reduce_kv(jnp.concatenate(all_kv_back, axis=1)), normed).astype(BF).T
     grad_output = t_mm(

time: 217 us -> 220 us (1.014)
  the two profiles are of different devices: /device:TPU:26 before, /device:TPU:10 now
where the time goes in v5:
time: 220 us; the launch traced here: 218 us
  waiting for transfers between devices  90.2 us (41%)
  starting transfers between devices  77.7 us (35%)
  blocking collectives  12.4 us (6%)
  other arithmetic  11.8 us (5%)
  Pallas kernels  11.1 us (5%)
  local copies, waits for them, and re-layouts  9.84 us (4%)
  matrix products  3.92 us (2%)
    ppermute x3, waiting for transfers between devices, exchange(): return lax.ppermute(message, 'section', mirror)  52.2 us
    ppermute x1, starting transfers between devices, on_device(): arrived = lax.ppermute(other, 'section', mirror)  14.5 us
    all_to_all x1, blocking collectives, gather(): lax.all_to_all(spread, 'tp', split_axis=0, concat_axis=0, axis_index_grou...  12.4 us
    all_to_all x1, waiting for transfers between devices, gather(): lax.all_to_all(spread, 'tp', split_axis=0, concat_axis=0, axis_index_grou...  11.1 us
    ppermute x3, starting transfers between devices, exchange(): return lax.ppermute(message, 'section', mirror)  10.7 us
    all_to_all x2, starting transfers between devices, reduce_blocks(): lax.all_to_all(chip, 'tp', split_axis=0, concat_axis=0, axis_index_groups...  10.1 us
    ppermute x2, waiting for transfers between devices, on_device(): fetched = [lax.ppermute(kv_own, 'tp', route) for route in kv_routes]  8.56 us
    ppermute x2, starting transfers between devices, on_device(): fetched = [lax.ppermute(kv_own, 'tp', route) for route in kv_routes]  6.76 us
  transfers between devices with their start and end apart: 20, of which 13 were waited for; matrix products, arithmetic and copies ran while one was open for 5% of the time, Pallas kernels for 0%

profile of v5, /device:TPU:10, one launch (start us, length us, event | category | flops | bytes accessed | tf_op | source)
XLA Modules:
  0.0 218.4 jit_solution(16384652845341770441)
XLA Ops:
  3.2 14.5 %collective-permute-start = (bf16[4,4,2048]{2,1,0:T(4,128)(2,1)S(1)}, bf16[4,4,2048]{2,1,0:T(4,128)(2,1)S(1)}, u32[]{:S(2)}, u32[]{:S(2)}) collective-permute-start(bf16[4,4,2048]{2,1,0:T(4,128)(2,1)S(1)} %broadcast_select_fusion.6), channel_id=1, source_target_pairs={{0,496},{16,480},{32,464},{48,448},{64,432},{80,416},{96,400},{112... | collective-permute-start | bytes 196616 | tf_op jit(solution)/shard_map/ppermute | solution.py:266
  17.7 4.0 %collective-permute-start.2 = (bf16[64,2048]{1,0:T(8,128)(2,1)}, bf16[64,2048]{1,0:T(8,128)(2,1)S(1)}, u32[]{:S(2)}, u32[]{:S(2)}) collective-permute-start(bf16[64,2048]{1,0:T(8,128)(2,1)} %bitcast.155), channel_id=1, source_target_pairs={{8,0},{9,1},{0,2},{1,3},{10,4},{11,5},{2,6},{3,7},{12,8},{13,9},{4... | collective-permute-start | bytes 786440 | tf_op jit(solution)/shard_map/ppermute | solution.py:282
  21.8 2.7 %collective-permute-start.1 = (bf16[64,2048]{1,0:T(8,128)(2,1)}, bf16[64,2048]{1,0:T(8,128)(2,1)S(1)}, u32[]{:S(2)}, u32[]{:S(2)}) collective-permute-start(bf16[64,2048]{1,0:T(8,128)(2,1)} %bitcast.156), channel_id=1, source_target_pairs={{0,0},{1,1},{8,2},{9,3},{2,4},{3,5},{10,6},{11,7},{4,8},{5,9},{12,... | collective-permute-start | bytes 786440 | tf_op jit(solution)/shard_map/ppermute | solution.py:282
  24.7 3.8 %collective-permute-done.2 = bf16[64,2048]{1,0:T(8,128)(2,1)S(1)} collective-permute-done((bf16[64,2048]{1,0:T(8,128)(2,1)}, bf16[64,2048]{1,0:T(8,128)(2,1)S(1)}, u32[]{:S(2)}, u32[]{:S(2)}) %collective-permute-start.2) | collective-permute-done | bytes 262176 | tf_op jit(solution)/shard_map/ppermute | solution.py:282
  28.5 4.8 %collective-permute-done.1 = bf16[64,2048]{1,0:T(8,128)(2,1)S(1)} collective-permute-done((bf16[64,2048]{1,0:T(8,128)(2,1)}, bf16[64,2048]{1,0:T(8,128)(2,1)S(1)}, u32[]{:S(2)}, u32[]{:S(2)}) %collective-permute-start.1) | collective-permute-done | bytes 262176 | tf_op jit(solution)/shard_map/ppermute | solution.py:282
  34.3 6.4 %all-to-all-start = ((bf16[8,32,2048]{2,1,0:T(8,128)(2,1)}), bf16[8,32,2048]{2,1,0:T(8,128)(2,1)S(1)}, u32[]{:S(2)}, u32[]{:S(2)}) async-start(bf16[8,32,2048]{2,1,0:T(8,128)(2,1)} %broadcast_in_dim.24), calls=%async_computation | async-start | bytes 2097152 | tf_op jit(solution)/shard_map/all_to_all | solution.py:302
  40.8 1.9 collective-permute-start.4
  42.7 11.1 %all-to-all-done = bf16[8,32,2048]{2,1,0:T(8,128)(2,1)S(1)} async-done(((bf16[8,32,2048]{2,1,0:T(8,128)(2,1)}), bf16[8,32,2048]{2,1,0:T(8,128)(2,1)S(1)}, u32[]{:S(2)}, u32[]{:S(2)}) %all-to-all-start) | async-done | bytes 1048608 | tf_op jit(solution)/shard_map/all_to_all | solution.py:302
  60.1 3.2 %shard_map.136 = (bf16[128,1408]{1,0:T(8,128)(2,1)S(1)}, f32[128,1408]{1,0:T(8,128)S(1)}, bf16[128,640]{1,0:T(8,128)(2,1)}, f32[128,640]{1,0:T(8,128)}, bf16[128...) custom-call(bf16[16,32,2048]{2,1,0:T(8,128)(2,1)S(1)} %bitcast.143, ...), custom_call_target="tpu_custom_call" | custom-call | tf_op jit(solution)/shard_map/pallas_call | solution.py:321
  63.3 3.2 %collective-permute-start.5 = (bf16[128,1408]{1,0:T(8,128)(2,1)S(1)}, bf16[128,1408]{1,0:T(8,128)(2,1)S(1)}, u32[]{:S(2)}, u32[]{:S(2)}) collective-permute-start(bf16[128,1408]{1,0:T(8,128)(2,1)S(1)} %get-tuple-element.49), channel_id=1, source_target_pairs={{0,496},{16,480},{32,464},{48,448},{64,432},{80,416},{96,400},{112... | collective-permute-start | bytes 1081352 | tf_op jit(solution)/shard_map/ppermute | solution.py:337
  66.5 22.5 %collective-permute-done.5.got_x = bf16[128,1408]{1,0:T(8,128)(2,1)S(1)} collective-permute-done((bf16[128,1408]{1,0:T(8,128)(2,1)S(1)}, bf16[128,1408]{1,0:T(8,128)(2,1)S(1)}, u32[]{:S(2)}, u32[]{:S(2)}) %collective-permute-start.5) | collective-permute-done | bytes 360480 | tf_op jit(solution)/shard_map/ppermute | solution.py:337
  90.0 3.1 %shard_map.137 = (bf16[8,16,2048]{2,1,0:T(8,128)(2,1)}, bf16[8,16,2048]{2,1,0:T(8,128)(2,1)}, bf16[128,2048]{1,0:T(8,128)(2,1)}, bf16[128,256]{1,0:T(8,128)(2,1)...) custom-call(s32[1]{0:T(128)} %bitcast.4.core, f32[128,1408]{1,0:T(8,128)S(1)} %get-tuple-element.48.own_x, ...), custom_call_target="tpu_custom_call" | custom-call | tf_op jit(solution)/shard_map/pallas_call | solution.py:353
  95.1 2.1 collective-permute-done.6
  97.2 2.0 add_convert_fusion.1
  99.1 5.3 %all-to-all-start.1 = ((bf16[8,16,2048]{2,1,0:T(8,128)(2,1)}), bf16[8,16,2048]{2,1,0:T(8,128)(2,1)}, u32[]{:S(2)}, u32[]{:S(2)}) async-start(bf16[8,16,2048]{2,1,0:T(8,128)(2,1)} %add_convert_fusion.1), calls=%async_computation.1 | async-start | bytes 1048576 | tf_op jit(solution)/shard_map/all_to_all | solution.py:371
  104.4 3.1 %collective-permute-start.7 = (bf16[128,640]{1,0:T(8,128)(2,1)}, bf16[128,640]{1,0:T(8,128)(2,1)S(1)}, u32[]{:S(2)}, u32[]{:S(2)}) collective-permute-start(bf16[128,640]{1,0:T(8,128)(2,1)} %get-tuple-element.55), channel_id=1, source_target_pairs={{0,496},{16,480},{32,464},{48,448},{64,432},{80,416},{96,400},{112... | collective-permute-start | bytes 491528 | tf_op jit(solution)/shard_map/ppermute | solution.py:337
  108.2 13.7 %collective-permute-done.7.rest_1_ = bf16[128,640]{1,0:T(8,128)(2,1)S(1)} collective-permute-done((bf16[128,640]{1,0:T(8,128)(2,1)}, bf16[128,640]{1,0:T(8,128)(2,1)S(1)}, u32[]{:S(2)}, u32[]{:S(2)}) %collective-permute-start.7) | collective-permute-done | bytes 163872 | tf_op jit(solution)/shard_map/ppermute | solution.py:337
  125.9 4.8 %collective-permute-start.8 = (bf16[4,2,2048]{2,1,0:T(2,128)(2,1)S(1)}, bf16[4,2,2048]{2,1,0:T(2,128)(2,1)}, u32[]{:S(2)}, u32[]{:S(2)}) collective-permute-start(bf16[4,2,2048]{2,1,0:T(2,128)(2,1)S(1)} %get-tuple-element.57), channel_id=1, source_target_pairs={{0,16},{16,32},{32,48},{48,64},{64,80},{80,96},{96,112},{112,128},... | collective-permute-start | bytes 98312 | tf_op jit(solution)/shard_map/ppermute | solution.py:446
  131.6 3.5 %collective-permute-done.8 = bf16[4,2,2048]{2,1,0:T(2,128)(2,1)} collective-permute-done((bf16[4,2,2048]{2,1,0:T(2,128)(2,1)S(1)}, bf16[4,2,2048]{2,1,0:T(2,128)(2,1)}, u32[]{:S(2)}, u32[]{:S(2)}) %collective-permute-start.8) | collective-permute-done | bytes 32800 | tf_op jit(solution)/shard_map/ppermute | solution.py:446
  137.5 12.4 %all_to_all.20 = bf16[8,16,2048]{2,1,0:T(8,128)(2,1)S(1)} all-to-all(bf16[8,16,2048]{2,1,0:T(8,128)(2,1)S(1)} %broadcast_in_dim.26), channel_id=1, replica_groups={{0,2,4,6,8,10,12,14},{1,3,5,7,9,11,13,15},{16,18,20,22,24,26,28,30},{17..., dimensions={0} | all-to-all | bytes 1048576 | tf_op jit(solution)/shard_map/all_to_all | solution.py:302
  155.6 4.4 %collective-permute-start.11 = (bf16[128,896]{1,0:T(8,128)(2,1)S(1)}, bf16[128,896]{1,0:T(8,128)(2,1)S(1)}, u32[]{:S(2)}, u32[]{:S(2)}) collective-permute-start(bf16[128,896]{1,0:T(8,128)(2,1)S(1)} %get-tuple-element.62), channel_id=1, source_target_pairs={{0,496},{16,480},{32,464},{48,448},{64,432},{80,416},{96,400},{112... | collective-permute-start | bytes 688136 | tf_op jit(solution)/shard_map/ppermute | solution.py:337
  160.0 15.9 %collective-permute-done.11.got_x = bf16[128,896]{1,0:T(8,128)(2,1)S(1)} collective-permute-done((bf16[128,896]{1,0:T(8,128)(2,1)S(1)}, bf16[128,896]{1,0:T(8,128)(2,1)S(1)}, u32[]{:S(2)}, u32[]{:S(2)}) %collective-permute-start.11) | collective-permute-done | bytes 229408 | tf_op jit(solution)/shard_map/ppermute | solution.py:337
  176.0 3.1 %shard_map.139 = (bf16[8,16,2304]{2,1,0:T(8,128)(2,1)}, bf16[8,16,2304]{2,1,0:T(8,128)(2,1)}, bf16[128,2048]{1,0:T(8,128)(2,1)}, bf16[128,256]{1,0:T(8,128)(2,1)...) custom-call(s32[1]{0:T(128)} %bitcast.4.core, f32[128,896]{1,0:T(8,128)S(1)} %get-tuple-element.61.own_x, ...), custom_call_target="tpu_custom_call" | custom-call | tf_op jit(solution)/shard_map/pallas_call | solution.py:353
  179.1 2.1 collective-permute-start.12
  182.1 2.4 %collective-permute-start.14 = (bf16[2,64,256]{2,1,0:T(8,128)(2,1)S(1)}, bf16[2,64,256]{2,1,0:T(8,128)(2,1)S(1)}, u32[]{:S(2)}, u32[]{:S(2)}) collective-permute-start(bf16[2,64,256]{2,1,0:T(8,128)(2,1)S(1)} %fusion.13), channel_id=1, source_target_pairs={{0,1},{1,0},{2,3},{3,2},{4,5},{5,4},{6,7},{7,6},{8,9},{9,8},{10,11... | collective-permute-start | bytes 196616 | tf_op jit(solution)/shard_map/ppermute | solution.py:381
  184.5 2.1 add_convert_fusion
  186.6 4.8 %all-to-all-start.3 = ((bf16[8,16,2304]{2,1,0:T(8,128)(2,1)}), bf16[8,16,2304]{2,1,0:T(8,128)(2,1)S(1)}, u32[]{:S(2)}, u32[]{:S(2)}) async-start(bf16[8,16,2304]{2,1,0:T(8,128)(2,1)} %add_convert_fusion), calls=%async_computation.3 | async-start | bytes 1179648 | tf_op jit(solution)/shard_map/all_to_all | solution.py:371
  191.6 3.5 %collective-permute-start.15 = (bf16[64,256]{1,0:T(8,128)(2,1)S(1)}, bf16[64,256]{1,0:T(8,128)(2,1)S(1)}, u32[]{:S(2)}, u32[]{:S(2)}) collective-permute-start(bf16[64,256]{1,0:T(8,128)(2,1)S(1)} %get-tuple-element.108), channel_id=1, source_target_pairs={{0,0},{1,1},{2,8},{3,9},{4,2},{5,3},{6,10},{7,11},{8,4},{9,5},{10,... | collective-permute-start | bytes 98312 | tf_op jit(solution)/shard_map/ppermute | solution.py:388
  195.1 1.9 collective-permute-start.16
  197.1 3.8 %collective-permute-done.15 = bf16[64,256]{1,0:T(8,128)(2,1)S(1)} collective-permute-done((bf16[64,256]{1,0:T(8,128)(2,1)S(1)}, bf16[64,256]{1,0:T(8,128)(2,1)S(1)}, u32[]{:S(2)}, u32[]{:S(2)}) %collective-permute-start.15) | collective-permute-done | bytes 32800 | tf_op jit(solution)/shard_map/ppermute | solution.py:388
  204.5 5.0 %collective-permute-start.13 = (bf16[4,4,2048]{2,1,0:T(4,128)(2,1)S(1)}, bf16[4,4,2048]{2,1,0:T(4,128)(2,1)S(1)}, u32[]{:S(2)}, u32[]{:S(2)}) collective-permute-start(bf16[4,4,2048]{2,1,0:T(4,128)(2,1)S(1)} %select_bitcast_fusion.8), channel_id=1, source_target_pairs={{0,496},{16,480},{32,464},{48,448},{64,432},{80,416},{96,400},{112... | collective-permute-start | bytes 196616 | tf_op jit(solution)/shard_map/ppermute | solution.py:479
  212.5 4.3 %collective-permute-done.13 = bf16[4,4,2048]{2,1,0:T(4,128)(2,1)S(1)} collective-permute-done((bf16[4,4,2048]{2,1,0:T(4,128)(2,1)S(1)}, bf16[4,4,2048]{2,1,0:T(4,128)(2,1)S(1)}, u32[]{:S(2)}, u32[]{:S(2)}) %collective-permute-start.13) | collective-permute-done | bytes 65568 | tf_op jit(solution)/shard_map/ppermute | solution.py:479
  (129 shorter events, 35.6 us)
Async XLA Ops:
  3.2 21.3 %collective-permute-start = (bf16[4,4,2048]{2,1,0:T(4,128)(2,1)S(1)}, bf16[4,4,2048]{2,1,0:T(4,128)(2,1)S(1)}, u32[]{:S(2)}, u32[]{:S(2)}) collective-permute-start(bf16[4,4,2048]{2,1,0:T(4,128)(2,1)S(1)} %broadcast_select_fusion.6), channel_id=1, source_target_pairs={{0,496},{16,480},{32,464},{48,448},{64,432},{80,416},{96,400},{112... | collective-permute-start | bytes 196616 | tf_op jit(solution)/shard_map/ppermute | solution.py:266
  17.7 10.7 %collective-permute-start.2 = (bf16[64,2048]{1,0:T(8,128)(2,1)}, bf16[64,2048]{1,0:T(8,128)(2,1)S(1)}, u32[]{:S(2)}, u32[]{:S(2)}) collective-permute-start(bf16[64,2048]{1,0:T(8,128)(2,1)} %bitcast.155), channel_id=1, source_target_pairs={{8,0},{9,1},{0,2},{1,3},{10,4},{11,5},{2,6},{3,7},{12,8},{13,9},{4... | collective-permute-start | bytes 786440 | tf_op jit(solution)/shard_map/ppermute | solution.py:282
  21.8 11.5 %collective-permute-start.1 = (bf16[64,2048]{1,0:T(8,128)(2,1)}, bf16[64,2048]{1,0:T(8,128)(2,1)S(1)}, u32[]{:S(2)}, u32[]{:S(2)}) collective-permute-start(bf16[64,2048]{1,0:T(8,128)(2,1)} %bitcast.156), channel_id=1, source_target_pairs={{0,0},{1,1},{8,2},{9,3},{2,4},{3,5},{10,6},{11,7},{4,8},{5,9},{12,... | collective-permute-start | bytes 786440 | tf_op jit(solution)/shard_map/ppermute | solution.py:282
  34.3 19.5 %all-to-all-start = ((bf16[8,32,2048]{2,1,0:T(8,128)(2,1)}), bf16[8,32,2048]{2,1,0:T(8,128)(2,1)S(1)}, u32[]{:S(2)}, u32[]{:S(2)}) async-start(bf16[8,32,2048]{2,1,0:T(8,128)(2,1)} %broadcast_in_dim.24), calls=%async_computation | async-start | bytes 2097152 | tf_op jit(solution)/shard_map/all_to_all | solution.py:302
  40.8 15.0 %collective-permute-start.4 = (bf16[2,64,2048]{2,1,0:T(8,128)(2,1)S(1)}, bf16[2,64,2048]{2,1,0:T(8,128)(2,1)}, u32[]{:S(2)}, u32[]{:S(2)}) collective-permute-start(bf16[2,64,2048]{2,1,0:T(8,128)(2,1)S(1)} %pad_maximum_fusion.3), channel_id=1, source_target_pairs={{0,1},{1,0},{2,3},{3,2},{4,5},{5,4},{6,7},{7,6},{8,9},{9,8},{10,11... | collective-permute-start | bytes 1572872 | tf_op jit(solution)/shard_map/ppermute | solution.py:291
  53.9 4.5 %collective-permute-start.3 = (bf16[8,32,2048]{2,1,0:T(8,128)(2,1)S(1)}, bf16[8,32,2048]{2,1,0:T(8,128)(2,1)S(1)}, u32[]{:S(2)}, u32[]{:S(2)}) collective-permute-start(bf16[8,32,2048]{2,1,0:T(8,128)(2,1)S(1)} %all-to-all-done), channel_id=1, source_target_pairs={{0,1},{1,0},{2,3},{3,2},{4,5},{5,4},{6,7},{7,6},{8,9},{9,8},{10,11... | collective-permute-start | bytes 3145736 | tf_op jit(solution)/shard_map/ppermute | solution.py:305
  63.3 25.7 %collective-permute-start.5 = (bf16[128,1408]{1,0:T(8,128)(2,1)S(1)}, bf16[128,1408]{1,0:T(8,128)(2,1)S(1)}, u32[]{:S(2)}, u32[]{:S(2)}) collective-permute-start(bf16[128,1408]{1,0:T(8,128)(2,1)S(1)} %get-tuple-element.49), channel_id=1, source_target_pairs={{0,496},{16,480},{32,464},{48,448},{64,432},{80,416},{96,400},{112... | collective-permute-start | bytes 1081352 | tf_op jit(solution)/shard_map/ppermute | solution.py:337
  93.1 14.4 %copy-start.19 = (bf16[2,1,2,4096]{3,2,1,0:T(2,128)(2,1)S(1)}, bf16[2,1,2,4096]{3,2,1,0:T(2,128)(2,1)}, u32[]{:S(2)}) copy-start(bf16[2,1,2,4096]{3,2,1,0:T(2,128)(2,1)} %param.13) | copy-start | bytes 98308
  93.1 14.4 %copy-start.20 = (bf16[2,1,2,4096]{3,2,1,0:T(2,128)(2,1)S(1)}, bf16[2,1,2,4096]{3,2,1,0:T(2,128)(2,1)}, u32[]{:S(2)}) copy-start(bf16[2,1,2,4096]{3,2,1,0:T(2,128)(2,1)} %param.10) | copy-start | bytes 98308
  93.1 4.0 %collective-permute-start.6 = (bf16[8,16,2048]{2,1,0:T(8,128)(2,1)}, bf16[8,16,2048]{2,1,0:T(8,128)(2,1)S(1)}, u32[]{:S(2)}, u32[]{:S(2)}) collective-permute-start(bf16[8,16,2048]{2,1,0:T(8,128)(2,1)} %get-tuple-element.52), channel_id=1, source_target_pairs={{0,1},{1,0},{2,3},{3,2},{4,5},{5,4},{6,7},{7,6},{8,9},{9,8},{10,11... | collective-permute-start | bytes 1572872 | tf_op jit(solution)/shard_map/ppermute | solution.py:366
  99.1 22.8 %all-to-all-start.1 = ((bf16[8,16,2048]{2,1,0:T(8,128)(2,1)}), bf16[8,16,2048]{2,1,0:T(8,128)(2,1)}, u32[]{:S(2)}, u32[]{:S(2)}) async-start(bf16[8,16,2048]{2,1,0:T(8,128)(2,1)} %add_convert_fusion.1), calls=%async_computation.1 | async-start | bytes 1048576 | tf_op jit(solution)/shard_map/all_to_all | solution.py:371
  104.4 17.5 %collective-permute-start.7 = (bf16[128,640]{1,0:T(8,128)(2,1)}, bf16[128,640]{1,0:T(8,128)(2,1)S(1)}, u32[]{:S(2)}, u32[]{:S(2)}) collective-permute-start(bf16[128,640]{1,0:T(8,128)(2,1)} %get-tuple-element.55), channel_id=1, source_target_pairs={{0,496},{16,480},{32,464},{48,448},{64,432},{80,416},{96,400},{112... | collective-permute-start | bytes 491528 | tf_op jit(solution)/shard_map/ppermute | solution.py:337
  123.9 7.6 %collective-permute-start.9 = (bf16[4,2,2048]{2,1,0:T(2,128)(2,1)}, bf16[4,2,2048]{2,1,0:T(2,128)(2,1)S(1)}, u32[]{:S(2)}, u32[]{:S(2)}) collective-permute-start(bf16[4,2,2048]{2,1,0:T(2,128)(2,1)} %get-tuple-element.58), channel_id=1, source_target_pairs={{16,0},{32,16},{48,32},{64,48},{80,64},{96,80},{112,96},{128,112},... | collective-permute-start | bytes 98312 | tf_op jit(solution)/shard_map/ppermute | solution.py:447
  125.9 9.2 %collective-permute-start.8 = (bf16[4,2,2048]{2,1,0:T(2,128)(2,1)S(1)}, bf16[4,2,2048]{2,1,0:T(2,128)(2,1)}, u32[]{:S(2)}, u32[]{:S(2)}) collective-permute-start(bf16[4,2,2048]{2,1,0:T(2,128)(2,1)S(1)} %get-tuple-element.57), channel_id=1, source_target_pairs={{0,16},{16,32},{32,48},{48,64},{64,80},{80,96},{96,112},{112,128},... | collective-permute-start | bytes 98312 | tf_op jit(solution)/shard_map/ppermute | solution.py:446
  149.9 3.8 %collective-permute-start.10 = (bf16[8,16,2048]{2,1,0:T(8,128)(2,1)S(1)}, bf16[8,16,2048]{2,1,0:T(8,128)(2,1)S(1)}, u32[]{:S(2)}, u32[]{:S(2)}) collective-permute-start(bf16[8,16,2048]{2,1,0:T(8,128)(2,1)S(1)} %all_to_all.20), channel_id=1, source_target_pairs={{0,1},{1,0},{2,3},{3,2},{4,5},{5,4},{6,7},{7,6},{8,9},{9,8},{10,11... | collective-permute-start | bytes 1572872 | tf_op jit(solution)/shard_map/ppermute | solution.py:305
  153.8 22.1 %copy-start.2 = (bf16[128,2048]{1,0:T(8,128)(2,1)S(1)}, bf16[128,2048]{1,0:T(8,128)(2,1)}, u32[]{:S(2)}) copy-start(bf16[128,2048]{1,0:T(8,128)(2,1)} %get-tuple-element.65.rest_2_) | copy-start | bytes 1572868
  153.8 22.1 %copy-start.4 = (f32[128,640]{1,0:T(8,128)S(1)}, f32[128,640]{1,0:T(8,128)}, u32[]{:S(2)}) copy-start(f32[128,640]{1,0:T(8,128)} %get-tuple-element.63.rest_0_) | copy-start | bytes 983044
  153.9 22.1 %copy-start.6 = (f32[1,2048]{1,0:T(1,128)S(1)}, f32[1,2048]{1,0:T(1,128)}, u32[]{:S(2)}) copy-start(f32[1,2048]{1,0:T(1,128)} %get-tuple-element.66.rest_7_) | copy-start | bytes 24580
  155.6 20.4 %collective-permute-start.11 = (bf16[128,896]{1,0:T(8,128)(2,1)S(1)}, bf16[128,896]{1,0:T(8,128)(2,1)S(1)}, u32[]{:S(2)}, u32[]{:S(2)}) collective-permute-start(bf16[128,896]{1,0:T(8,128)(2,1)S(1)} %get-tuple-element.62), channel_id=1, source_target_pairs={{0,496},{16,480},{32,464},{48,448},{64,432},{80,416},{96,400},{112... | collective-permute-start | bytes 688136 | tf_op jit(solution)/shard_map/ppermute | solution.py:337
  179.1 12.3 %copy-start.7 = (bf16[128,2048]{1,0:T(8,128)(2,1)S(1)}, bf16[128,2048]{1,0:T(8,128)(2,1)}, u32[]{:S(2)}) copy-start(bf16[128,2048]{1,0:T(8,128)(2,1)} %get-tuple-element.69) | copy-start | bytes 1572868
  179.1 5.4 %collective-permute-start.12 = (bf16[8,16,2304]{2,1,0:T(8,128)(2,1)}, bf16[8,16,2304]{2,1,0:T(8,128)(2,1)S(1)}, u32[]{:S(2)}, u32[]{:S(2)}) collective-permute-start(bf16[8,16,2304]{2,1,0:T(8,128)(2,1)} %get-tuple-element.68), channel_id=1, source_target_pairs={{0,1},{1,0},{2,3},{3,2},{4,5},{5,4},{6,7},{7,6},{8,9},{9,8},{10,11... | collective-permute-start | bytes 1769480 | tf_op jit(solution)/shard_map/ppermute | solution.py:366
  182.1 9.4 %collective-permute-start.14 = (bf16[2,64,256]{2,1,0:T(8,128)(2,1)S(1)}, bf16[2,64,256]{2,1,0:T(8,128)(2,1)S(1)}, u32[]{:S(2)}, u32[]{:S(2)}) collective-permute-start(bf16[2,64,256]{2,1,0:T(8,128)(2,1)S(1)} %fusion.13), channel_id=1, source_target_pairs={{0,1},{1,0},{2,3},{3,2},{4,5},{5,4},{6,7},{7,6},{8,9},{9,8},{10,11... | collective-permute-start | bytes 196616 | tf_op jit(solution)/shard_map/ppermute | solution.py:381
  184.5 12.6 %copy-start.8 = (bf16[128,2048]{1,0:T(8,128)(2,1)S(1)}, bf16[128,2048]{1,0:T(8,128)(2,1)}, u32[]{:S(2)}) copy-start(bf16[128,2048]{1,0:T(8,128)(2,1)} %get-tuple-element.70) | copy-start | bytes 1572868
  186.6 16.9 %all-to-all-start.3 = ((bf16[8,16,2304]{2,1,0:T(8,128)(2,1)}), bf16[8,16,2304]{2,1,0:T(8,128)(2,1)S(1)}, u32[]{:S(2)}, u32[]{:S(2)}) async-start(bf16[8,16,2304]{2,1,0:T(8,128)(2,1)} %add_convert_fusion), calls=%async_computation.3 | async-start | bytes 1179648 | tf_op jit(solution)/shard_map/all_to_all | solution.py:371
  191.4 12.1 %copy-start.10 = (bf16[2,2048]{1,0:T(2,128)(2,1)S(1)}, bf16[2,2048]{1,0:T(2,128)(2,1)}, u32[]{:S(2)}) copy-start(bf16[2,2048]{1,0:T(2,128)(2,1)} %copy-done.9) | copy-start | bytes 24580
  191.4 12.1 %copy-start.12 = (bf16[2,2048]{1,0:T(2,128)(2,1)S(1)}, bf16[2,2048]{1,0:T(2,128)(2,1)}, u32[]{:S(2)}) copy-start(bf16[2,2048]{1,0:T(2,128)(2,1)} %copy-done.11) | copy-start | bytes 24580
  191.5 12.1 %copy-start.14 = (bf16[2,2048]{1,0:T(2,128)(2,1)S(1)}, bf16[2,2048]{1,0:T(2,128)(2,1)}, u32[]{:S(2)}) copy-start(bf16[2,2048]{1,0:T(2,128)(2,1)} %copy-done.13) | copy-start | bytes 24580
  191.6 18.0 %copy-start.15 = (bf16[128,256]{1,0:T(8,128)(2,1)S(1)}, bf16[128,256]{1,0:T(8,128)(2,1)}, u32[]{:S(2)}) copy-start(bf16[128,256]{1,0:T(8,128)(2,1)} %get-tuple-element.75) | copy-start | bytes 196612
  191.6 18.0 %copy-start.16 = (bf16[128,256]{1,0:T(8,128)(2,1)S(1)}, bf16[128,256]{1,0:T(8,128)(2,1)}, u32[]{:S(2)}) copy-start(bf16[128,256]{1,0:T(8,128)(2,1)} %get-tuple-element.76) | copy-start | bytes 196612
  191.6 9.3 %collective-permute-start.15 = (bf16[64,256]{1,0:T(8,128)(2,1)S(1)}, bf16[64,256]{1,0:T(8,128)(2,1)S(1)}, u32[]{:S(2)}, u32[]{:S(2)}) collective-permute-start(bf16[64,256]{1,0:T(8,128)(2,1)S(1)} %get-tuple-element.108), channel_id=1, source_target_pairs={{0,0},{1,1},{2,8},{3,9},{4,2},{5,3},{6,10},{7,11},{8,4},{9,5},{10,... | collective-permute-start | bytes 98312 | tf_op jit(solution)/shard_map/ppermute | solution.py:388
  195.1 7.3 %collective-permute-start.16 = (bf16[64,256]{1,0:T(8,128)(2,1)S(1)}, bf16[64,256]{1,0:T(8,128)(2,1)S(1)}, u32[]{:S(2)}, u32[]{:S(2)}) collective-permute-start(bf16[64,256]{1,0:T(8,128)(2,1)S(1)} %get-tuple-element.109), channel_id=1, source_target_pairs={{0,8},{1,9},{2,0},{3,1},{4,10},{5,11},{6,2},{7,3},{8,12},{9,13},{1... | collective-permute-start | bytes 98312 | tf_op jit(solution)/shard_map/ppermute | solution.py:388
  204.5 12.3 %collective-permute-start.13 = (bf16[4,4,2048]{2,1,0:T(4,128)(2,1)S(1)}, bf16[4,4,2048]{2,1,0:T(4,128)(2,1)S(1)}, u32[]{:S(2)}, u32[]{:S(2)}) collective-permute-start(bf16[4,4,2048]{2,1,0:T(4,128)(2,1)S(1)} %select_bitcast_fusion.8), channel_id=1, source_target_pairs={{0,496},{16,480},{32,464},{48,448},{64,432},{80,416},{96,400},{112... | collective-permute-start | bytes 196616 | tf_op jit(solution)/shard_map/ppermute | solution.py:479
  (13 other events, 46.3 us)

commit v6 on v5

--- a/solution.py
+++ b/solution.py
@@ -125,18 +125,13 @@
     if last:
         gain_before, rest = rest[0], rest[1:]
     outs, sems = rest[: plan["outs"]], rest[-1]
-    block, other_block = rest[plan["outs"]], rest[plan["outs"] + 1]
+    block, other_block = outs[:2]
     leaving = []
 
     def leave(index, value):
-        buffer = rest[plan["outs"] + index]
+        buffer = rest[plan["outs"] + index - 2]
         buffer[...] = value
-        send(index)
-
-    def send(index):
-        copy = pltpu.make_async_copy(
-            rest[plan["outs"] + index], outs[index], sems.at[index]
-        )
+        copy = pltpu.make_async_copy(buffer, outs[index], sems.at[index - 2])
         copy.start()
         leaving.append(copy)
     rows, columns = plan["rows"], query_mat.shape[1]
@@ -216,8 +211,6 @@
             other_block[d, :, half:] = spread
     else:
         leave(6, gain_part)
-    send(0)
-    send(1)
     for copy in leaving:
         copy.wait()
 
@@ -310,14 +303,14 @@
 
     eval_columns = columns + 2 * HD
 
-    def project(gathered, groups, kept_arrays):
+    def project(gathered, groups, kept_arrays, near=()):
         shapes, far = [], []
         for i, (acts, cot) in enumerate(groups):
             size = len(acts) * eval_columns + (0 if cot is None else columns) + HD
             shapes += [((tokens, size), BF), ((tokens, size), F32)]
             far += [i > 0] * 2
         shapes += [((tokens, half), BF)] * len(kept_arrays)
-        far += [True] * len(kept_arrays)
+        far += [kept_array not in near for kept_array in kept_arrays]
         outs = pl.pallas_call(
             functools.partial(project_body, groups, kept_arrays, far, rows),
             out_shape=[
@@ -352,11 +345,11 @@
         extra = [gain_before] if last else []
         return pl.pallas_call(
             functools.partial(attend_body, {**plan, "outs": len(shapes)}, len(pieces)),
-            out_shape=[pltpu.HBM(shape.shape, shape.dtype) for shape in shapes],
+            out_shape=shapes[:2] + [pltpu.HBM(shape.shape, shape.dtype) for shape in shapes[2:]],
             in_specs=[SMEM] + [VMEM] * (5 + len(pieces) + len(extra)),
-            out_specs=[HBM] * len(shapes),
-            scratch_shapes=[pltpu.VMEM(shape.shape, shape.dtype) for shape in shapes]
-            + [pltpu.SemaphoreType.DMA((len(shapes),))],
+            out_specs=[VMEM] * 2 + [HBM] * (len(shapes) - 2),
+            scratch_shapes=[pltpu.VMEM(shape.shape, shape.dtype) for shape in shapes[2:]]
+            + [pltpu.SemaphoreType.DMA((len(shapes) - 2,))],
             compiler_params=PARAMS,
         )(core, *pieces, stash, norm_gain, query_mat, kv_mat, output_mat, *extra)
 
@@ -371,8 +364,6 @@
         received = lax.all_to_all(
             chip, "tp", split_axis=0, concat_axis=0, axis_index_groups=same_core, tiled=True
         )
-        if beside is not None:
-            received, beside = lax.optimization_barrier((received, beside))
         return jnp.sum(received.astype(F32), axis=0), beside
 
     def reduce_kv(blocks):
@@ -401,7 +392,7 @@
     gathered = gather(held)
     kept_arrays = tuple(range(1, 2 + ticks))
     groups = [((0, 2), 1)] + [((2 + k,), None) for k in range(1, ticks)]
-    projected, (cots, *stash) = project(gathered, groups, kept_arrays)
+    projected, (cots, *stash) = project(gathered, groups, kept_arrays, near=(2,))
     (message, own_x), later = projected[0], projected[1:]
     got_x = exchange(message)
     all_cots = [cots]
@@ -445,7 +436,9 @@
             going_up, going_down = lax.optimization_barrier((going_up, going_down))
             from_below = lax.ppermute(going_up, "section", ahead)
             from_above = lax.ppermute(going_down, "section", behind)
-            from_below, from_above = lax.optimization_barrier((from_below, from_above))
+            from_below, from_above, arrived_s = lax.optimization_barrier(
+                (from_below, from_above, arrived_s)
+            )
             fresh = jnp.stack(
                 [fresh_acts[0, k], fresh_acts[1, k], fresh_grads[0, k], fresh_grads[1, k]]
             )

time: 220 us -> 207 us (0.941)
  the two profiles are of different devices: /device:TPU:10 before, /device:TPU:26 now
where the time goes in v6:
time: 207 us; the launch traced here: 205 us
  starting transfers between devices  80.7 us (39%)
  waiting for transfers between devices  77.5 us (37%)
  blocking collectives  12.3 us (6%)
  Pallas kernels  9.82 us (5%)
  other arithmetic  9.62 us (5%)
  local copies, waits for them, and re-layouts  8.79 us (4%)
  matrix products  4.97 us (2%)
    ppermute x3, waiting for transfers between devices, exchange(): return lax.ppermute(message, 'section', mirror)  38.4 us
    ppermute x3, starting transfers between devices, exchange(): return lax.ppermute(message, 'section', mirror)  13.4 us
    ppermute x1, starting transfers between devices, on_device(): arrived = lax.ppermute(other, 'section', mirror)  13.2 us
    all_to_all x1, blocking collectives, gather(): lax.all_to_all(spread, 'tp', split_axis=0, concat_axis=0, axis_index_grou...  12.3 us
    all_to_all x1, waiting for transfers between devices, gather(): lax.all_to_all(spread, 'tp', split_axis=0, concat_axis=0, axis_index_grou...  11 us
    all_to_all x2, starting transfers between devices, reduce_blocks(): lax.all_to_all(chip, 'tp', split_axis=0, concat_axis=0, axis_index_groups...  10.4 us
    ppermute x2, waiting for transfers between devices, on_device(): fetched = [lax.ppermute(kv_own, 'tp', route) for route in kv_routes]  8.79 us
    ppermute x2, starting transfers between devices, on_device(): fetched = [lax.ppermute(kv_own, 'tp', route) for route in kv_routes]  6.76 us
  transfers between devices with their start and end apart: 20, of which 13 were waited for; matrix products, arithmetic and copies ran while one was open for 6% of the time, Pallas kernels for 0%

profile of v6, /device:TPU:26, one launch (start us, length us, event | category | flops | bytes accessed | tf_op | source)
XLA Modules:
  0.0 205.2 jit_solution(3140992814837607150)
XLA Ops:
  3.2 13.2 %collective-permute-start = (bf16[4,4,2048]{2,1,0:T(4,128)(2,1)S(1)}, bf16[4,4,2048]{2,1,0:T(4,128)(2,1)S(1)}, u32[]{:S(2)}, u32[]{:S(2)}) collective-permute-start(bf16[4,4,2048]{2,1,0:T(4,128)(2,1)S(1)} %broadcast_select_fusion.6), channel_id=1, source_target_pairs={{0,496},{16,480},{32,464},{48,448},{64,432},{80,416},{96,400},{112... | collective-permute-start | bytes 196616 | tf_op jit(solution)/shard_map/ppermute | solution.py:259
  16.4 4.0 %collective-permute-start.2 = (bf16[64,2048]{1,0:T(8,128)(2,1)}, bf16[64,2048]{1,0:T(8,128)(2,1)S(1)}, u32[]{:S(2)}, u32[]{:S(2)}) collective-permute-start(bf16[64,2048]{1,0:T(8,128)(2,1)} %bitcast.155), channel_id=1, source_target_pairs={{8,0},{9,1},{0,2},{1,3},{10,4},{11,5},{2,6},{3,7},{12,8},{13,9},{4... | collective-permute-start | bytes 786440 | tf_op jit(solution)/shard_map/ppermute | solution.py:275
  20.4 2.7 %collective-permute-start.1 = (bf16[64,2048]{1,0:T(8,128)(2,1)}, bf16[64,2048]{1,0:T(8,128)(2,1)S(1)}, u32[]{:S(2)}, u32[]{:S(2)}) collective-permute-start(bf16[64,2048]{1,0:T(8,128)(2,1)} %bitcast.156), channel_id=1, source_target_pairs={{0,0},{1,1},{8,2},{9,3},{2,4},{3,5},{10,6},{11,7},{4,8},{5,9},{12,... | collective-permute-start | bytes 786440 | tf_op jit(solution)/shard_map/ppermute | solution.py:275
  23.3 3.8 %collective-permute-done.2 = bf16[64,2048]{1,0:T(8,128)(2,1)S(1)} collective-permute-done((bf16[64,2048]{1,0:T(8,128)(2,1)}, bf16[64,2048]{1,0:T(8,128)(2,1)S(1)}, u32[]{:S(2)}, u32[]{:S(2)}) %collective-permute-start.2) | collective-permute-done | bytes 262176 | tf_op jit(solution)/shard_map/ppermute | solution.py:275
  27.2 5.0 %collective-permute-done.1 = bf16[64,2048]{1,0:T(8,128)(2,1)S(1)} collective-permute-done((bf16[64,2048]{1,0:T(8,128)(2,1)}, bf16[64,2048]{1,0:T(8,128)(2,1)S(1)}, u32[]{:S(2)}, u32[]{:S(2)}) %collective-permute-start.1) | collective-permute-done | bytes 262176 | tf_op jit(solution)/shard_map/ppermute | solution.py:275
  33.2 6.3 %all-to-all-start = ((bf16[8,32,2048]{2,1,0:T(8,128)(2,1)}), bf16[8,32,2048]{2,1,0:T(8,128)(2,1)S(1)}, u32[]{:S(2)}, u32[]{:S(2)}) async-start(bf16[8,32,2048]{2,1,0:T(8,128)(2,1)} %broadcast_in_dim.24), calls=%async_computation | async-start | bytes 2097152 | tf_op jit(solution)/shard_map/all_to_all | solution.py:295
  39.6 1.9 collective-permute-start.4
  41.5 11.0 %all-to-all-done = bf16[8,32,2048]{2,1,0:T(8,128)(2,1)S(1)} async-done(((bf16[8,32,2048]{2,1,0:T(8,128)(2,1)}), bf16[8,32,2048]{2,1,0:T(8,128)(2,1)S(1)}, u32[]{:S(2)}, u32[]{:S(2)}) %all-to-all-start) | async-done | bytes 1048608 | tf_op jit(solution)/shard_map/all_to_all | solution.py:295
  58.8 3.0 %shard_map.136 = (bf16[128,1408]{1,0:T(8,128)(2,1)S(1)}, f32[128,1408]{1,0:T(8,128)S(1)}, bf16[128,640]{1,0:T(8,128)(2,1)}, f32[128,640]{1,0:T(8,128)}, bf16[128...) custom-call(bf16[16,32,2048]{2,1,0:T(8,128)(2,1)S(1)} %bitcast.143, ...), custom_call_target="tpu_custom_call" | custom-call | tf_op jit(solution)/shard_map/pallas_call | solution.py:314
  61.8 3.2 %collective-permute-start.5 = (bf16[128,1408]{1,0:T(8,128)(2,1)S(1)}, bf16[128,1408]{1,0:T(8,128)(2,1)S(1)}, u32[]{:S(2)}, u32[]{:S(2)}) collective-permute-start(bf16[128,1408]{1,0:T(8,128)(2,1)S(1)} %get-tuple-element.48), channel_id=1, source_target_pairs={{0,496},{16,480},{32,464},{48,448},{64,432},{80,416},{96,400},{112... | collective-permute-start | bytes 1081352 | tf_op jit(solution)/shard_map/ppermute | solution.py:330
  64.9 22.9 %collective-permute-done.5.got_x = bf16[128,1408]{1,0:T(8,128)(2,1)S(1)} collective-permute-done((bf16[128,1408]{1,0:T(8,128)(2,1)S(1)}, bf16[128,1408]{1,0:T(8,128)(2,1)S(1)}, u32[]{:S(2)}, u32[]{:S(2)}) %collective-permute-start.5) | collective-permute-done | bytes 360480 | tf_op jit(solution)/shard_map/ppermute | solution.py:330
  87.8 2.7 %shard_map.137 = (bf16[8,16,2048]{2,1,0:T(8,128)(2,1)S(1)}, bf16[8,16,2048]{2,1,0:T(8,128)(2,1)S(1)}, bf16[128,2048]{1,0:T(8,128)(2,1)}, bf16[128,256]{1,0:T(8,1...) custom-call(s32[1]{0:T(128)} %bitcast.4.core, ...), custom_call_target="tpu_custom_call" | custom-call | tf_op jit(solution)/shard_map/pallas_call | solution.py:346
  90.5 1.9 collective-permute-start.6
  95.3 5.2 %all-to-all-start.1 = ((bf16[8,16,2048]{2,1,0:T(8,128)(2,1)}), bf16[8,16,2048]{2,1,0:T(8,128)(2,1)}, u32[]{:S(2)}, u32[]{:S(2)}) async-start(bf16[8,16,2048]{2,1,0:T(8,128)(2,1)} %add_convert_fusion.1), calls=%async_computation.1 | async-start | bytes 1048576 | tf_op jit(solution)/shard_map/all_to_all | solution.py:364
  101.1 3.7 %collective-permute-start.9 = (bf16[128,640]{1,0:T(8,128)(2,1)}, bf16[128,640]{1,0:T(8,128)(2,1)S(1)}, u32[]{:S(2)}, u32[]{:S(2)}) collective-permute-start(bf16[128,640]{1,0:T(8,128)(2,1)} %get-tuple-element.56), channel_id=1, source_target_pairs={{0,496},{16,480},{32,464},{48,448},{64,432},{80,416},{96,400},{112... | collective-permute-start | bytes 491528 | tf_op jit(solution)/shard_map/ppermute | solution.py:330
  104.8 5.0 %all-to-all-done.1 = bf16[8,16,2048]{2,1,0:T(8,128)(2,1)} async-done(((bf16[8,16,2048]{2,1,0:T(8,128)(2,1)}), bf16[8,16,2048]{2,1,0:T(8,128)(2,1)}, u32[]{:S(2)}, u32[]{:S(2)}) %all-to-all-start.1) | async-done | bytes 524320 | tf_op jit(solution)/shard_map/all_to_all | solution.py:364
  111.9 2.1 %collective-permute-start.8 = (bf16[4,2,2048]{2,1,0:T(2,128)(2,1)}, bf16[4,2,2048]{2,1,0:T(2,128)(2,1)S(1)}, u32[]{:S(2)}, u32[]{:S(2)}) collective-permute-start(bf16[4,2,2048]{2,1,0:T(2,128)(2,1)} %get-tuple-element.55), channel_id=1, source_target_pairs={{16,0},{32,16},{48,32},{64,48},{80,64},{96,80},{112,96},{128,112},... | collective-permute-start | bytes 98312 | tf_op jit(solution)/shard_map/ppermute | solution.py:438
  114.0 4.6 %collective-permute-start.7 = (bf16[4,2,2048]{2,1,0:T(2,128)(2,1)S(1)}, bf16[4,2,2048]{2,1,0:T(2,128)(2,1)}, u32[]{:S(2)}, u32[]{:S(2)}) collective-permute-start(bf16[4,2,2048]{2,1,0:T(2,128)(2,1)S(1)} %get-tuple-element.54), channel_id=1, source_target_pairs={{0,16},{16,32},{32,48},{48,64},{64,80},{80,96},{96,112},{112,128},... | collective-permute-start | bytes 98312 | tf_op jit(solution)/shard_map/ppermute | solution.py:437
  119.5 3.8 %collective-permute-done.7 = bf16[4,2,2048]{2,1,0:T(2,128)(2,1)} collective-permute-done((bf16[4,2,2048]{2,1,0:T(2,128)(2,1)S(1)}, bf16[4,2,2048]{2,1,0:T(2,128)(2,1)}, u32[]{:S(2)}, u32[]{:S(2)}) %collective-permute-start.7) | collective-permute-done | bytes 32800 | tf_op jit(solution)/shard_map/ppermute | solution.py:437
  125.7 12.3 %all_to_all.20 = bf16[8,16,2048]{2,1,0:T(8,128)(2,1)S(1)} all-to-all(bf16[8,16,2048]{2,1,0:T(8,128)(2,1)S(1)} %broadcast_in_dim.26), channel_id=1, replica_groups={{0,2,4,6,8,10,12,14},{1,3,5,7,9,11,13,15},{16,18,20,22,24,26,28,30},{17..., dimensions={0} | all-to-all | bytes 1048576 | tf_op jit(solution)/shard_map/all_to_all | solution.py:295
  138.0 1.9 collective-permute-start.10
  143.7 6.5 %collective-permute-start.11 = (bf16[128,896]{1,0:T(8,128)(2,1)S(1)}, bf16[128,896]{1,0:T(8,128)(2,1)S(1)}, u32[]{:S(2)}, u32[]{:S(2)}) collective-permute-start(bf16[128,896]{1,0:T(8,128)(2,1)S(1)} %get-tuple-element.60), channel_id=1, source_target_pairs={{0,496},{16,480},{32,464},{48,448},{64,432},{80,416},{96,400},{112... | collective-permute-start | bytes 688136 | tf_op jit(solution)/shard_map/ppermute | solution.py:330
  150.2 15.5 %collective-permute-done.11.got_x = bf16[128,896]{1,0:T(8,128)(2,1)S(1)} collective-permute-done((bf16[128,896]{1,0:T(8,128)(2,1)S(1)}, bf16[128,896]{1,0:T(8,128)(2,1)S(1)}, u32[]{:S(2)}, u32[]{:S(2)}) %collective-permute-start.11) | collective-permute-done | bytes 229408 | tf_op jit(solution)/shard_map/ppermute | solution.py:330
  165.8 2.4 %shard_map.139 = (bf16[8,16,2304]{2,1,0:T(8,128)(2,1)S(1)}, bf16[8,16,2304]{2,1,0:T(8,128)(2,1)S(1)}, bf16[128,2048]{1,0:T(8,128)(2,1)}, bf16[128,256]{1,0:T(8,1...) custom-call(s32[1]{0:T(128)} %bitcast.4.core, f32[128,896]{1,0:T(8,128)S(1)} %get-tuple-element.59.own_x, ...), custom_call_target="tpu_custom_call" | custom-call | tf_op jit(solution)/shard_map/pallas_call | solution.py:346
  168.2 2.1 %collective-permute-start.12 = (bf16[8,16,2304]{2,1,0:T(8,128)(2,1)S(1)}, bf16[8,16,2304]{2,1,0:T(8,128)(2,1)S(1)}, u32[]{:S(2)}, u32[]{:S(2)}) collective-permute-start(bf16[8,16,2304]{2,1,0:T(8,128)(2,1)S(1)} %get-tuple-element.66), channel_id=1, source_target_pairs={{0,1},{1,0},{2,3},{3,2},{4,5},{5,4},{6,7},{7,6},{8,9},{9,8},{10,11... | collective-permute-start | bytes 1769480 | tf_op jit(solution)/shard_map/ppermute | solution.py:359
  171.2 2.4 %collective-permute-start.14 = (bf16[2,64,256]{2,1,0:T(8,128)(2,1)S(1)}, bf16[2,64,256]{2,1,0:T(8,128)(2,1)S(1)}, u32[]{:S(2)}, u32[]{:S(2)}) collective-permute-start(bf16[2,64,256]{2,1,0:T(8,128)(2,1)S(1)} %fusion.13), channel_id=1, source_target_pairs={{0,1},{1,0},{2,3},{3,2},{4,5},{5,4},{6,7},{7,6},{8,9},{9,8},{10,11... | collective-permute-start | bytes 196616 | tf_op jit(solution)/shard_map/ppermute | solution.py:372
  174.6 5.2 %all-to-all-start.3 = ((bf16[8,16,2304]{2,1,0:T(8,128)(2,1)}), bf16[8,16,2304]{2,1,0:T(8,128)(2,1)S(1)}, u32[]{:S(2)}, u32[]{:S(2)}) async-start(bf16[8,16,2304]{2,1,0:T(8,128)(2,1)} %add_convert_fusion), calls=%async_computation.3 | async-start | bytes 1179648 | tf_op jit(solution)/shard_map/all_to_all | solution.py:364
  180.0 3.5 %collective-permute-start.15 = (bf16[64,256]{1,0:T(8,128)(2,1)S(1)}, bf16[64,256]{1,0:T(8,128)(2,1)S(1)}, u32[]{:S(2)}, u32[]{:S(2)}) collective-permute-start(bf16[64,256]{1,0:T(8,128)(2,1)S(1)} %get-tuple-element.106), channel_id=1, source_target_pairs={{0,0},{1,1},{2,8},{3,9},{4,2},{5,3},{6,10},{7,11},{8,4},{9,5},{10,... | collective-permute-start | bytes 98312 | tf_op jit(solution)/shard_map/ppermute | solution.py:379
  183.6 1.9 collective-permute-start.16
  185.5 4.0 %collective-permute-done.15 = bf16[64,256]{1,0:T(8,128)(2,1)S(1)} collective-permute-done((bf16[64,256]{1,0:T(8,128)(2,1)S(1)}, bf16[64,256]{1,0:T(8,128)(2,1)S(1)}, u32[]{:S(2)}, u32[]{:S(2)}) %collective-permute-start.15) | collective-permute-done | bytes 32800 | tf_op jit(solution)/shard_map/ppermute | solution.py:379
  192.9 6.4 %collective-permute-start.13 = (bf16[4,4,2048]{2,1,0:T(4,128)(2,1)S(1)}, bf16[4,4,2048]{2,1,0:T(4,128)(2,1)S(1)}, u32[]{:S(2)}, u32[]{:S(2)}) collective-permute-start(bf16[4,4,2048]{2,1,0:T(4,128)(2,1)S(1)} %select_bitcast_fusion.8), channel_id=1, source_target_pairs={{0,496},{16,480},{32,464},{48,448},{64,432},{80,416},{96,400},{112... | collective-permute-start | bytes 196616 | tf_op jit(solution)/shard_map/ppermute | solution.py:472
  200.8 2.5 %fusion.1 = bf16[1,2048,256]{2,1,0:T(8,128)(2,1)} fusion(bf16[128,2048]{1,0:T(8,128)(2,1)} %get-tuple-element.78, bf16[128,2048]{1,0:T(8,128)(2,1)S(1)} %copy-done.20, bf16[128,256]{1,0:T(8,128)(2,1)S(1)} %copy-done.22, bf16[128,256]{1,0:T(8,128)(2,1)S(1)} %copy-done.21), kind=kOutput, calls=%fused_computation.3 | convolution fusion | flops 271319040 | bytes 2228224 | tf_op jit(solution)/shard_map/dot_general | solution.py:19
  (125 shorter events, 31.0 us)
Async XLA Ops:
  3.2 19.9 %collective-permute-start = (bf16[4,4,2048]{2,1,0:T(4,128)(2,1)S(1)}, bf16[4,4,2048]{2,1,0:T(4,128)(2,1)S(1)}, u32[]{:S(2)}, u32[]{:S(2)}) collective-permute-start(bf16[4,4,2048]{2,1,0:T(4,128)(2,1)S(1)} %broadcast_select_fusion.6), channel_id=1, source_target_pairs={{0,496},{16,480},{32,464},{48,448},{64,432},{80,416},{96,400},{112... | collective-permute-start | bytes 196616 | tf_op jit(solution)/shard_map/ppermute | solution.py:259
  16.4 10.8 %collective-permute-start.2 = (bf16[64,2048]{1,0:T(8,128)(2,1)}, bf16[64,2048]{1,0:T(8,128)(2,1)S(1)}, u32[]{:S(2)}, u32[]{:S(2)}) collective-permute-start(bf16[64,2048]{1,0:T(8,128)(2,1)} %bitcast.155), channel_id=1, source_target_pairs={{8,0},{9,1},{0,2},{1,3},{10,4},{11,5},{2,6},{3,7},{12,8},{13,9},{4... | collective-permute-start | bytes 786440 | tf_op jit(solution)/shard_map/ppermute | solution.py:275
  20.4 11.7 %collective-permute-start.1 = (bf16[64,2048]{1,0:T(8,128)(2,1)}, bf16[64,2048]{1,0:T(8,128)(2,1)S(1)}, u32[]{:S(2)}, u32[]{:S(2)}) collective-permute-start(bf16[64,2048]{1,0:T(8,128)(2,1)} %bitcast.156), channel_id=1, source_target_pairs={{0,0},{1,1},{8,2},{9,3},{2,4},{3,5},{10,6},{11,7},{4,8},{5,9},{12,... | collective-permute-start | bytes 786440 | tf_op jit(solution)/shard_map/ppermute | solution.py:275
  33.2 19.3 %all-to-all-start = ((bf16[8,32,2048]{2,1,0:T(8,128)(2,1)}), bf16[8,32,2048]{2,1,0:T(8,128)(2,1)S(1)}, u32[]{:S(2)}, u32[]{:S(2)}) async-start(bf16[8,32,2048]{2,1,0:T(8,128)(2,1)} %broadcast_in_dim.24), calls=%async_computation | async-start | bytes 2097152 | tf_op jit(solution)/shard_map/all_to_all | solution.py:295
  39.6 14.8 %collective-permute-start.4 = (bf16[2,64,2048]{2,1,0:T(8,128)(2,1)S(1)}, bf16[2,64,2048]{2,1,0:T(8,128)(2,1)}, u32[]{:S(2)}, u32[]{:S(2)}) collective-permute-start(bf16[2,64,2048]{2,1,0:T(8,128)(2,1)S(1)} %pad_maximum_fusion.3), channel_id=1, source_target_pairs={{0,1},{1,0},{2,3},{3,2},{4,5},{5,4},{6,7},{7,6},{8,9},{9,8},{10,11... | collective-permute-start | bytes 1572872 | tf_op jit(solution)/shard_map/ppermute | solution.py:284
  52.5 4.5 %collective-permute-start.3 = (bf16[8,32,2048]{2,1,0:T(8,128)(2,1)S(1)}, bf16[8,32,2048]{2,1,0:T(8,128)(2,1)S(1)}, u32[]{:S(2)}, u32[]{:S(2)}) collective-permute-start(bf16[8,32,2048]{2,1,0:T(8,128)(2,1)S(1)} %all-to-all-done), channel_id=1, source_target_pairs={{0,1},{1,0},{2,3},{3,2},{4,5},{5,4},{6,7},{7,6},{8,9},{9,8},{10,11... | collective-permute-start | bytes 3145736 | tf_op jit(solution)/shard_map/ppermute | solution.py:298
  61.8 26.0 %collective-permute-start.5 = (bf16[128,1408]{1,0:T(8,128)(2,1)S(1)}, bf16[128,1408]{1,0:T(8,128)(2,1)S(1)}, u32[]{:S(2)}, u32[]{:S(2)}) collective-permute-start(bf16[128,1408]{1,0:T(8,128)(2,1)S(1)} %get-tuple-element.48), channel_id=1, source_target_pairs={{0,496},{16,480},{32,464},{48,448},{64,432},{80,416},{96,400},{112... | collective-permute-start | bytes 1081352 | tf_op jit(solution)/shard_map/ppermute | solution.py:330
  90.5 10.0 %copy-start.18 = (bf16[2,1,2,4096]{3,2,1,0:T(2,128)(2,1)S(1)}, bf16[2,1,2,4096]{3,2,1,0:T(2,128)(2,1)}, u32[]{:S(2)}) copy-start(bf16[2,1,2,4096]{3,2,1,0:T(2,128)(2,1)} %param.13) | copy-start | bytes 98308
  90.5 9.9 %copy-start.19 = (bf16[2,1,2,4096]{3,2,1,0:T(2,128)(2,1)S(1)}, bf16[2,1,2,4096]{3,2,1,0:T(2,128)(2,1)}, u32[]{:S(2)}) copy-start(bf16[2,1,2,4096]{3,2,1,0:T(2,128)(2,1)} %param.10) | copy-start | bytes 98308
  90.5 3.8 %collective-permute-start.6 = (bf16[8,16,2048]{2,1,0:T(8,128)(2,1)S(1)}, bf16[8,16,2048]{2,1,0:T(8,128)(2,1)S(1)}, u32[]{:S(2)}, u32[]{:S(2)}) collective-permute-start(bf16[8,16,2048]{2,1,0:T(8,128)(2,1)S(1)} %get-tuple-element.51), channel_id=1, source_target_pairs={{0,1},{1,0},{2,3},{3,2},{4,5},{5,4},{6,7},{7,6},{8,9},{9,8},{10,11... | collective-permute-start | bytes 1572872 | tf_op jit(solution)/shard_map/ppermute | solution.py:359
  95.3 14.6 %all-to-all-start.1 = ((bf16[8,16,2048]{2,1,0:T(8,128)(2,1)}), bf16[8,16,2048]{2,1,0:T(8,128)(2,1)}, u32[]{:S(2)}, u32[]{:S(2)}) async-start(bf16[8,16,2048]{2,1,0:T(8,128)(2,1)} %add_convert_fusion.1), calls=%async_computation.1 | async-start | bytes 1048576 | tf_op jit(solution)/shard_map/all_to_all | solution.py:364
  101.1 18.4 %collective-permute-start.9 = (bf16[128,640]{1,0:T(8,128)(2,1)}, bf16[128,640]{1,0:T(8,128)(2,1)S(1)}, u32[]{:S(2)}, u32[]{:S(2)}) collective-permute-start(bf16[128,640]{1,0:T(8,128)(2,1)} %get-tuple-element.56), channel_id=1, source_target_pairs={{0,496},{16,480},{32,464},{48,448},{64,432},{80,416},{96,400},{112... | collective-permute-start | bytes 491528 | tf_op jit(solution)/shard_map/ppermute | solution.py:330
  111.9 7.6 %collective-permute-start.8 = (bf16[4,2,2048]{2,1,0:T(2,128)(2,1)}, bf16[4,2,2048]{2,1,0:T(2,128)(2,1)S(1)}, u32[]{:S(2)}, u32[]{:S(2)}) collective-permute-start(bf16[4,2,2048]{2,1,0:T(2,128)(2,1)} %get-tuple-element.55), channel_id=1, source_target_pairs={{16,0},{32,16},{48,32},{64,48},{80,64},{96,80},{112,96},{128,112},... | collective-permute-start | bytes 98312 | tf_op jit(solution)/shard_map/ppermute | solution.py:438
  114.0 9.3 %collective-permute-start.7 = (bf16[4,2,2048]{2,1,0:T(2,128)(2,1)S(1)}, bf16[4,2,2048]{2,1,0:T(2,128)(2,1)}, u32[]{:S(2)}, u32[]{:S(2)}) collective-permute-start(bf16[4,2,2048]{2,1,0:T(2,128)(2,1)S(1)} %get-tuple-element.54), channel_id=1, source_target_pairs={{0,16},{16,32},{32,48},{48,64},{64,80},{80,96},{96,112},{112,128},... | collective-permute-start | bytes 98312 | tf_op jit(solution)/shard_map/ppermute | solution.py:437
  138.0 3.8 %collective-permute-start.10 = (bf16[8,16,2048]{2,1,0:T(8,128)(2,1)S(1)}, bf16[8,16,2048]{2,1,0:T(8,128)(2,1)S(1)}, u32[]{:S(2)}, u32[]{:S(2)}) collective-permute-start(bf16[8,16,2048]{2,1,0:T(8,128)(2,1)S(1)} %all_to_all.20), channel_id=1, source_target_pairs={{0,1},{1,0},{2,3},{3,2},{4,5},{5,4},{6,7},{7,6},{8,9},{9,8},{10,11... | collective-permute-start | bytes 1572872 | tf_op jit(solution)/shard_map/ppermute | solution.py:298
  142.0 23.8 %copy-start.2 = (bf16[128,2048]{1,0:T(8,128)(2,1)S(1)}, bf16[128,2048]{1,0:T(8,128)(2,1)}, u32[]{:S(2)}) copy-start(bf16[128,2048]{1,0:T(8,128)(2,1)} %get-tuple-element.63.rest_2_) | copy-start | bytes 1572868
  142.0 23.8 %copy-start.3 = (f32[128,640]{1,0:T(8,128)S(1)}, f32[128,640]{1,0:T(8,128)}, u32[]{:S(2)}) copy-start(f32[128,640]{1,0:T(8,128)} %get-tuple-element.61.rest_0_) | copy-start | bytes 983044
  142.0 23.8 %copy-start.5 = (f32[1,2048]{1,0:T(1,128)S(1)}, f32[1,2048]{1,0:T(1,128)}, u32[]{:S(2)}) copy-start(f32[1,2048]{1,0:T(1,128)} %get-tuple-element.64.rest_7_) | copy-start | bytes 24580
  143.7 22.0 %collective-permute-start.11 = (bf16[128,896]{1,0:T(8,128)(2,1)S(1)}, bf16[128,896]{1,0:T(8,128)(2,1)S(1)}, u32[]{:S(2)}, u32[]{:S(2)}) collective-permute-start(bf16[128,896]{1,0:T(8,128)(2,1)S(1)} %get-tuple-element.60), channel_id=1, source_target_pairs={{0,496},{16,480},{32,464},{48,448},{64,432},{80,416},{96,400},{112... | collective-permute-start | bytes 688136 | tf_op jit(solution)/shard_map/ppermute | solution.py:330
  168.2 11.6 %copy-start.6 = (bf16[128,2048]{1,0:T(8,128)(2,1)S(1)}, bf16[128,2048]{1,0:T(8,128)(2,1)}, u32[]{:S(2)}) copy-start(bf16[128,2048]{1,0:T(8,128)(2,1)} %get-tuple-element.67) | copy-start | bytes 1572868
  168.2 5.4 %collective-permute-start.12 = (bf16[8,16,2304]{2,1,0:T(8,128)(2,1)S(1)}, bf16[8,16,2304]{2,1,0:T(8,128)(2,1)S(1)}, u32[]{:S(2)}, u32[]{:S(2)}) collective-permute-start(bf16[8,16,2304]{2,1,0:T(8,128)(2,1)S(1)} %get-tuple-element.66), channel_id=1, source_target_pairs={{0,1},{1,0},{2,3},{3,2},{4,5},{5,4},{6,7},{7,6},{8,9},{9,8},{10,11... | collective-permute-start | bytes 1769480 | tf_op jit(solution)/shard_map/ppermute | solution.py:359
  171.2 8.8 %collective-permute-start.14 = (bf16[2,64,256]{2,1,0:T(8,128)(2,1)S(1)}, bf16[2,64,256]{2,1,0:T(8,128)(2,1)S(1)}, u32[]{:S(2)}, u32[]{:S(2)}) collective-permute-start(bf16[2,64,256]{2,1,0:T(8,128)(2,1)S(1)} %fusion.13), channel_id=1, source_target_pairs={{0,1},{1,0},{2,3},{3,2},{4,5},{5,4},{6,7},{7,6},{8,9},{9,8},{10,11... | collective-permute-start | bytes 196616 | tf_op jit(solution)/shard_map/ppermute | solution.py:372
  173.6 11.9 %copy-start.7 = (bf16[128,2048]{1,0:T(8,128)(2,1)S(1)}, bf16[128,2048]{1,0:T(8,128)(2,1)}, u32[]{:S(2)}) copy-start(bf16[128,2048]{1,0:T(8,128)(2,1)} %get-tuple-element.68) | copy-start | bytes 1572868
  174.6 17.3 %all-to-all-start.3 = ((bf16[8,16,2304]{2,1,0:T(8,128)(2,1)}), bf16[8,16,2304]{2,1,0:T(8,128)(2,1)S(1)}, u32[]{:S(2)}, u32[]{:S(2)}) async-start(bf16[8,16,2304]{2,1,0:T(8,128)(2,1)} %add_convert_fusion), calls=%async_computation.3 | async-start | bytes 1179648 | tf_op jit(solution)/shard_map/all_to_all | solution.py:364
  179.9 12.1 %copy-start.9 = (bf16[2,2048]{1,0:T(2,128)(2,1)S(1)}, bf16[2,2048]{1,0:T(2,128)(2,1)}, u32[]{:S(2)}) copy-start(bf16[2,2048]{1,0:T(2,128)(2,1)} %copy-done.8) | copy-start | bytes 24580
  179.9 12.1 %copy-start.11 = (bf16[2,2048]{1,0:T(2,128)(2,1)S(1)}, bf16[2,2048]{1,0:T(2,128)(2,1)}, u32[]{:S(2)}) copy-start(bf16[2,2048]{1,0:T(2,128)(2,1)} %copy-done.10) | copy-start | bytes 24580
  179.9 12.1 %copy-start.13 = (bf16[2,2048]{1,0:T(2,128)(2,1)S(1)}, bf16[2,2048]{1,0:T(2,128)(2,1)}, u32[]{:S(2)}) copy-start(bf16[2,2048]{1,0:T(2,128)(2,1)} %copy-done.12) | copy-start | bytes 24580
  180.0 19.4 %copy-start.14 = (bf16[128,256]{1,0:T(8,128)(2,1)S(1)}, bf16[128,256]{1,0:T(8,128)(2,1)}, u32[]{:S(2)}) copy-start(bf16[128,256]{1,0:T(8,128)(2,1)} %get-tuple-element.73) | copy-start | bytes 196612
  180.0 19.4 %copy-start.15 = (bf16[128,256]{1,0:T(8,128)(2,1)S(1)}, bf16[128,256]{1,0:T(8,128)(2,1)}, u32[]{:S(2)}) copy-start(bf16[128,256]{1,0:T(8,128)(2,1)} %get-tuple-element.74) | copy-start | bytes 196612
  180.0 9.5 %collective-permute-start.15 = (bf16[64,256]{1,0:T(8,128)(2,1)S(1)}, bf16[64,256]{1,0:T(8,128)(2,1)S(1)}, u32[]{:S(2)}, u32[]{:S(2)}) collective-permute-start(bf16[64,256]{1,0:T(8,128)(2,1)S(1)} %get-tuple-element.106), channel_id=1, source_target_pairs={{0,0},{1,1},{2,8},{3,9},{4,2},{5,3},{6,10},{7,11},{8,4},{9,5},{10,... | collective-permute-start | bytes 98312 | tf_op jit(solution)/shard_map/ppermute | solution.py:379
  183.6 7.3 %collective-permute-start.16 = (bf16[64,256]{1,0:T(8,128)(2,1)S(1)}, bf16[64,256]{1,0:T(8,128)(2,1)S(1)}, u32[]{:S(2)}, u32[]{:S(2)}) collective-permute-start(bf16[64,256]{1,0:T(8,128)(2,1)S(1)} %get-tuple-element.107), channel_id=1, source_target_pairs={{0,8},{1,9},{2,0},{3,1},{4,10},{5,11},{6,2},{7,3},{8,12},{9,13},{1... | collective-permute-start | bytes 98312 | tf_op jit(solution)/shard_map/ppermute | solution.py:379
  192.9 10.6 %collective-permute-start.13 = (bf16[4,4,2048]{2,1,0:T(4,128)(2,1)S(1)}, bf16[4,4,2048]{2,1,0:T(4,128)(2,1)S(1)}, u32[]{:S(2)}, u32[]{:S(2)}) collective-permute-start(bf16[4,4,2048]{2,1,0:T(4,128)(2,1)S(1)} %select_bitcast_fusion.8), channel_id=1, source_target_pairs={{0,496},{16,480},{32,464},{48,448},{64,432},{80,416},{96,400},{112... | collective-permute-start | bytes 196616 | tf_op jit(solution)/shard_map/ppermute | solution.py:472
  (11 other events, 41.2 us)

commit v7 on v6

--- a/solution.py
+++ b/solution.py
@@ -273,7 +273,6 @@
     ]
     swap_cores = [(i, i ^ 1) for i in range(shards)]
     fetched = [lax.ppermute(kv_own, "tp", route) for route in kv_routes]
-    held, fetched = lax.optimization_barrier((held, fetched))
     second_chip = (me // 2) % 2 == 1
     mine = jnp.stack(
         [

time: 207 us -> 210 us (1.014)
  waiting for transfers between devices: 77.5 us -> 90.1 us
  starting transfers between devices: 80.7 us -> 73.7 us
    all_to_all x1, waiting for transfers between devices: 11 us -> 0.01 us  [gather(): lax.all_to_all(spread, 'tp', split_axis=0, concat_axis=0, axis_index_grou...]
    ppermute x2, waiting for transfers between devices: 8.79 us -> 15 us  [on_device(): fetched = [lax.ppermute(kv_own, 'tp', route) for route in kv_routes]]
    ppermute x1, waiting for transfers between devices: 0.18 us -> 5.73 us  [on_device(): returned = lax.ppermute(theirs, 'section', mirror)]
    ppermute x1, waiting for transfers between devices: 0.01 us -> 4.62 us  [on_device(): arrived = lax.ppermute(other, 'section', mirror)]
    ppermute x1, starting transfers between devices: 6.43 us -> 1.92 us  [on_device(): returned = lax.ppermute(theirs, 'section', mirror)]
    ppermute x3, waiting for transfers between devices: 38.4 us -> 42.9 us  [exchange(): return lax.ppermute(message, 'section', mirror)]
    ppermute x3, starting transfers between devices: 13.4 us -> 9.22 us  [exchange(): return lax.ppermute(message, 'section', mirror)]
    all_to_all x2, waiting for transfers between devices: 5.03 us -> 8.66 us  [reduce_blocks(): lax.all_to_all(chip, 'tp', split_axis=0, concat_axis=0, axis_index_groups...]
  transfers between devices with their start and end apart: 20 -> 20, of which waited for: 13 -> 13; matrix products, arithmetic and copies ran while one was open for 6% -> 5% of each run, Pallas kernels for 0% -> 0%
where the time goes in v7:
time: 210 us; the launch traced here: 209 us
  waiting for transfers between devices  90.1 us (43%)
  starting transfers between devices  73.7 us (35%)
  blocking collectives  11.4 us (5%)
  Pallas kernels  9.82 us (5%)
  other arithmetic  9.65 us (5%)
  local copies, waits for them, and re-layouts  8.8 us (4%)
  matrix products  3.92 us (2%)
    ppermute x3, waiting for transfers between devices, exchange(): return lax.ppermute(message, 'section', mirror)  42.9 us
    ppermute x2, waiting for transfers between devices, on_device(): fetched = [lax.ppermute(kv_own, 'tp', route) for route in kv_routes]  15 us
    ppermute x1, starting transfers between devices, on_device(): arrived = lax.ppermute(other, 'section', mirror)  13.2 us
    all_to_all x1, blocking collectives, gather(): lax.all_to_all(spread, 'tp', split_axis=0, concat_axis=0, axis_index_grou...  11.4 us
    all_to_all x2, starting transfers between devices, reduce_blocks(): lax.all_to_all(chip, 'tp', split_axis=0, concat_axis=0, axis_index_groups...  11.2 us
    ppermute x3, starting transfers between devices, exchange(): return lax.ppermute(message, 'section', mirror)  9.22 us
    all_to_all x2, waiting for transfers between devices, reduce_blocks(): lax.all_to_all(chip, 'tp', split_axis=0, concat_axis=0, axis_index_groups...  8.66 us
    ppermute x2, starting transfers between devices, on_device(): fetched = [lax.ppermute(kv_own, 'tp', route) for route in kv_routes]  7.63 us
  transfers between devices with their start and end apart: 20, of which 13 were waited for; matrix products, arithmetic and copies ran while one was open for 5% of the time, Pallas kernels for 0%

profile of v7, /device:TPU:26, one launch (start us, length us, event | category | flops | bytes accessed | tf_op | source)
XLA Modules:
  0.0 208.8 jit_solution(11493363389731750705)
XLA Ops:
  3.2 13.2 %collective-permute-start = (bf16[4,4,2048]{2,1,0:T(4,128)(2,1)S(1)}, bf16[4,4,2048]{2,1,0:T(4,128)(2,1)S(1)}, u32[]{:S(2)}, u32[]{:S(2)}) collective-permute-start(bf16[4,4,2048]{2,1,0:T(4,128)(2,1)S(1)} %broadcast_select_fusion.6), channel_id=1, source_target_pairs={{0,496},{16,480},{32,464},{48,448},{64,432},{80,416},{96,400},{112... | collective-permute-start | bytes 196616 | tf_op jit(solution)/shard_map/ppermute | solution.py:259
  16.4 4.6 %collective-permute-done = bf16[4,4,2048]{2,1,0:T(4,128)(2,1)S(1)} collective-permute-done((bf16[4,4,2048]{2,1,0:T(4,128)(2,1)S(1)}, bf16[4,4,2048]{2,1,0:T(4,128)(2,1)S(1)}, u32[]{:S(2)}, u32[]{:S(2)}) %collective-permute-start) | collective-permute-done | bytes 65568 | tf_op jit(solution)/shard_map/ppermute | solution.py:259
  22.3 5.7 %all-to-all-start = ((bf16[8,32,2048]{2,1,0:T(8,128)(2,1)}), bf16[8,32,2048]{2,1,0:T(8,128)(2,1)S(1)}, u32[]{:S(2)}, u32[]{:S(2)}) async-start(bf16[8,32,2048]{2,1,0:T(8,128)(2,1)} %broadcast_in_dim.24), calls=%async_computation | async-start | bytes 2097152 | tf_op jit(solution)/shard_map/all_to_all | solution.py:294
  28.0 3.4 %collective-permute-start.3 = (bf16[64,2048]{1,0:T(8,128)(2,1)S(1)}, bf16[64,2048]{1,0:T(8,128)(2,1)S(1)}, u32[]{:S(2)}, u32[]{:S(2)}) collective-permute-start(bf16[64,2048]{1,0:T(8,128)(2,1)S(1)} %bitcast.159), channel_id=1, source_target_pairs={{0,0},{1,1},{8,2},{9,3},{2,4},{3,5},{10,6},{11,7},{4,8},{5,9},{12,... | collective-permute-start | bytes 786440 | tf_op jit(solution)/shard_map/ppermute | solution.py:275
  31.3 4.3 %collective-permute-start.2 = (bf16[64,2048]{1,0:T(8,128)(2,1)S(1)}, bf16[64,2048]{1,0:T(8,128)(2,1)S(1)}, u32[]{:S(2)}, u32[]{:S(2)}) collective-permute-start(bf16[64,2048]{1,0:T(8,128)(2,1)S(1)} %bitcast.160), channel_id=1, source_target_pairs={{8,0},{9,1},{0,2},{1,3},{10,4},{11,5},{2,6},{3,7},{12,8},{13,9},{4... | collective-permute-start | bytes 786440 | tf_op jit(solution)/shard_map/ppermute | solution.py:275
  35.6 12.4 %collective-permute-done.3 = bf16[64,2048]{1,0:T(8,128)(2,1)S(1)} collective-permute-done((bf16[64,2048]{1,0:T(8,128)(2,1)S(1)}, bf16[64,2048]{1,0:T(8,128)(2,1)S(1)}, u32[]{:S(2)}, u32[]{:S(2)}) %collective-permute-start.3) | collective-permute-done | bytes 262176 | tf_op jit(solution)/shard_map/ppermute | solution.py:275
  48.1 2.6 %collective-permute-done.2 = bf16[64,2048]{1,0:T(8,128)(2,1)S(1)} collective-permute-done((bf16[64,2048]{1,0:T(8,128)(2,1)S(1)}, bf16[64,2048]{1,0:T(8,128)(2,1)S(1)}, u32[]{:S(2)}, u32[]{:S(2)}) %collective-permute-start.2) | collective-permute-done | bytes 262176 | tf_op jit(solution)/shard_map/ppermute | solution.py:275
  50.7 1.9 collective-permute-start.4
  52.7 2.4 %collective-permute-start.1 = (bf16[8,32,2048]{2,1,0:T(8,128)(2,1)S(1)}, bf16[8,32,2048]{2,1,0:T(8,128)(2,1)S(1)}, u32[]{:S(2)}, u32[]{:S(2)}) collective-permute-start(bf16[8,32,2048]{2,1,0:T(8,128)(2,1)S(1)} %all-to-all-done), channel_id=1, source_target_pairs={{0,1},{1,0},{2,3},{3,2},{4,5},{5,4},{6,7},{7,6},{8,9},{9,8},{10,11... | collective-permute-start | bytes 3145736 | tf_op jit(solution)/shard_map/ppermute | solution.py:297
  59.1 3.0 %shard_map.136 = (bf16[128,1408]{1,0:T(8,128)(2,1)S(1)}, f32[128,1408]{1,0:T(8,128)S(1)}, bf16[128,640]{1,0:T(8,128)(2,1)}, f32[128,640]{1,0:T(8,128)}, bf16[128...) custom-call(bf16[16,32,2048]{2,1,0:T(8,128)(2,1)S(1)} %bitcast.148, ...), custom_call_target="tpu_custom_call" | custom-call | tf_op jit(solution)/shard_map/pallas_call | solution.py:313
  62.1 5.1 %collective-permute-start.5 = (bf16[128,1408]{1,0:T(8,128)(2,1)S(1)}, bf16[128,1408]{1,0:T(8,128)(2,1)S(1)}, u32[]{:S(2)}, u32[]{:S(2)}) collective-permute-start(bf16[128,1408]{1,0:T(8,128)(2,1)S(1)} %get-tuple-element.42), channel_id=1, source_target_pairs={{0,496},{16,480},{32,464},{48,448},{64,432},{80,416},{96,400},{112... | collective-permute-start | bytes 1081352 | tf_op jit(solution)/shard_map/ppermute | solution.py:329
  67.2 23.7 %collective-permute-done.5.got_x = bf16[128,1408]{1,0:T(8,128)(2,1)S(1)} collective-permute-done((bf16[128,1408]{1,0:T(8,128)(2,1)S(1)}, bf16[128,1408]{1,0:T(8,128)(2,1)S(1)}, u32[]{:S(2)}, u32[]{:S(2)}) %collective-permute-start.5) | collective-permute-done | bytes 360480 | tf_op jit(solution)/shard_map/ppermute | solution.py:329
  90.9 2.7 %shard_map.137 = (bf16[8,16,2048]{2,1,0:T(8,128)(2,1)S(1)}, bf16[8,16,2048]{2,1,0:T(8,128)(2,1)S(1)}, bf16[128,2048]{1,0:T(8,128)(2,1)}, bf16[128,256]{1,0:T(8,1...) custom-call(s32[1]{0:T(128)} %bitcast.1.core, ...), custom_call_target="tpu_custom_call" | custom-call | tf_op jit(solution)/shard_map/pallas_call | solution.py:345
  93.6 1.9 collective-permute-start.6
  98.4 6.0 %all-to-all-start.1 = ((bf16[8,16,2048]{2,1,0:T(8,128)(2,1)}), bf16[8,16,2048]{2,1,0:T(8,128)(2,1)}, u32[]{:S(2)}, u32[]{:S(2)}) async-start(bf16[8,16,2048]{2,1,0:T(8,128)(2,1)} %add_convert_fusion.1), calls=%async_computation.1 | async-start | bytes 1048576 | tf_op jit(solution)/shard_map/all_to_all | solution.py:363
  105.0 2.2 %collective-permute-start.9 = (bf16[128,640]{1,0:T(8,128)(2,1)}, bf16[128,640]{1,0:T(8,128)(2,1)S(1)}, u32[]{:S(2)}, u32[]{:S(2)}) collective-permute-start(bf16[128,640]{1,0:T(8,128)(2,1)} %get-tuple-element.50), channel_id=1, source_target_pairs={{0,496},{16,480},{32,464},{48,448},{64,432},{80,416},{96,400},{112... | collective-permute-start | bytes 491528 | tf_op jit(solution)/shard_map/ppermute | solution.py:329
  107.2 8.7 %all-to-all-done.1 = bf16[8,16,2048]{2,1,0:T(8,128)(2,1)} async-done(((bf16[8,16,2048]{2,1,0:T(8,128)(2,1)}), bf16[8,16,2048]{2,1,0:T(8,128)(2,1)}, u32[]{:S(2)}, u32[]{:S(2)}) %all-to-all-start.1) | async-done | bytes 524320 | tf_op jit(solution)/shard_map/all_to_all | solution.py:363
  119.8 4.8 %collective-permute-start.7 = (bf16[4,2,2048]{2,1,0:T(2,128)(2,1)S(1)}, bf16[4,2,2048]{2,1,0:T(2,128)(2,1)}, u32[]{:S(2)}, u32[]{:S(2)}) collective-permute-start(bf16[4,2,2048]{2,1,0:T(2,128)(2,1)S(1)} %get-tuple-element.48), channel_id=1, source_target_pairs={{0,16},{16,32},{32,48},{48,64},{64,80},{80,96},{96,112},{112,128},... | collective-permute-start | bytes 98312 | tf_op jit(solution)/shard_map/ppermute | solution.py:436
  125.5 3.2 %collective-permute-done.7 = bf16[4,2,2048]{2,1,0:T(2,128)(2,1)} collective-permute-done((bf16[4,2,2048]{2,1,0:T(2,128)(2,1)S(1)}, bf16[4,2,2048]{2,1,0:T(2,128)(2,1)}, u32[]{:S(2)}, u32[]{:S(2)}) %collective-permute-start.7) | collective-permute-done | bytes 32800 | tf_op jit(solution)/shard_map/ppermute | solution.py:436
  131.1 11.4 %all_to_all.20 = bf16[8,16,2048]{2,1,0:T(8,128)(2,1)S(1)} all-to-all(bf16[8,16,2048]{2,1,0:T(8,128)(2,1)S(1)} %broadcast_in_dim.26), channel_id=1, replica_groups={{0,2,4,6,8,10,12,14},{1,3,5,7,9,11,13,15},{16,18,20,22,24,26,28,30},{17..., dimensions={0} | all-to-all | bytes 1048576 | tf_op jit(solution)/shard_map/all_to_all | solution.py:294
  142.5 1.9 collective-permute-start.10
  148.2 1.9 collective-permute-start.11
  150.2 19.2 %collective-permute-done.11.got_x = bf16[128,896]{1,0:T(8,128)(2,1)S(1)} collective-permute-done((bf16[128,896]{1,0:T(8,128)(2,1)S(1)}, bf16[128,896]{1,0:T(8,128)(2,1)S(1)}, u32[]{:S(2)}, u32[]{:S(2)}) %collective-permute-start.11) | collective-permute-done | bytes 229408 | tf_op jit(solution)/shard_map/ppermute | solution.py:329
  169.4 2.4 %shard_map.139 = (bf16[8,16,2304]{2,1,0:T(8,128)(2,1)S(1)}, bf16[8,16,2304]{2,1,0:T(8,128)(2,1)S(1)}, bf16[128,2048]{1,0:T(8,128)(2,1)}, bf16[128,256]{1,0:T(8,1...) custom-call(s32[1]{0:T(128)} %bitcast.1.core, f32[128,896]{1,0:T(8,128)S(1)} %get-tuple-element.53.own_x, ...), custom_call_target="tpu_custom_call" | custom-call | tf_op jit(solution)/shard_map/pallas_call | solution.py:345
  171.8 2.1 collective-permute-start.12
  174.8 2.4 %collective-permute-start.14 = (bf16[2,64,256]{2,1,0:T(8,128)(2,1)S(1)}, bf16[2,64,256]{2,1,0:T(8,128)(2,1)S(1)}, u32[]{:S(2)}, u32[]{:S(2)}) collective-permute-start(bf16[2,64,256]{2,1,0:T(8,128)(2,1)S(1)} %fusion.14), channel_id=1, source_target_pairs={{0,1},{1,0},{2,3},{3,2},{4,5},{5,4},{6,7},{7,6},{8,9},{9,8},{10,11... | collective-permute-start | bytes 196616 | tf_op jit(solution)/shard_map/ppermute | solution.py:371
  178.1 5.2 %all-to-all-start.3 = ((bf16[8,16,2304]{2,1,0:T(8,128)(2,1)}), bf16[8,16,2304]{2,1,0:T(8,128)(2,1)S(1)}, u32[]{:S(2)}, u32[]{:S(2)}) async-start(bf16[8,16,2304]{2,1,0:T(8,128)(2,1)} %add_convert_fusion), calls=%async_computation.3 | async-start | bytes 1179648 | tf_op jit(solution)/shard_map/all_to_all | solution.py:363
  183.6 3.5 %collective-permute-start.15 = (bf16[64,256]{1,0:T(8,128)(2,1)S(1)}, bf16[64,256]{1,0:T(8,128)(2,1)S(1)}, u32[]{:S(2)}, u32[]{:S(2)}) collective-permute-start(bf16[64,256]{1,0:T(8,128)(2,1)S(1)} %get-tuple-element.100), channel_id=1, source_target_pairs={{0,0},{1,1},{2,8},{3,9},{4,2},{5,3},{6,10},{7,11},{8,4},{9,5},{10,... | collective-permute-start | bytes 98312 | tf_op jit(solution)/shard_map/ppermute | solution.py:378
  187.1 1.9 collective-permute-start.16
  189.1 4.0 %collective-permute-done.15 = bf16[64,256]{1,0:T(8,128)(2,1)S(1)} collective-permute-done((bf16[64,256]{1,0:T(8,128)(2,1)S(1)}, bf16[64,256]{1,0:T(8,128)(2,1)S(1)}, u32[]{:S(2)}, u32[]{:S(2)}) %collective-permute-start.15) | collective-permute-done | bytes 32800 | tf_op jit(solution)/shard_map/ppermute | solution.py:378
  196.5 1.9 collective-permute-start.13
  201.4 5.7 %collective-permute-done.13 = bf16[4,4,2048]{2,1,0:T(4,128)(2,1)S(1)} collective-permute-done((bf16[4,4,2048]{2,1,0:T(4,128)(2,1)S(1)}, bf16[4,4,2048]{2,1,0:T(4,128)(2,1)S(1)}, u32[]{:S(2)}, u32[]{:S(2)}) %collective-permute-start.13) | collective-permute-done | bytes 65568 | tf_op jit(solution)/shard_map/ppermute | solution.py:471
  (129 shorter events, 32.0 us)
Async XLA Ops:
  3.1 24.8 %copy-start.22 = (bf16[1,2048,64]{1,2,0:T(8,128)(2,1)S(1)}, bf16[1,2048,64]{1,2,0:T(8,128)(2,1)}, u32[]{:S(2)}) copy-start(bf16[1,2048,64]{1,2,0:T(8,128)(2,1)} %param.16) | copy-start | bytes 786436
  3.2 17.8 %collective-permute-start = (bf16[4,4,2048]{2,1,0:T(4,128)(2,1)S(1)}, bf16[4,4,2048]{2,1,0:T(4,128)(2,1)S(1)}, u32[]{:S(2)}, u32[]{:S(2)}) collective-permute-start(bf16[4,4,2048]{2,1,0:T(4,128)(2,1)S(1)} %broadcast_select_fusion.6), channel_id=1, source_target_pairs={{0,496},{16,480},{32,464},{48,448},{64,432},{80,416},{96,400},{112... | collective-permute-start | bytes 196616 | tf_op jit(solution)/shard_map/ppermute | solution.py:259
  22.3 30.4 %all-to-all-start = ((bf16[8,32,2048]{2,1,0:T(8,128)(2,1)}), bf16[8,32,2048]{2,1,0:T(8,128)(2,1)S(1)}, u32[]{:S(2)}, u32[]{:S(2)}) async-start(bf16[8,32,2048]{2,1,0:T(8,128)(2,1)} %broadcast_in_dim.24), calls=%async_computation | async-start | bytes 2097152 | tf_op jit(solution)/shard_map/all_to_all | solution.py:294
  28.0 20.1 %collective-permute-start.3 = (bf16[64,2048]{1,0:T(8,128)(2,1)S(1)}, bf16[64,2048]{1,0:T(8,128)(2,1)S(1)}, u32[]{:S(2)}, u32[]{:S(2)}) collective-permute-start(bf16[64,2048]{1,0:T(8,128)(2,1)S(1)} %bitcast.159), channel_id=1, source_target_pairs={{0,0},{1,1},{8,2},{9,3},{2,4},{3,5},{10,6},{11,7},{4,8},{5,9},{12,... | collective-permute-start | bytes 786440 | tf_op jit(solution)/shard_map/ppermute | solution.py:275
  31.3 19.3 %collective-permute-start.2 = (bf16[64,2048]{1,0:T(8,128)(2,1)S(1)}, bf16[64,2048]{1,0:T(8,128)(2,1)S(1)}, u32[]{:S(2)}, u32[]{:S(2)}) collective-permute-start(bf16[64,2048]{1,0:T(8,128)(2,1)S(1)} %bitcast.160), channel_id=1, source_target_pairs={{8,0},{9,1},{0,2},{1,3},{10,4},{11,5},{2,6},{3,7},{12,8},{13,9},{4... | collective-permute-start | bytes 786440 | tf_op jit(solution)/shard_map/ppermute | solution.py:275
  50.7 4.4 %collective-permute-start.4 = (bf16[2,64,2048]{2,1,0:T(8,128)(2,1)S(1)}, bf16[2,64,2048]{2,1,0:T(8,128)(2,1)}, u32[]{:S(2)}, u32[]{:S(2)}) collective-permute-start(bf16[2,64,2048]{2,1,0:T(8,128)(2,1)S(1)} %pad_maximum_fusion.3), channel_id=1, source_target_pairs={{0,1},{1,0},{2,3},{3,2},{4,5},{5,4},{6,7},{7,6},{8,9},{9,8},{10,11... | collective-permute-start | bytes 1572872 | tf_op jit(solution)/shard_map/ppermute | solution.py:283
  52.7 4.7 %collective-permute-start.1 = (bf16[8,32,2048]{2,1,0:T(8,128)(2,1)S(1)}, bf16[8,32,2048]{2,1,0:T(8,128)(2,1)S(1)}, u32[]{:S(2)}, u32[]{:S(2)}) collective-permute-start(bf16[8,32,2048]{2,1,0:T(8,128)(2,1)S(1)} %all-to-all-done), channel_id=1, source_target_pairs={{0,1},{1,0},{2,3},{3,2},{4,5},{5,4},{6,7},{7,6},{8,9},{9,8},{10,11... | collective-permute-start | bytes 3145736 | tf_op jit(solution)/shard_map/ppermute | solution.py:297
  62.1 28.8 %collective-permute-start.5 = (bf16[128,1408]{1,0:T(8,128)(2,1)S(1)}, bf16[128,1408]{1,0:T(8,128)(2,1)S(1)}, u32[]{:S(2)}, u32[]{:S(2)}) collective-permute-start(bf16[128,1408]{1,0:T(8,128)(2,1)S(1)} %get-tuple-element.42), channel_id=1, source_target_pairs={{0,496},{16,480},{32,464},{48,448},{64,432},{80,416},{96,400},{112... | collective-permute-start | bytes 1081352 | tf_op jit(solution)/shard_map/ppermute | solution.py:329
  93.6 10.8 %copy-start.18 = (bf16[2,1,2,4096]{3,2,1,0:T(2,128)(2,1)S(1)}, bf16[2,1,2,4096]{3,2,1,0:T(2,128)(2,1)}, u32[]{:S(2)}) copy-start(bf16[2,1,2,4096]{3,2,1,0:T(2,128)(2,1)} %param.13) | copy-start | bytes 98308
  93.6 3.8 %collective-permute-start.6 = (bf16[8,16,2048]{2,1,0:T(8,128)(2,1)S(1)}, bf16[8,16,2048]{2,1,0:T(8,128)(2,1)S(1)}, u32[]{:S(2)}, u32[]{:S(2)}) collective-permute-start(bf16[8,16,2048]{2,1,0:T(8,128)(2,1)S(1)} %get-tuple-element.45), channel_id=1, source_target_pairs={{0,1},{1,0},{2,3},{3,2},{4,5},{5,4},{6,7},{7,6},{8,9},{9,8},{10,11... | collective-permute-start | bytes 1572872 | tf_op jit(solution)/shard_map/ppermute | solution.py:358
  98.4 17.5 %all-to-all-start.1 = ((bf16[8,16,2048]{2,1,0:T(8,128)(2,1)}), bf16[8,16,2048]{2,1,0:T(8,128)(2,1)}, u32[]{:S(2)}, u32[]{:S(2)}) async-start(bf16[8,16,2048]{2,1,0:T(8,128)(2,1)} %add_convert_fusion.1), calls=%async_computation.1 | async-start | bytes 1048576 | tf_op jit(solution)/shard_map/all_to_all | solution.py:363
  105.0 20.5 %collective-permute-start.9 = (bf16[128,640]{1,0:T(8,128)(2,1)}, bf16[128,640]{1,0:T(8,128)(2,1)S(1)}, u32[]{:S(2)}, u32[]{:S(2)}) collective-permute-start(bf16[128,640]{1,0:T(8,128)(2,1)} %get-tuple-element.50), channel_id=1, source_target_pairs={{0,496},{16,480},{32,464},{48,448},{64,432},{80,416},{96,400},{112... | collective-permute-start | bytes 491528 | tf_op jit(solution)/shard_map/ppermute | solution.py:329
  117.9 7.6 %collective-permute-start.8 = (bf16[4,2,2048]{2,1,0:T(2,128)(2,1)}, bf16[4,2,2048]{2,1,0:T(2,128)(2,1)S(1)}, u32[]{:S(2)}, u32[]{:S(2)}) collective-permute-start(bf16[4,2,2048]{2,1,0:T(2,128)(2,1)} %get-tuple-element.49), channel_id=1, source_target_pairs={{16,0},{32,16},{48,32},{64,48},{80,64},{96,80},{112,96},{128,112},... | collective-permute-start | bytes 98312 | tf_op jit(solution)/shard_map/ppermute | solution.py:437
  119.8 8.9 %collective-permute-start.7 = (bf16[4,2,2048]{2,1,0:T(2,128)(2,1)S(1)}, bf16[4,2,2048]{2,1,0:T(2,128)(2,1)}, u32[]{:S(2)}, u32[]{:S(2)}) collective-permute-start(bf16[4,2,2048]{2,1,0:T(2,128)(2,1)S(1)} %get-tuple-element.48), channel_id=1, source_target_pairs={{0,16},{16,32},{32,48},{48,64},{64,80},{80,96},{96,112},{112,128},... | collective-permute-start | bytes 98312 | tf_op jit(solution)/shard_map/ppermute | solution.py:436
  142.5 3.8 %collective-permute-start.10 = (bf16[8,16,2048]{2,1,0:T(8,128)(2,1)S(1)}, bf16[8,16,2048]{2,1,0:T(8,128)(2,1)S(1)}, u32[]{:S(2)}, u32[]{:S(2)}) collective-permute-start(bf16[8,16,2048]{2,1,0:T(8,128)(2,1)S(1)} %all_to_all.20), channel_id=1, source_target_pairs={{0,1},{1,0},{2,3},{3,2},{4,5},{5,4},{6,7},{7,6},{8,9},{9,8},{10,11... | collective-permute-start | bytes 1572872 | tf_op jit(solution)/shard_map/ppermute | solution.py:297
  146.5 22.9 %copy-start.2 = (bf16[128,2048]{1,0:T(8,128)(2,1)S(1)}, bf16[128,2048]{1,0:T(8,128)(2,1)}, u32[]{:S(2)}) copy-start(bf16[128,2048]{1,0:T(8,128)(2,1)} %get-tuple-element.57.rest_2_) | copy-start | bytes 1572868
  146.5 22.9 %copy-start.3 = (f32[128,640]{1,0:T(8,128)S(1)}, f32[128,640]{1,0:T(8,128)}, u32[]{:S(2)}) copy-start(f32[128,640]{1,0:T(8,128)} %get-tuple-element.55.rest_0_) | copy-start | bytes 983044
  146.5 22.9 %copy-start.5 = (f32[1,2048]{1,0:T(1,128)S(1)}, f32[1,2048]{1,0:T(1,128)}, u32[]{:S(2)}) copy-start(f32[1,2048]{1,0:T(1,128)} %get-tuple-element.58.rest_7_) | copy-start | bytes 24580
  148.2 21.1 %collective-permute-start.11 = (bf16[128,896]{1,0:T(8,128)(2,1)S(1)}, bf16[128,896]{1,0:T(8,128)(2,1)S(1)}, u32[]{:S(2)}, u32[]{:S(2)}) collective-permute-start(bf16[128,896]{1,0:T(8,128)(2,1)S(1)} %get-tuple-element.54), channel_id=1, source_target_pairs={{0,496},{16,480},{32,464},{48,448},{64,432},{80,416},{96,400},{112... | collective-permute-start | bytes 688136 | tf_op jit(solution)/shard_map/ppermute | solution.py:329
  171.8 11.6 %copy-start.6 = (bf16[128,2048]{1,0:T(8,128)(2,1)S(1)}, bf16[128,2048]{1,0:T(8,128)(2,1)}, u32[]{:S(2)}) copy-start(bf16[128,2048]{1,0:T(8,128)(2,1)} %get-tuple-element.61) | copy-start | bytes 1572868
  171.8 5.4 %collective-permute-start.12 = (bf16[8,16,2304]{2,1,0:T(8,128)(2,1)S(1)}, bf16[8,16,2304]{2,1,0:T(8,128)(2,1)S(1)}, u32[]{:S(2)}, u32[]{:S(2)}) collective-permute-start(bf16[8,16,2304]{2,1,0:T(8,128)(2,1)S(1)} %get-tuple-element.60), channel_id=1, source_target_pairs={{0,1},{1,0},{2,3},{3,2},{4,5},{5,4},{6,7},{7,6},{8,9},{9,8},{10,11... | collective-permute-start | bytes 1769480 | tf_op jit(solution)/shard_map/ppermute | solution.py:358
  174.8 8.8 %collective-permute-start.14 = (bf16[2,64,256]{2,1,0:T(8,128)(2,1)S(1)}, bf16[2,64,256]{2,1,0:T(8,128)(2,1)S(1)}, u32[]{:S(2)}, u32[]{:S(2)}) collective-permute-start(bf16[2,64,256]{2,1,0:T(8,128)(2,1)S(1)} %fusion.14), channel_id=1, source_target_pairs={{0,1},{1,0},{2,3},{3,2},{4,5},{5,4},{6,7},{7,6},{8,9},{9,8},{10,11... | collective-permute-start | bytes 196616 | tf_op jit(solution)/shard_map/ppermute | solution.py:371
  177.2 11.9 %copy-start.7 = (bf16[128,2048]{1,0:T(8,128)(2,1)S(1)}, bf16[128,2048]{1,0:T(8,128)(2,1)}, u32[]{:S(2)}) copy-start(bf16[128,2048]{1,0:T(8,128)(2,1)} %get-tuple-element.62) | copy-start | bytes 1572868
  178.1 17.3 %all-to-all-start.3 = ((bf16[8,16,2304]{2,1,0:T(8,128)(2,1)}), bf16[8,16,2304]{2,1,0:T(8,128)(2,1)S(1)}, u32[]{:S(2)}, u32[]{:S(2)}) async-start(bf16[8,16,2304]{2,1,0:T(8,128)(2,1)} %add_convert_fusion), calls=%async_computation.3 | async-start | bytes 1179648 | tf_op jit(solution)/shard_map/all_to_all | solution.py:363
  183.4 12.1 %copy-start.9 = (bf16[2,2048]{1,0:T(2,128)(2,1)S(1)}, bf16[2,2048]{1,0:T(2,128)(2,1)}, u32[]{:S(2)}) copy-start(bf16[2,2048]{1,0:T(2,128)(2,1)} %copy-done.8) | copy-start | bytes 24580
  183.4 12.1 %copy-start.11 = (bf16[2,2048]{1,0:T(2,128)(2,1)S(1)}, bf16[2,2048]{1,0:T(2,128)(2,1)}, u32[]{:S(2)}) copy-start(bf16[2,2048]{1,0:T(2,128)(2,1)} %copy-done.10) | copy-start | bytes 24580
  183.5 12.1 %copy-start.13 = (bf16[2,2048]{1,0:T(2,128)(2,1)S(1)}, bf16[2,2048]{1,0:T(2,128)(2,1)}, u32[]{:S(2)}) copy-start(bf16[2,2048]{1,0:T(2,128)(2,1)} %copy-done.12) | copy-start | bytes 24580
  183.6 14.9 %copy-start.14 = (bf16[128,256]{1,0:T(8,128)(2,1)S(1)}, bf16[128,256]{1,0:T(8,128)(2,1)}, u32[]{:S(2)}) copy-start(bf16[128,256]{1,0:T(8,128)(2,1)} %get-tuple-element.67) | copy-start | bytes 196612
  183.6 14.9 %copy-start.15 = (bf16[128,256]{1,0:T(8,128)(2,1)S(1)}, bf16[128,256]{1,0:T(8,128)(2,1)}, u32[]{:S(2)}) copy-start(bf16[128,256]{1,0:T(8,128)(2,1)} %get-tuple-element.68) | copy-start | bytes 196612
  183.6 9.5 %collective-permute-start.15 = (bf16[64,256]{1,0:T(8,128)(2,1)S(1)}, bf16[64,256]{1,0:T(8,128)(2,1)S(1)}, u32[]{:S(2)}, u32[]{:S(2)}) collective-permute-start(bf16[64,256]{1,0:T(8,128)(2,1)S(1)} %get-tuple-element.100), channel_id=1, source_target_pairs={{0,0},{1,1},{2,8},{3,9},{4,2},{5,3},{6,10},{7,11},{8,4},{9,5},{10,... | collective-permute-start | bytes 98312 | tf_op jit(solution)/shard_map/ppermute | solution.py:378
  187.1 7.3 %collective-permute-start.16 = (bf16[64,256]{1,0:T(8,128)(2,1)S(1)}, bf16[64,256]{1,0:T(8,128)(2,1)S(1)}, u32[]{:S(2)}, u32[]{:S(2)}) collective-permute-start(bf16[64,256]{1,0:T(8,128)(2,1)S(1)} %get-tuple-element.101), channel_id=1, source_target_pairs={{0,8},{1,9},{2,0},{3,1},{4,10},{5,11},{6,2},{7,3},{8,12},{9,13},{1... | collective-permute-start | bytes 98312 | tf_op jit(solution)/shard_map/ppermute | solution.py:378
  196.5 10.6 %collective-permute-start.13 = (bf16[4,4,2048]{2,1,0:T(4,128)(2,1)S(1)}, bf16[4,4,2048]{2,1,0:T(4,128)(2,1)S(1)}, u32[]{:S(2)}, u32[]{:S(2)}) collective-permute-start(bf16[4,4,2048]{2,1,0:T(4,128)(2,1)S(1)} %select_bitcast_fusion.8), channel_id=1, source_target_pairs={{0,496},{16,480},{32,464},{48,448},{64,432},{80,416},{96,400},{112... | collective-permute-start | bytes 196616 | tf_op jit(solution)/shard_map/ppermute | solution.py:471
  (13 other events, 42.4 us)
